TPU v7x, 128 devices: a whole 4x4x4 slice. The times are simulated.
128 devices in a mesh: dp: 32 (over z, x, core), row: 2 (over y_hi), col: 2 (over y_lo).
Axes of the slice: x: 4, y: 4 (y_hi: 2, y_lo: 2; y = y_hi * 2 + y_lo), z: 4, core: 2. Of those that a mesh axis runs over, the one named last changes fastest.
Arguments:
- hidden_in: bfloat16 [10240, 1024], P(('dp', 'col'), 'row'), may hold values from -8 to 8
- cotangent: bfloat16 [10240, 1024], P(('dp', 'col'), 'row'), may hold values from -6 to 6
- seq_ids: int32 [10240], P('dp'), may hold values from 0 to 3, as said below
- qkv_weight: float32 [2, 1024, 3072], P(None, ('row', 'dp'), 'col'), may hold values from -0.1875 to 0.1875
- qkv_first: float32 [2, 1024, 3072], P(None, ('row', 'dp'), 'col'), may hold values from -96 to 96
- qkv_second: float32 [2, 1024, 3072], P(None, ('row', 'dp'), 'col'), may hold values from 604.16 to 9728
- out_weight: float32 [2, 1024, 1024], P(None, ('col', 'dp'), 'row'), may hold values from -0.75 to 0.75
- out_first: float32 [2, 1024, 1024], P(None, ('col', 'dp'), 'row'), may hold values from -10 to 10
- out_second: float32 [2, 1024, 1024], P(None, ('col', 'dp'), 'row'), may hold values from 6.144 to 97.28
- up_weight: float32 [2, 1024, 4096], P(None, ('row', 'dp'), 'col'), may hold values from -0.1875 to 0.1875
- up_first: float32 [2, 1024, 4096], P(None, ('row', 'dp'), 'col'), may hold values from -16 to 16
- up_second: float32 [2, 1024, 4096], P(None, ('row', 'dp'), 'col'), may hold values from 16.384 to 266.24
- down_weight: float32 [2, 4096, 1024], P(None, ('col', 'dp'), 'row'), may hold values from -0.09375 to 0.09375
- down_first: float32 [2, 4096, 1024], P(None, ('col', 'dp'), 'row'), may hold values from -32 to 32
- down_second: float32 [2, 4096, 1024], P(None, ('col', 'dp'), 'row'), may hold values from 67.584 to 1075.2
- qkv_bias: float32 [2, 3072], P(None, ('col', 'row', 'dp')), may hold values from -1.25 to 1.25
- qkv_bias_first: float32 [2, 3072], P(None, ('col', 'row', 'dp')), may hold values from -96 to 96
- qkv_bias_second: float32 [2, 3072], P(None, ('col', 'row', 'dp')), may hold values from 604.16 to 9728
- up_bias: float32 [2, 4096], P(None, ('col', 'row', 'dp')), may hold values from -1.25 to 1.25
- up_bias_first: float32 [2, 4096], P(None, ('col', 'row', 'dp')), may hold values from -16 to 16
- up_bias_second: float32 [2, 4096], P(None, ('col', 'row', 'dp')), may hold values from 16.384 to 266.24
- row_vectors: float32 [2, 6, 1024], P(None, None, 'row'), may hold values from -0.6 to 1.45
- row_first: float32 [2, 6, 1024], P(None, None, 'row'), may hold values from -64 to 64
- row_second: float32 [2, 6, 1024], P(None, None, 'row'), may hold values from 266.24 to 4300.8
Outputs:
- hidden_out: bfloat16 [10240, 1024], P(('dp', 'col'), 'row')
- input_grad: float32 [10240, 1024], P(('dp', 'col'), 'row')
- qkv_weight_new: float32 [2, 1024, 3072], P(None, ('row', 'dp'), 'col')
- qkv_first_new: float32 [2, 1024, 3072], P(None, ('row', 'dp'), 'col')
- qkv_second_new: float32 [2, 1024, 3072], P(None, ('row', 'dp'), 'col')
- out_weight_new: float32 [2, 1024, 1024], P(None, ('col', 'dp'), 'row')
- out_first_new: float32 [2, 1024, 1024], P(None, ('col', 'dp'), 'row')
- out_second_new: float32 [2, 1024, 1024], P(None, ('col', 'dp'), 'row')
- up_weight_new: float32 [2, 1024, 4096], P(None, ('row', 'dp'), 'col')
- up_first_new: float32 [2, 1024, 4096], P(None, ('row', 'dp'), 'col')
- up_second_new: float32 [2, 1024, 4096], P(None, ('row', 'dp'), 'col')
- down_weight_new: float32 [2, 4096, 1024], P(None, ('col', 'dp'), 'row')
- down_first_new: float32 [2, 4096, 1024], P(None, ('col', 'dp'), 'row')
- down_second_new: float32 [2, 4096, 1024], P(None, ('col', 'dp'), 'row')
- qkv_bias_new: float32 [2, 3072], P(None, ('col', 'row', 'dp'))
- qkv_bias_first_new: float32 [2, 3072], P(None, ('col', 'row', 'dp'))
- qkv_bias_second_new: float32 [2, 3072], P(None, ('col', 'row', 'dp'))
- up_bias_new: float32 [2, 4096], P(None, ('col', 'row', 'dp'))
- up_bias_first_new: float32 [2, 4096], P(None, ('col', 'row', 'dp'))
- up_bias_second_new: float32 [2, 4096], P(None, ('col', 'row', 'dp'))
- row_vectors_new: float32 [2, 6, 1024], P(None, None, 'row')
- row_first_new: float32 [2, 6, 1024], P(None, None, 'row')
- row_second_new: float32 [2, 6, 1024], P(None, None, 'row')
Inputs may be any that keep to these rules, and one draw needn't show every extreme that they name: `seq_ids`: within each data group of 320 slots the numbers never fall; the value 3 marks padding, which stands after all live slots and occurs in some group; one sequence of every group covers the group's two middle slots; in every draw one group holds a single sequence of 320 slots.
All inputs are finite; a program needn't handle non-finite values.
Results may differ from a plain program's by a relative error of at most 0.012.
Values may be sent and summed in bfloat16 or wider, within the bound.
A program may use at most 128 MiB of HBM per device.

v0:
```python
from functools import partial

import jax
import jax.numpy as jnp
from jax import lax
from jax.sharding import PartitionSpec as P

D = 1024
HEAD = 64
ROT = 16
LAYERS = 2
SEQS = 3
STEP = 10


EPS_NORM = 1e-05
EPS_ADAM = 1e-08
BETA_ONE = 0.9
BETA_TWO = 0.95
RATE_MATRIX = 0.06
RATE_VECTOR = 0.6
DECAY_MATRIX = 0.01
ROPE_BASE = 10000.0
MASK_VALUE = -1e30
CONTRACT_ROWS = (((0,), (0,)), ((), ()))
CONTRACT_COLS = (((1,), (1,)), ((), ()))


def side_by_side(arrays, axis, dim, along):
    widths = [a.shape[along] for a in arrays]
    both = jnp.concatenate(arrays, axis=along)
    whole = lax.all_gather(both, axis, axis=dim, tiled=True)
    return tuple(jnp.split(whole, [sum(widths[:k]) for k in range(1, len(widths))], axis=along))


def copy_for_each(array, axis):
    copies = jnp.broadcast_to(array, (lax.axis_size(axis), *array.shape))
    return lax.all_to_all(copies, axis, split_axis=0, concat_axis=0, tiled=True)


def taken_together(array, axis):
    return copy_for_each(array, axis).sum(axis=0)


def packed_total(arrays, axis):
    ends = [0]
    for a in arrays:
        ends.append(ends[-1] + a.size)
    running = taken_together(jnp.concatenate([a.ravel() for a in arrays]), axis)
    return tuple((running[b:e].reshape(a.shape) for a, b, e in zip(arrays, ends, ends[1:])))


def in_blocks(array, dim, devices):
    before, after = (array.shape[:dim], array.shape[dim + 1 :])
    return jnp.moveaxis(array.reshape(*before, devices, -1, *after), dim, 0)


def sent_and_summed(array, axis, dim):
    devices = lax.axis_size(axis)
    tiles = lax.all_to_all(in_blocks(array, dim, devices), axis, 0, 0, tiled=True)
    return jnp.sum(tiles, axis=0)


def joined_along(tiles, dim):
    tiles = jnp.moveaxis(tiles, 0, dim)
    lengths = tiles.shape
    return tiles.reshape(*lengths[:dim], lengths[dim] * lengths[dim + 1], *lengths[dim + 2 :])


def gather_directly(array, axis, dim):
    return joined_along(copy_for_each(array, axis), dim)


def sent_together(arrays, axis, dim, along):
    both = jnp.concatenate(arrays, axis=along)
    whole, at, done = (sent_and_summed(both, axis, dim), 0, [])
    for a in arrays:
        done.append(lax.slice_in_dim(whole, at, at + a.shape[along], axis=along))
        at += a.shape[along]
    return tuple(done)


def sent_together_2(arrays, axis, dim, along):
    widths = [a.shape[along] for a in arrays]
    both = jnp.concatenate(arrays, axis=along)
    whole = lax.psum_scatter(both, axis, scatter_dimension=dim, tiled=True)
    return tuple(jnp.split(whole, [sum(widths[:k]) for k in range(1, len(widths))], axis=along))


def sequence_layout(group_ids):
    length = group_ids.shape[0]
    labels = jnp.arange(SEQS + 1, dtype=jnp.int32)
    member = (group_ids[:, None] == labels[None, :]).astype(jnp.int32)
    counts = jnp.sum(member, 0, dtype=jnp.int32)
    lower_ids = (labels[None, :] < group_ids[:, None]).astype(jnp.int32)
    starts = jnp.sum(lower_ids * counts[None, :], 1, dtype=jnp.int32)
    places = jnp.arange(length, dtype=jnp.int32)
    positions = places - starts
    allowed = (group_ids[:, None] == group_ids[None, :]) & (places[None, :] <= places[:, None])
    live_rows = (group_ids < SEQS).astype(jnp.float32)
    return (positions, allowed, live_rows)


def rope_tables(positions):
    steps_half = jnp.arange(ROT // 2, dtype=jnp.float32)
    frequency = ROPE_BASE ** (-2.0 * steps_half / ROT)
    angles = positions.astype(jnp.float32)[:, None] * frequency[None, :]
    angles = jnp.concatenate([angles, angles], 1)
    return (jnp.cos(angles), jnp.sin(angles))


def rotate_fwd(values, cosine, sine):
    half_rot = ROT // 2
    head_part = values[..., :ROT]
    turned = jnp.concatenate([-head_part[..., half_rot:], head_part[..., :half_rot]], -1)
    rotated = head_part * cosine[:, None, :] + turned * sine[:, None, :]
    return jnp.concatenate([rotated, values[..., ROT:]], -1)


def rotate_back(gradient, cosine, sine):
    half_rot = ROT // 2
    head_part = gradient[..., :ROT]
    scaled = head_part * sine[:, None, :]
    turned = jnp.concatenate([scaled[..., half_rot:], -scaled[..., :half_rot]], -1)
    return jnp.concatenate([head_part * cosine[:, None, :] + turned, gradient[..., ROT:]], -1)


def masked_scores(query, key_rows, allowed):
    score_scale = HEAD ** (-0.5)
    scores = (
        jnp.einsum("qhd,khd->hqk", query, key_rows, preferred_element_type=jnp.float32)
        * score_scale
    )
    return jnp.where(allowed[None], scores, MASK_VALUE)


def attend(query, key_rows, value_rows, allowed):
    scores = masked_scores(query, key_rows, allowed)
    peak = jnp.max(scores, -1, keepdims=True)
    expo = jnp.exp(scores - peak)
    row_total = jnp.sum(expo, -1, keepdims=True)
    probs = expo / row_total
    log_total = peak + jnp.log(row_total)
    attended = jnp.einsum(
        "hqk,khd->qhd", probs.astype(jnp.bfloat16), value_rows, preferred_element_type=jnp.float32
    )
    return (attended, log_total)


def attend_back(query, key_rows, value_rows, allowed, log_total, grad_attended):
    score_scale = HEAD ** (-0.5)
    probs = jnp.exp(masked_scores(query, key_rows, allowed) - log_total)
    grad_value = jnp.einsum(
        "hqk,qhd->khd",
        probs.astype(jnp.bfloat16),
        grad_attended,
        preferred_element_type=jnp.float32,
    )
    grad_probs = jnp.einsum(
        "qhd,khd->hqk", grad_attended, value_rows, preferred_element_type=jnp.float32
    )
    inner = jnp.sum(grad_probs * probs, -1, keepdims=True)
    grad_raw = (probs * (grad_probs - inner) * score_scale).astype(jnp.bfloat16)
    grad_query = jnp.einsum("hqk,khd->qhd", grad_raw, key_rows, preferred_element_type=jnp.float32)
    grad_key = jnp.einsum("hqk,qhd->khd", grad_raw, query, preferred_element_type=jnp.float32)
    return (grad_query, grad_key, grad_value)


def adamw(master, moment_one, moment_two, gradient, step_rate, step_decay):
    one_new = BETA_ONE * moment_one + (1.0 - BETA_ONE) * gradient
    two_new = BETA_TWO * moment_two + (1.0 - BETA_TWO) * gradient * gradient
    one_hat = one_new / (1.0 - BETA_ONE**STEP)
    two_hat = two_new / (1.0 - BETA_TWO**STEP)
    master_new = master - step_rate * (
        one_hat / (jnp.sqrt(two_hat) + EPS_ADAM) + step_decay * master
    )
    return (master_new, one_new, two_new)


def on_device(
    hidden_in,
    cotangent,
    seq_ids,
    qkv_weight,
    qkv_first,
    qkv_second,
    out_weight,
    out_first,
    out_second,
    up_weight,
    up_first,
    up_second,
    down_weight,
    down_first,
    down_second,
    qkv_bias,
    qkv_bias_first,
    qkv_bias_second,
    up_bias,
    up_bias_first,
    up_bias_second,
    row_vectors,
    row_first,
    row_second,
):
    tokens_half = hidden_in.shape[0]
    group_len = seq_ids.shape[0]
    gathered = (
        *side_by_side(
            (
                qkv_weight.astype(jnp.bfloat16),
                out_weight.astype(jnp.bfloat16),
                up_weight.astype(jnp.bfloat16),
            ),
            "dp",
            1,
            2,
        ),
        lax.all_gather(down_weight.astype(jnp.bfloat16), "dp", axis=1, tiled=True),
        lax.all_gather(qkv_bias.astype(jnp.bfloat16), "dp", axis=1, tiled=True),
        lax.all_gather(up_bias.astype(jnp.bfloat16), "dp", axis=1, tiled=True),
    )
    qkv_mat, out_mat, up_mat, down_mat, qkv_shift, up_shift = gathered
    heads_here = qkv_shift.shape[1] // (3 * HEAD)
    positions, allowed, live_rows = sequence_layout(seq_ids)
    cosine, sine = rope_tables(positions)
    local_live = lax.dynamic_slice_in_dim(
        live_rows, lax.axis_index("col") * tokens_half, tokens_half
    )
    state = hidden_in.astype(jnp.float32)
    caches = []
    for layer_index in range(LAYERS):
        vectors = row_vectors[layer_index]
        totals = packed_total((jnp.sum(state, 1), jnp.sum(state * state, 1)), "row")
        average = totals[0] / D
        spread = totals[1] / D - average * average
        inv_std = lax.rsqrt(spread + EPS_NORM)
        normal_hat = (state - average[:, None]) * inv_std[:, None]
        attn_in = (normal_hat * vectors[0] + vectors[1]).astype(jnp.bfloat16)
        mlp_in = (normal_hat * vectors[2] + vectors[3]).astype(jnp.bfloat16)
        rows_attn, rows_mlp = side_by_side((attn_in, mlp_in), "col", 0, 1)
        qkv_part = jnp.dot(rows_attn, qkv_mat[layer_index], preferred_element_type=jnp.float32)
        up_part = jnp.dot(rows_mlp, up_mat[layer_index], preferred_element_type=jnp.float32)
        qkv_sum, up_sum = (sent_and_summed(qkv_part, "row", 1), sent_and_summed(up_part, "row", 1))
        joined = (qkv_sum + qkv_shift[layer_index].astype(jnp.float32)).reshape(
            group_len, heads_here, 3 * HEAD
        )
        query = rotate_fwd(joined[..., :HEAD], cosine, sine).astype(jnp.bfloat16)
        key_rows = rotate_fwd(joined[..., HEAD : 2 * HEAD], cosine, sine).astype(jnp.bfloat16)
        value_rows = joined[..., 2 * HEAD :].astype(jnp.bfloat16)
        attended, log_total = attend(query, key_rows, value_rows, allowed)
        attended_low = attended.reshape(group_len, heads_here * HEAD).astype(jnp.bfloat16)
        hidden_pre = up_sum + up_shift[layer_index].astype(jnp.float32)
        activated = jax.nn.gelu(hidden_pre, approximate=False).astype(jnp.bfloat16)
        rows_heads, rows_units = (
            gather_directly(attended_low, "row", 1),
            gather_directly(activated, "row", 1),
        )
        attn_part = jnp.dot(rows_heads, out_mat[layer_index], preferred_element_type=jnp.float32)
        mlp_part = jnp.dot(rows_units, down_mat[layer_index], preferred_element_type=jnp.float32)
        attn_sum, mlp_sum = sent_together((attn_part, mlp_part), "col", 0, 1)
        caches.append(
            (
                inv_std,
                normal_hat,
                rows_attn,
                rows_mlp,
                query,
                key_rows,
                value_rows,
                log_total,
                hidden_pre,
                rows_heads,
                rows_units,
            )
        )
        state = state + attn_sum + vectors[4] + mlp_sum + vectors[5]
    hidden_out = state.astype(jnp.bfloat16)
    grad_state = cotangent.astype(jnp.float32) * local_live[:, None]
    layer_grads = [None] * LAYERS
    vector_parts = [None] * LAYERS
    for layer_index in reversed(range(LAYERS)):
        (
            inv_std,
            normal_hat,
            rows_attn,
            rows_mlp,
            query,
            key_rows,
            value_rows,
            log_total,
            hidden_pre,
            rows_heads,
            rows_units,
        ) = caches[layer_index]
        vectors = row_vectors[layer_index]
        grad_branch = grad_state.astype(jnp.bfloat16)
        branch_bias = jnp.sum(grad_branch.astype(jnp.float32), 0)
        rows_grad = gather_directly(grad_branch, "col", 0)
        grad_out_mat = lax.dot_general(
            rows_heads, rows_grad, CONTRACT_ROWS, preferred_element_type=jnp.float32
        )
        grad_down_mat = lax.dot_general(
            rows_units, rows_grad, CONTRACT_ROWS, preferred_element_type=jnp.float32
        )
        heads_part = lax.dot_general(
            rows_grad, out_mat[layer_index], CONTRACT_COLS, preferred_element_type=jnp.float32
        )
        units_part = lax.dot_general(
            rows_grad, down_mat[layer_index], CONTRACT_COLS, preferred_element_type=jnp.float32
        )
        grad_heads, grad_units = (
            sent_and_summed(heads_part, "row", 1),
            sent_and_summed(units_part, "row", 1),
        )
        gelu_value, gelu_pull = jax.vjp(partial(jax.nn.gelu, approximate=False), hidden_pre)
        grad_pre = gelu_pull(grad_units)[0].astype(jnp.bfloat16)
        grad_attended = grad_heads.reshape(group_len, heads_here, HEAD).astype(jnp.bfloat16)
        grad_query, grad_key, grad_value = attend_back(
            query, key_rows, value_rows, allowed, log_total, grad_attended
        )
        grad_joined = jnp.concatenate(
            [
                rotate_back(grad_query, cosine, sine),
                rotate_back(grad_key, cosine, sine),
                grad_value,
            ],
            -1,
        )
        grad_joined = grad_joined.reshape(group_len, heads_here * 3 * HEAD).astype(jnp.bfloat16)
        grad_qkv_shift = jnp.sum(grad_joined.astype(jnp.float32), 0)
        grad_up_shift = jnp.sum(grad_pre.astype(jnp.float32), 0)
        rows_joined, rows_pre = (
            gather_directly(grad_joined, "row", 1),
            gather_directly(grad_pre, "row", 1),
        )
        grad_qkv_mat = lax.dot_general(
            rows_attn, rows_joined, CONTRACT_ROWS, preferred_element_type=jnp.float32
        )
        grad_up_mat = lax.dot_general(
            rows_mlp, rows_pre, CONTRACT_ROWS, preferred_element_type=jnp.float32
        )
        attn_in_part = lax.dot_general(
            rows_joined, qkv_mat[layer_index], CONTRACT_COLS, preferred_element_type=jnp.float32
        )
        mlp_in_part = lax.dot_general(
            rows_pre, up_mat[layer_index], CONTRACT_COLS, preferred_element_type=jnp.float32
        )
        grad_attn_in, grad_mlp_in = sent_together((attn_in_part, mlp_in_part), "col", 0, 1)
        grad_hat = grad_attn_in * vectors[0] + grad_mlp_in * vectors[2]
        stats = packed_total((jnp.sum(grad_hat, 1), jnp.sum(grad_hat * normal_hat, 1)), "row")
        vector_parts[layer_index] = jnp.stack(
            [
                jnp.sum(grad_attn_in * normal_hat, 0),
                jnp.sum(grad_attn_in, 0),
                jnp.sum(grad_mlp_in * normal_hat, 0),
                jnp.sum(grad_mlp_in, 0),
                branch_bias,
                branch_bias,
            ]
        )
        grad_state = grad_state + inv_std[:, None] * (
            grad_hat - stats[0][:, None] / D - normal_hat * stats[1][:, None] / D
        )
        layer_grads[layer_index] = (
            *sent_together_2((grad_qkv_mat, grad_out_mat, grad_up_mat), "dp", 0, 1),
            lax.psum_scatter(grad_down_mat, "dp", scatter_dimension=0, tiled=True),
            lax.psum_scatter(grad_qkv_shift, "dp", scatter_dimension=0, tiled=True),
            lax.psum_scatter(grad_up_shift, "dp", scatter_dimension=0, tiled=True),
        )
    stacked = tuple(
        (
            jnp.stack([layer_grads[layer_number][member] for layer_number in range(LAYERS)])
            for member in range(6)
        )
    )
    vector_grad = taken_together(jnp.stack(vector_parts), ("dp", "col"))
    qkv_new = adamw(qkv_weight, qkv_first, qkv_second, stacked[0], RATE_MATRIX, DECAY_MATRIX)
    out_new = adamw(out_weight, out_first, out_second, stacked[1], RATE_MATRIX, DECAY_MATRIX)
    up_new = adamw(up_weight, up_first, up_second, stacked[2], RATE_MATRIX, DECAY_MATRIX)
    down_new = adamw(down_weight, down_first, down_second, stacked[3], RATE_MATRIX, DECAY_MATRIX)
    qkv_bias_new = adamw(qkv_bias, qkv_bias_first, qkv_bias_second, stacked[4], RATE_MATRIX, 0.0)
    up_bias_new = adamw(up_bias, up_bias_first, up_bias_second, stacked[5], RATE_MATRIX, 0.0)
    row_new = adamw(row_vectors, row_first, row_second, vector_grad, RATE_VECTOR, 0.0)
    return (
        hidden_out,
        grad_state,
        qkv_new[0],
        qkv_new[1],
        qkv_new[2],
        out_new[0],
        out_new[1],
        out_new[2],
        up_new[0],
        up_new[1],
        up_new[2],
        down_new[0],
        down_new[1],
        down_new[2],
        qkv_bias_new[0],
        qkv_bias_new[1],
        qkv_bias_new[2],
        up_bias_new[0],
        up_bias_new[1],
        up_bias_new[2],
        row_new[0],
        row_new[1],
        row_new[2],
    )


def solution(mesh):
    placed = (
        P(("dp", "col"), "row"),
        P(("dp", "col"), "row"),
        P("dp"),
        P(None, ("row", "dp"), "col"),
        P(None, ("row", "dp"), "col"),
        P(None, ("row", "dp"), "col"),
        P(None, ("col", "dp"), "row"),
        P(None, ("col", "dp"), "row"),
        P(None, ("col", "dp"), "row"),
        P(None, ("row", "dp"), "col"),
        P(None, ("row", "dp"), "col"),
        P(None, ("row", "dp"), "col"),
        P(None, ("col", "dp"), "row"),
        P(None, ("col", "dp"), "row"),
        P(None, ("col", "dp"), "row"),
        P(None, ("col", "row", "dp")),
        P(None, ("col", "row", "dp")),
        P(None, ("col", "row", "dp")),
        P(None, ("col", "row", "dp")),
        P(None, ("col", "row", "dp")),
        P(None, ("col", "row", "dp")),
        P(None, None, "row"),
        P(None, None, "row"),
        P(None, None, "row"),
    )
    return jax.shard_map(
        on_device,
        mesh=mesh,
        in_specs=placed,
        out_specs=(
            P(("dp", "col"), "row"),
            P(("dp", "col"), "row"),
            P(None, ("row", "dp"), "col"),
            P(None, ("row", "dp"), "col"),
            P(None, ("row", "dp"), "col"),
            P(None, ("col", "dp"), "row"),
            P(None, ("col", "dp"), "row"),
            P(None, ("col", "dp"), "row"),
            P(None, ("row", "dp"), "col"),
            P(None, ("row", "dp"), "col"),
            P(None, ("row", "dp"), "col"),
            P(None, ("col", "dp"), "row"),
            P(None, ("col", "dp"), "row"),
            P(None, ("col", "dp"), "row"),
            P(None, ("col", "row", "dp")),
            P(None, ("col", "row", "dp")),
            P(None, ("col", "row", "dp")),
            P(None, ("col", "row", "dp")),
            P(None, ("col", "row", "dp")),
            P(None, ("col", "row", "dp")),
            P(None, None, "row"),
            P(None, None, "row"),
            P(None, None, "row"),
        ),
        check_vma=False,
    )
```

profile of v0, /device:TPU:8, one launch (start us, length us, event | category | flops | bytes accessed | tf_op | source)
XLA Modules:
  0.0 795.8 jit_solution(10199039282103954075)
XLA Ops:
  16.1 22.8 %all-gather.1 = bf16[32,32,2]{1,2,0:T(2,128)(2,1)S(1)} all-gather(bf16[1,32,2]{1,2,0:T(2,128)(2,1)S(1)} %convert_bitcast_fusion), channel_id=1, replica_groups=mesh['dp'=32,'row'=2,'col'=2] {'dp'}, dimensions={0}, use_global_device_ids=true | all-gather | bytes 4224 | tf_op jit(solution)/shard_map/all_gather | solution.py:221
  40.1 20.3 %all-gather = bf16[32,24,2]{1,2,0:T(2,128)(2,1)S(1)} all-gather(bf16[1,24,2]{1,2,0:T(2,128)(2,1)S(1)} %convert_bitcast_fusion.1), channel_id=1, replica_groups=mesh['dp'=32,'row'=2,'col'=2] {'dp'}, dimensions={0}, use_global_device_ids=true | all-gather | bytes 3168 | tf_op jit(solution)/shard_map/all_gather | solution.py:220
  60.8 10.6 %all_gather.18 = bf16[320,1024]{1,0:T(8,128)(2,1)S(1)} all-gather(bf16[160,1024]{1,0:T(8,128)(2,1)S(1)} %pad_maximum_fusion.6), channel_id=1, replica_groups=mesh['dp'=32,'row'=2,'col'=2] {'col'}, dimensions={0}, use_global_device_ids=true | all-gather | bytes 983040 | tf_op jit(solution)/shard_map/all_gather | solution.py:32
  95.6 14.5 %all-to-all-done.1 = f32[2,320,768]{2,1,0:T(8,128)} async-done(((f32[2,320,768]{2,1,0:T(8,128)}), f32[2,320,768]{2,1,0:T(8,128)}, u32[]{:S(2)}, u32[]{:S(2)}) %all-to-all-start.1) | async-done | bytes 1966112 | tf_op jit(solution)/shard_map/all_to_all | solution.py:60
  120.0 26.6 %all-to-all-done.3 = f32[2,320,1024]{2,1,0:T(8,128)} async-done(((f32[2,320,1024]{2,1,0:T(8,128)}), f32[2,320,1024]{2,1,0:T(8,128)}, u32[]{:S(2)}, u32[]{:S(2)}) %all-to-all-start.3) | async-done | bytes 2621472 | tf_op jit(solution)/shard_map/all_to_all | solution.py:60
  164.9 13.5 %all-to-all-done.4 = bf16[2,320,1024]{2,1,0:T(8,128)(2,1)S(1)} async-done(((bf16[2,320,1024]{2,1,0:T(8,128)(2,1)}), bf16[2,320,1024]{2,1,0:T(8,128)(2,1)S(1)}, u32[]{:S(2)}, u32[]{:S(2)}) %all-to-all-start.4) | async-done | bytes 1310752 | tf_op jit(solution)/shard_map/all_to_all | solution.py:38
  185.1 6.0 all-to-all-start.5
  196.3 6.5 all-to-all-done.5
  204.4 5.9 all-to-all-start.12
  223.7 5.2 all-to-all-start.15
  236.0 19.5 %all-to-all-done.15 = f32[2,320,1024]{2,1,0:T(8,128)} async-done(((f32[2,320,1024]{2,1,0:T(8,128)}), f32[2,320,1024]{2,1,0:T(8,128)}, u32[]{:S(2)}, u32[]{:S(2)}) %all-to-all-start.15) | async-done | bytes 2621472 | tf_op jit(solution)/shard_map/all_to_all | solution.py:60
  259.0 9.2 %all_gather.23 = bf16[320,1024]{1,0:T(8,128)(2,1)S(1)} all-gather(bf16[160,1024]{1,0:T(8,128)(2,1)} %pad_maximum_fusion.7), channel_id=1, replica_groups=mesh['dp'=32,'row'=2,'col'=2] {'col'}, dimensions={0}, use_global_device_ids=true | all-gather | bytes 983040 | tf_op jit(solution)/shard_map/all_gather | solution.py:32
  283.2 11.0 %all-to-all-done.7 = f32[2,320,768]{2,1,0:T(8,128)} async-done(((f32[2,320,768]{2,1,0:T(8,128)}), f32[2,320,768]{2,1,0:T(8,128)}, u32[]{:S(2)}, u32[]{:S(2)}) %all-to-all-start.7) | async-done | bytes 1966112 | tf_op jit(solution)/shard_map/all_to_all | solution.py:60
  308.8 13.8 %all-to-all-done.9 = f32[2,320,1024]{2,1,0:T(8,128)} async-done(((f32[2,320,1024]{2,1,0:T(8,128)}), f32[2,320,1024]{2,1,0:T(8,128)}, u32[]{:S(2)}, u32[]{:S(2)}) %all-to-all-start.9) | async-done | bytes 2621472 | tf_op jit(solution)/shard_map/all_to_all | solution.py:60
  324.7 5.6 convert_reduce_fusion
  338.5 12.3 %all-to-all-done.10 = bf16[2,320,1024]{2,1,0:T(8,128)(2,1)} async-done(((bf16[2,320,1024]{2,1,0:T(8,128)(2,1)}), bf16[2,320,1024]{2,1,0:T(8,128)(2,1)}, u32[]{:S(2)}, u32[]{:S(2)}) %all-to-all-start.10) | async-done | bytes 1310752 | tf_op jit(solution)/shard_map/all_to_all | solution.py:38
  382.6 20.2 %all_to_all.139 = bf16[2,320,768]{2,1,0:T(8,128)(2,1)} all-to-all(bf16[2,320,768]{2,1,0:T(8,128)(2,1)S(1)} %broadcast_in_dim.63), channel_id=1, replica_groups=mesh['dp'=32,'row'=2,'col'=2] {'row'}, dimensions={0} | all-to-all | bytes 1966080 | tf_op jit(solution)/shard_map/all_to_all | solution.py:38
  414.8 8.8 %all-to-all-done.16 = bf16[2,320,1024]{2,1,0:T(8,128)(2,1)} async-done(((bf16[2,320,1024]{2,1,0:T(8,128)(2,1)}), bf16[2,320,1024]{2,1,0:T(8,128)(2,1)}, u32[]{:S(2)}, u32[]{:S(2)}) %all-to-all-start.16) | async-done | bytes 1310752 | tf_op jit(solution)/shard_map/all_to_all | solution.py:38
  429.3 6.1 all-to-all-start.17
  440.5 6.0 all-to-all-done.17
  446.5 5.3 all-to-all-start.11
  461.2 5.2 all-to-all-start.18
  474.1 8.6 %all_to_all.140 = bf16[2,160,512]{2,1,0:T(8,128)(2,1)S(1)} all-to-all(bf16[2,160,512]{2,1,0:T(8,128)(2,1)S(1)} %broadcast_in_dim.66), channel_id=1, replica_groups=mesh['dp'=32,'row'=2,'col'=2] {'col'}, dimensions={0} | all-to-all | bytes 655360 | tf_op jit(solution)/shard_map/all_to_all | solution.py:38
  504.9 9.1 %all-to-all-done.20 = f32[2,320,256]{2,1,0:T(8,128)} async-done(((f32[2,320,256]{2,1,0:T(8,128)}), f32[2,320,256]{2,1,0:T(8,128)}, u32[]{:S(2)}, u32[]{:S(2)}) %all-to-all-start.20) | async-done | bytes 655392 | tf_op jit(solution)/shard_map/all_to_all | solution.py:60
  538.2 5.4 all-to-all-done.22
  554.3 5.4 all-to-all-done.21
  570.5 11.4 %all-to-all-done.23 = bf16[2,320,1024]{2,1,0:T(8,128)(2,1)} async-done(((bf16[2,320,1024]{2,1,0:T(8,128)(2,1)}), bf16[2,320,1024]{2,1,0:T(8,128)(2,1)}, u32[]{:S(2)}, u32[]{:S(2)}) %all-to-all-start.23) | async-done | bytes 1310752 | tf_op jit(solution)/shard_map/all_to_all | solution.py:38
  596.9 7.9 all-to-all-start.24
  606.8 6.8 all-to-all-done.24
  618.7 5.2 all-to-all-done.25
  625.6 6.6 all-to-all-start.26
  632.8 142.6 %all-reduce.4 = (f32[768]{0:T(1024)S(1)}, f32[768]{0:T(1024)S(1)}, f32[1024]{0:T(1024)S(1)}, f32[1024]{0:T(1024)S(1)}) all-reduce(f32[768]{0:T(1024)S(1)} %reduce_sum.448, f32[768]{0:T(1024)S(1)} %reduce_sum.446, f32[1024]{0:T(1024)S(1)} %copy-done.101, ...), channel_id=7, replica_groups=mesh['dp'=32,'row'=2,'col'=2] {'dp'}, use_global_device_ids=true, to_apply=%region_39.40.clone | all-reduce | flops 3584 | bytes 28672
  (489 shorter events, 314.3 us)
Async XLA Ops:
  7.3 64.2 %all-gather.5.cloned.1.call-start = ((), (), s32[]{:S(2)}) async-start(), calls=%async_computation.31 | async-start | bytes 8650752 | tf_op jit(solution)/shard_map/all_gather | solution.py:32
  11.7 48.8 %all-to-all-start = ((f32[2,1,320]{2,1,0:T(1,128)}), f32[2,1,320]{2,1,0:T(1,128)S(1)}, u32[]{:S(2)}, u32[]{:S(2)}) async-start(f32[2,1,320]{2,1,0:T(1,128)} %broadcast_in_dim.54), calls=%async_computation | async-start | bytes 6144 | tf_op jit(solution)/shard_map/all_to_all | solution.py:38
  15.3 165.7 %all-gather.7.cloned.1.call-start = ((), (), s32[]{:S(2)}) async-start(), calls=%async_computation.32 | async-start | bytes 4325376 | tf_op jit(solution)/shard_map/all_gather | solution.py:219
  39.9 195.2 %copy-start.94 = (f32[1,1,512]{2,0,1:T(1,128)}, f32[1,1,512]{2,0,1:T(1,128)S(1)}, u32[]{:S(2)}) copy-start(f32[1,1,512]{2,0,1:T(1,128)S(1)} %get-tuple-element.137) | copy-start | bytes 6148
  80.0 30.1 %all-to-all-start.1 = ((f32[2,320,768]{2,1,0:T(8,128)}), f32[2,320,768]{2,1,0:T(8,128)}, u32[]{:S(2)}, u32[]{:S(2)}) async-start(f32[2,320,768]{2,1,0:T(8,128)} %convolution_bitcast_fusion.5), calls=%async_computation.1 | async-start | bytes 3932160 | tf_op jit(solution)/shard_map/all_to_all | solution.py:60
  110.1 36.5 %all-to-all-start.3 = ((f32[2,320,1024]{2,1,0:T(8,128)}), f32[2,320,1024]{2,1,0:T(8,128)}, u32[]{:S(2)}, u32[]{:S(2)}) async-start(f32[2,320,1024]{2,1,0:T(8,128)} %convolution_bitcast_fusion.3), calls=%async_computation.3 | async-start | bytes 5242880 | tf_op jit(solution)/shard_map/all_to_all | solution.py:60
  147.3 10.5 %all-to-all-start.2 = ((bf16[2,320,256]{2,1,0:T(8,128)(2,1)}), bf16[2,320,256]{2,1,0:T(8,128)(2,1)S(1)}, u32[]{:S(2)}, u32[]{:S(2)}) async-start(bf16[2,320,256]{2,1,0:T(8,128)(2,1)} %broadcast_in_dim.57), calls=%async_computation.2 | async-start | bytes 655360 | tf_op jit(solution)/shard_map/all_to_all | solution.py:38
  159.0 19.4 %all-to-all-start.4 = ((bf16[2,320,1024]{2,1,0:T(8,128)(2,1)}), bf16[2,320,1024]{2,1,0:T(8,128)(2,1)S(1)}, u32[]{:S(2)}, u32[]{:S(2)}) async-start(bf16[2,320,1024]{2,1,0:T(8,128)(2,1)} %broadcast_in_dim.58), calls=%async_computation.4 | async-start | bytes 2621440 | tf_op jit(solution)/shard_map/all_to_all | solution.py:38
  185.1 17.7 %all-to-all-start.5 = ((f32[2,160,1024]{2,1,0:T(8,128)}), f32[2,160,1024]{2,1,0:T(8,128)}, u32[]{:S(2)}, u32[]{:S(2)}) async-start(f32[2,160,1024]{2,1,0:T(8,128)} %bitcast.248), calls=%async_computation.5 | async-start | bytes 2621440 | tf_op jit(solution)/shard_map/all_to_all | solution.py:60
  204.4 10.2 %all-to-all-start.12 = ((bf16[2,160,512]{2,1,0:T(8,128)(2,1)}), bf16[2,160,512]{2,1,0:T(8,128)(2,1)}, u32[]{:S(2)}, u32[]{:S(2)}) async-start(bf16[2,160,512]{2,1,0:T(8,128)(2,1)} %broadcast_in_dim.62), calls=%async_computation.12 | async-start | bytes 655360 | tf_op jit(solution)/shard_map/all_to_all | solution.py:38
  215.2 8.5 %all-to-all-start.6 = ((f32[2,1,320]{2,1,0:T(1,128)}), f32[2,1,320]{2,1,0:T(1,128)S(1)}, u32[]{:S(2)}, u32[]{:S(2)}) async-start(f32[2,1,320]{2,1,0:T(1,128)} %broadcast_in_dim.59), calls=%async_computation.6 | async-start | bytes 6144 | tf_op jit(solution)/shard_map/all_to_all | solution.py:38
  223.7 31.8 %all-to-all-start.15 = ((f32[2,320,1024]{2,1,0:T(8,128)}), f32[2,320,1024]{2,1,0:T(8,128)}, u32[]{:S(2)}, u32[]{:S(2)}) async-start(f32[2,320,1024]{2,1,0:T(8,128)} %convolution_bitcast_fusion.1), calls=%async_computation.15 | async-start | bytes 5242880 | tf_op jit(solution)/shard_map/all_to_all | solution.py:60
  255.5 15.6 %all-to-all-start.13 = ((f32[2,320,256]{2,1,0:T(8,128)}), f32[2,320,256]{2,1,0:T(8,128)S(1)}, u32[]{:S(2)}, u32[]{:S(2)}) async-start(f32[2,320,256]{2,1,0:T(8,128)} %convolution_bitcast_fusion.7), calls=%async_computation.13 | async-start | bytes 1310720 | tf_op jit(solution)/shard_map/all_to_all | solution.py:60
  272.0 22.1 %all-to-all-start.7 = ((f32[2,320,768]{2,1,0:T(8,128)}), f32[2,320,768]{2,1,0:T(8,128)}, u32[]{:S(2)}, u32[]{:S(2)}) async-start(f32[2,320,768]{2,1,0:T(8,128)} %convolution_bitcast_fusion.4), calls=%async_computation.7 | async-start | bytes 3932160 | tf_op jit(solution)/shard_map/all_to_all | solution.py:60
  294.2 28.4 %all-to-all-start.9 = ((f32[2,320,1024]{2,1,0:T(8,128)}), f32[2,320,1024]{2,1,0:T(8,128)}, u32[]{:S(2)}, u32[]{:S(2)}) async-start(f32[2,320,1024]{2,1,0:T(8,128)} %convolution_bitcast_fusion.2), calls=%async_computation.9 | async-start | bytes 5242880 | tf_op jit(solution)/shard_map/all_to_all | solution.py:60
  331.9 18.9 %all-to-all-start.10 = ((bf16[2,320,1024]{2,1,0:T(8,128)(2,1)}), bf16[2,320,1024]{2,1,0:T(8,128)(2,1)}, u32[]{:S(2)}, u32[]{:S(2)}) async-start(bf16[2,320,1024]{2,1,0:T(8,128)(2,1)} %broadcast_in_dim.61), calls=%async_computation.10 | async-start | bytes 2621440 | tf_op jit(solution)/shard_map/all_to_all | solution.py:38
  351.5 29.9 %all-to-all-start.8 = ((bf16[2,320,256]{2,1,0:T(8,128)(2,1)}), bf16[2,320,256]{2,1,0:T(8,128)(2,1)}, u32[]{:S(2)}, u32[]{:S(2)}) async-start(bf16[2,320,256]{2,1,0:T(8,128)(2,1)} %broadcast_in_dim.60), calls=%async_computation.8 | async-start | bytes 655360 | tf_op jit(solution)/shard_map/all_to_all | solution.py:38
  355.6 424.6 %reduce-scatter.11.cloned.1.call-start = ((), (), s32[]{:S(2)}) async-start(), calls=%async_computation.36 | async-start | bytes 4325376 | tf_op jit(solution)/shard_map/reduce_scatter | solution.py:367
  404.0 19.6 %all-to-all-start.16 = ((bf16[2,320,1024]{2,1,0:T(8,128)(2,1)}), bf16[2,320,1024]{2,1,0:T(8,128)(2,1)}, u32[]{:S(2)}, u32[]{:S(2)}) async-start(bf16[2,320,1024]{2,1,0:T(8,128)(2,1)} %broadcast_in_dim.64), calls=%async_computation.16 | async-start | bytes 2621440 | tf_op jit(solution)/shard_map/all_to_all | solution.py:38
  429.3 17.2 %all-to-all-start.17 = ((f32[2,160,1024]{2,1,0:T(8,128)}), f32[2,160,1024]{2,1,0:T(8,128)}, u32[]{:S(2)}, u32[]{:S(2)}) async-start(f32[2,160,1024]{2,1,0:T(8,128)} %bitcast.247), calls=%async_computation.17 | async-start | bytes 2621440 | tf_op jit(solution)/shard_map/all_to_all | solution.py:60
  446.5 14.1 %all-to-all-start.11 = ((f32[2,160,1024]{2,1,0:T(8,128)}), f32[2,160,1024]{2,1,0:T(8,128)S(1)}, u32[]{:S(2)}, u32[]{:S(2)}) async-start(f32[2,160,1024]{2,1,0:T(8,128)} %bitcast.246), calls=%async_computation.11 | async-start | bytes 2621440 | tf_op jit(solution)/shard_map/all_to_all | solution.py:60
  461.2 10.5 %all-to-all-start.18 = ((f32[2,1,320]{2,1,0:T(1,128)}), f32[2,1,320]{2,1,0:T(1,128)S(1)}, u32[]{:S(2)}, u32[]{:S(2)}) async-start(f32[2,1,320]{2,1,0:T(1,128)} %broadcast_in_dim.65), calls=%async_computation.18 | async-start | bytes 6144 | tf_op jit(solution)/shard_map/all_to_all | solution.py:38
  466.4 313.9 %reduce-scatter.9.cloned.1.call-start = ((), (), s32[]{:S(2)}) async-start(), calls=%async_computation.35 | async-start | bytes 4325376 | tf_op jit(solution)/shard_map/reduce_scatter | solution.py:367
  485.9 296.4 %reduce-scatter.7.cloned.1.call-start = ((), (), s32[]{:S(2)}) async-start(), calls=%async_computation.34 | async-start | bytes 8650752 | tf_op jit(solution)/shard_map/reduce_scatter | solution.py:86
  497.0 16.9 %all-to-all-start.20 = ((f32[2,320,256]{2,1,0:T(8,128)}), f32[2,320,256]{2,1,0:T(8,128)}, u32[]{:S(2)}, u32[]{:S(2)}) async-start(f32[2,320,256]{2,1,0:T(8,128)} %convolution_bitcast_fusion.6), calls=%async_computation.20 | async-start | bytes 1310720 | tf_op jit(solution)/shard_map/all_to_all | solution.py:60
  513.9 29.7 %all-to-all-start.22 = ((f32[2,320,1024]{2,1,0:T(8,128)}), f32[2,320,1024]{2,1,0:T(8,128)}, u32[]{:S(2)}, u32[]{:S(2)}) async-start(f32[2,320,1024]{2,1,0:T(8,128)} %convolution_bitcast_fusion), calls=%async_computation.22 | async-start | bytes 5242880 | tf_op jit(solution)/shard_map/all_to_all | solution.py:60
  544.7 15.0 %all-to-all-start.21 = ((bf16[2,320,768]{2,1,0:T(8,128)(2,1)}), bf16[2,320,768]{2,1,0:T(8,128)(2,1)}, u32[]{:S(2)}, u32[]{:S(2)}) async-start(bf16[2,320,768]{2,1,0:T(8,128)(2,1)} %broadcast_in_dim.67), calls=%async_computation.21 | async-start | bytes 1966080 | tf_op jit(solution)/shard_map/all_to_all | solution.py:38
  561.0 20.9 %all-to-all-start.23 = ((bf16[2,320,1024]{2,1,0:T(8,128)(2,1)}), bf16[2,320,1024]{2,1,0:T(8,128)(2,1)}, u32[]{:S(2)}, u32[]{:S(2)}) async-start(bf16[2,320,1024]{2,1,0:T(8,128)(2,1)} %broadcast_in_dim.68), calls=%async_computation.23 | async-start | bytes 2621440 | tf_op jit(solution)/shard_map/all_to_all | solution.py:38
  565.7 219.3 %reduce-scatter.5.cloned.1.call-start = ((), (), s32[]{:S(2)}) async-start(), calls=%async_computation.33 | async-start | bytes 8650752 | tf_op jit(solution)/shard_map/reduce_scatter | solution.py:86
  596.9 16.7 %all-to-all-start.24 = ((f32[2,160,1024]{2,1,0:T(8,128)}), f32[2,160,1024]{2,1,0:T(8,128)S(1)}, u32[]{:S(2)}, u32[]{:S(2)}) async-start(f32[2,160,1024]{2,1,0:T(8,128)} %bitcast.85), calls=%async_computation.24 | async-start | bytes 2621440 | tf_op jit(solution)/shard_map/all_to_all | solution.py:60
  615.4 8.5 %all-to-all-start.25 = ((f32[2,1,320]{2,1,0:T(1,128)}), f32[2,1,320]{2,1,0:T(1,128)S(1)}, u32[]{:S(2)}, u32[]{:S(2)}) async-start(f32[2,1,320]{2,1,0:T(1,128)} %broadcast_in_dim.69), calls=%async_computation.25 | async-start | bytes 6144 | tf_op jit(solution)/shard_map/all_to_all | solution.py:38
  625.6 153.4 %all-to-all-start.26 = ((f32[64,2,6,512]{3,1,2,0:T(2,128)}), f32[64,2,6,512]{3,1,2,0:T(2,128)S(1)}, u32[]{:S(2)}, u32[]{:S(2)}) async-start(f32[64,2,6,512]{3,1,2,0:T(2,128)} %broadcast_in_dim.70), calls=%async_computation.30 | async-start | bytes 3145728 | tf_op jit(solution)/shard_map/all_to_all | solution.py:38
  (123 other events, 2259.8 us)
Sparse Core Ops, SparseCore 0:
  11.0 55.4 all-gather.4
  69.4 45.7 all-gather.6
  362.0 84.6 reduce-scatter.10
  486.0 80.5 reduce-scatter.8
  570.2 107.8 reduce-scatter.6
  682.1 92.1 reduce-scatter.4
where the time goes:
time: 809 us; the launch traced here: 796 us
  blocking collectives  234 us (29%)
  waiting for transfers between devices  187 us (23%)
  starting transfers between devices  121 us (15%)
  matrix products  84.3 us (10%)
  other arithmetic  77.6 us (10%)
  local copies, waits for them, and re-layouts  74 us (9%)
  between operations  17.4 us (2%)
    unnamed x1, blocking collectives  143 us
    all_to_all x12, waiting for transfers between devices, sent_and_summed(): lax.all_to_all(in_blocks(array, dim, devices), axis, 0, 0, tiled=True)  123 us
    all_to_all x13, waiting for transfers between devices, copy_for_each(): return lax.all_to_all(copies, axis, split_axis=0, concat_axis=0, tiled=True)  64 us
    all_to_all x12, starting transfers between devices, sent_and_summed(): lax.all_to_all(in_blocks(array, dim, devices), axis, 0, 0, tiled=True)  63.4 us
    all_to_all x13, starting transfers between devices, copy_for_each(): return lax.all_to_all(copies, axis, split_axis=0, concat_axis=0, tiled=True)  57.2 us
    all_to_all x2, blocking collectives, copy_for_each(): return lax.all_to_all(copies, axis, split_axis=0, concat_axis=0, tiled=True)  28.8 us
    all_gather x1, blocking collectives, on_device(): lax.all_gather(up_bias.astype(jnp.bfloat16), 'dp', axis=1, tiled=True)  22.8 us
    reduce_sum x12, other arithmetic, sent_and_summed(): return jnp.sum(tiles, axis=0)  22 us
  transfers between devices with their start and end apart: 31, of which 20 were waited for; matrix products, arithmetic and copies ran while one was open for 25% of the time, Pallas kernels for 0%

commit v1 on v0

v1 whole, which is shorter than its diff:
```python
import math
from functools import partial

import jax
import jax.numpy as jnp
from jax import lax
from jax.experimental import pallas as pl
from jax.experimental.pallas import tpu as pltpu
from jax.sharding import PartitionSpec as P

D = 1024
HEAD = 64
ROT = 16
LAYERS = 2
SEQS = 3
STEP = 10


EPS_NORM = 1e-05
EPS_ADAM = 1e-08
BETA_ONE = 0.9
BETA_TWO = 0.95
RATE_MATRIX = 0.06
RATE_VECTOR = 0.6
DECAY_MATRIX = 0.01
ROPE_BASE = 10000.0
MASK_VALUE = -1e30
CONTRACT_ROWS = (((0,), (0,)), ((), ()))
CONTRACT_COLS = (((1,), (1,)), ((), ()))

BF = jnp.bfloat16
F32 = jnp.float32
MESH = pl.DeviceIdType.MESH
GRIDS = {32: (4, 4, 2), 8: (2, 2, 2)}
VEC_ROWS = 8
VMEM_SPEC = pl.BlockSpec(memory_space=pltpu.VMEM)


def params(collective_id, mib):
    return pltpu.CompilerParams(
        collective_id=collective_id, has_side_effects=True, vmem_limit_bytes=mib << 20
    )


def remote(src, dst, sends, recvs, at, device):
    return pltpu.make_async_remote_copy(
        src_ref=src,
        dst_ref=dst,
        send_sem=sends.at[at],
        recv_sem=recvs.at[at],
        device_id=device,
        device_id_type=MESH,
    )


def greet(device):
    pl.semaphore_signal(
        pltpu.get_barrier_semaphore(), inc=1, device_id=device, device_id_type=MESH
    )


def greeted(count):
    pl.semaphore_wait(pltpu.get_barrier_semaphore(), count)


def group_place():
    return lax.axis_index("row") * 2 + lax.axis_index("col")


def group_peer(place, step):
    other = lax.rem(place + step, 4)
    return {"row": other // 2, "col": lax.rem(other, 2)}


def over(lengths, body):
    total = math.prod(lengths)

    def one(index, carry):
        place, rest = [], index
        for length in reversed(lengths):
            place.append(lax.rem(rest, length))
            rest = rest // length
        body(*reversed(place))
        return carry

    lax.fori_loop(0, total, one, 0)


def sequence_layout(group_ids):
    length = group_ids.shape[0]
    labels = jnp.arange(SEQS + 1, dtype=jnp.int32)
    member = (group_ids[:, None] == labels[None, :]).astype(jnp.int32)
    counts = jnp.sum(member, 0, dtype=jnp.int32)
    lower_ids = (labels[None, :] < group_ids[:, None]).astype(jnp.int32)
    starts = jnp.sum(lower_ids * counts[None, :], 1, dtype=jnp.int32)
    places = jnp.arange(length, dtype=jnp.int32)
    positions = places - starts
    allowed = (group_ids[:, None] == group_ids[None, :]) & (places[None, :] <= places[:, None])
    live_rows = (group_ids < SEQS).astype(jnp.float32)
    return (positions, allowed, live_rows)


def rope_tables(positions):
    steps_half = jnp.arange(ROT // 2, dtype=jnp.float32)
    frequency = ROPE_BASE ** (-2.0 * steps_half / ROT)
    angles = positions.astype(jnp.float32)[:, None] * frequency[None, :]
    angles = jnp.concatenate([angles, angles], 1)
    return (jnp.cos(angles), jnp.sin(angles))


def adamw(master, moment_one, moment_two, gradient, step_rate, step_decay):
    one_new = BETA_ONE * moment_one + (1.0 - BETA_ONE) * gradient
    two_new = BETA_TWO * moment_two + (1.0 - BETA_TWO) * gradient * gradient
    one_hat = one_new / (1.0 - BETA_ONE**STEP)
    two_hat = two_new / (1.0 - BETA_TWO**STEP)
    master_new = master - step_rate * (
        one_hat / (jnp.sqrt(two_hat) + EPS_ADAM) + step_decay * master
    )
    return (master_new, one_new, two_new)


class Copies:
    def __init__(self, sends, recvs):
        self.sends, self.recvs, self.count = sends, recvs, 0

    def to(self, src, dst, device):
        copy = remote(src, dst, self.sends, self.recvs, self.count, device)
        self.count += 1
        return copy


class Ring:
    def __init__(self, length, place, device_at):
        self.length, self.place, self.device_at = length, place, device_at
        self.ways = ((0, 1), (1, -1)) if length > 2 else ((0, 1),)

    def at(self, step):
        return lax.rem(self.place + step + self.length, self.length)

    def device(self, step):
        return self.device_at(self.at(step))


class RingGather:
    def __init__(self, copies, ring, views, sources=None, arrived=None):
        self.copies, self.ring, self.views = copies, ring, views
        self.sources, self.arrived = sources, arrived
        self.near, self.far = [[], []], [[], []]

    def start(self):
        for way, step in self.ring.ways:
            for k, view in enumerate(self.views):
                own = view(self.ring.place, None)
                src = self.sources[k] if self.sources else own
                copy = self.copies.to(src, own, self.ring.device(step))
                copy.start()
                self.near[way].append(copy)

    def middle(self):
        for way, step in self.ring.ways:
            for copy in self.near[way]:
                copy.wait_recv()
            came_from = self.ring.at(-step)
            if self.ring.length > 2:
                for view in self.views:
                    ref = view(came_from, way)
                    if ref is not None:
                        copy = self.copies.to(ref, ref, self.ring.device(step))
                        copy.start()
                        self.far[way].append(copy)
            if self.arrived:
                self.arrived(came_from)

    def end(self):
        for copy in self.far[0] + self.far[1]:
            copy.wait_recv()
        if self.arrived and self.ring.length > 2:
            self.arrived(self.ring.at(2))

    def finish(self):
        for copy in self.near[0] + self.near[1] + self.far[0] + self.far[1]:
            copy.wait_send()


class Summand:
    def __init__(self, ref, index, count, width, near, far):
        self.ref, self.index, self.count, self.width = ref, index, count, width
        self.near, self.far = near, far

    def view(self, target, start, width):
        return self.ref.at[self.index(slice(None), target, start, width)]

    def add(self, target, start, width, other):
        def one(lead):
            at = self.index(lead, target, start, width)
            more = other[...] if self.count is None else other[lead]
            self.ref[at] = (self.ref[at].astype(F32) + more.astype(F32)).astype(BF)

        if self.count is None:
            one(None)
        else:
            over((self.count,), one)

    def total(self, lead, target, ways):
        value = self.ref[self.index(lead, target, 0, self.width)].astype(F32)
        for way in range(ways):
            more = self.far[way][...] if self.count is None else self.far[way][lead]
            value = value + more.astype(F32)
        return value


class RingSum:
    def __init__(self, copies, ring, summands):
        self.copies, self.ring, self.summands = copies, ring, summands
        self.near, self.far = [[], []], [[], []]

    def start(self):
        if self.ring.length == 2:
            return
        for way, step in self.ring.ways:
            for s in self.summands:
                half = s.width // 2
                copy = self.copies.to(
                    s.view(self.ring.at(2), way * half, half), s.near[way], self.ring.device(step)
                )
                copy.start()
                self.near[way].append(copy)

    def middle(self):
        for way, step in self.ring.ways:
            target = self.ring.at(step)
            for k, s in enumerate(self.summands):
                if self.ring.length > 2:
                    self.near[way][k].wait_recv()
                    s.add(target, way * (s.width // 2), s.width // 2, s.near[way])
                copy = self.copies.to(
                    s.view(target, 0, s.width), s.far[way], self.ring.device(step)
                )
                copy.start()
                self.far[way].append(copy)

    def end(self):
        for copy in self.far[0] + self.far[1]:
            copy.wait_recv()

    def total(self, k, lead=None):
        return self.summands[k].total(lead, self.ring.place, len(self.ring.ways))

    def finish(self):
        for copy in self.near[0] + self.near[1] + self.far[0] + self.far[1]:
            copy.wait_send()


def lanes_at(start, width):
    if not isinstance(start, int):
        start = pl.multiple_of(start, 128)
    return pl.ds(start, width)


class Slice:
    def __init__(self, grid):
        self.grid = grid
        nz, nx, nc = grid
        d = lax.axis_index("dp")
        self.d, self.z, self.x, self.core = d, d // (nx * nc), lax.rem(d // nc, nx), lax.rem(d, nc)
        self.row, self.col = lax.axis_index("row"), lax.axis_index("col")
        self.half = nz * nx * nc // 2
        self.place = group_place()
        self.zls = nz // 2
        self.partner = self.dp(self.z, self.x, 1 - self.core)
        self.z_ring = Ring(nz, self.z, lambda z: self.dp(z, self.x, self.core))
        self.x_ring = Ring(nx, self.x, lambda x: self.dp(self.z, x, self.core))
        self.y_ring = Ring(4, self.place, lambda q: {"row": q // 2, "col": lax.rem(q, 2)})

    def dp(self, z, x, core):
        _, nx, nc = self.grid
        return {"dp": (z * nx + x) * nc + core}

    def greet_rings(self, rings, whole=False):
        count = 0
        for ring in rings:
            steps = range(1, ring.length) if whole else [step for _, step in ring.ways]
            for step in steps:
                greet(ring.device(step))
                count += 1
        return count


class WeightGather:
    def __init__(self, here, cut, copies, local, wa, wb, wc, full_a, full_b, full_c):
        self.here, self.copies, self.core_copies = here, copies, []
        grid = here.grid
        lanes = wb.shape[-1]
        a_rows, a_lanes, b_rows = wa.shape[0], wa.shape[1], wb.shape[0]
        a_cut = (pl.ds(0, a_rows // 2), pl.ds(a_rows // 2, a_rows // 2))
        b_cut = (pl.ds(0, cut), pl.ds(cut, b_rows - cut))
        z, x, core, zls = here.z, here.x, here.core, here.zls

        def part(width, half):
            return (0, width) if half is None else (half * (width // 2), width // 2)

        def chunk(order, kind, along, half):
            zz, xx = (along, x) if order == 0 else (z, along)
            if kind == "a":
                return full_a.at[zz, xx, core, a_cut[order], pl.ds(*part(a_lanes, half))]
            if kind == "b":
                start, width = part(lanes, half)
                at = lanes_at((zz // zls) * lanes + start, width)
                return full_b.at[lax.rem(zz, zls), xx, core, b_cut[order], at]
            return None if half == 1 else full_c.at[zz, xx, core]

        def line(order, kind, along, half):
            if kind == "a":
                at = pl.ds(*part(a_lanes, half))
                if order == 0:
                    return full_a.at[:, along, core, a_cut[0], at]
                return full_a.at[along, :, core, a_cut[1], at]
            if kind == "b":
                if order == 0:
                    return full_b.at[:, along, core, b_cut[0], pl.ds(*part(2 * lanes, half))]
                start, width = part(lanes, half)
                at = lanes_at((along // zls) * lanes + start, width)
                return full_b.at[lax.rem(along, zls), :, core, b_cut[1], at]
            return None if half == 1 else full_c.at[:, along, core]

        rings = ((here.z_ring, here.x_ring), (here.x_ring, here.z_ring))
        self.first, self.second, self.lines, self.own = [], [], [], []
        for order in range(2):
            kinds = ["a", "b", "c"] if order == 0 and wc is not None else ["a", "b"]
            sources = [wa.at[a_cut[order]], wb.at[b_cut[order]], wc][: len(kinds)]
            chunks = [partial(chunk, order, kind) for kind in kinds]
            lines = [partial(line, order, kind) for kind in kinds]
            for k, view in enumerate(chunks):
                self.own.append(
                    pltpu.make_async_copy(
                        sources[k], view(rings[order][0].place, None), local.at[order * 3 + k]
                    )
                )
            self.first.append(RingGather(copies, rings[order][0], chunks, sources))
            self.second.append(
                RingGather(copies, rings[order][1], lines, None, partial(self.forward, order))
            )
            self.lines.append(lines)

    def forward(self, order, along):
        for view in self.lines[order]:
            ref = view(along, None)
            copy = self.copies.to(ref, ref, self.here.partner)
            copy.start()
            self.core_copies.append(copy)

    def start(self):
        for ring in self.first:
            ring.start()
        for copy in self.own:
            copy.start()

    def first_middle(self):
        for ring in self.first:
            ring.middle()

    def turn(self):
        for copy in self.own:
            copy.wait()
        for order in range(2):
            self.first[order].end()
            self.second[order].start()
            self.forward(order, self.second[order].ring.place)

    def second_middle(self):
        for ring in self.second:
            ring.middle()

    def end(self):
        for ring in self.second:
            ring.end()

    def finish(self):
        for ring in self.first + self.second:
            ring.finish()
        for copy in self.core_copies:
            copy.wait()


def start_kernel(
    grid,
    cut,
    hid,
    cot,
    vec,
    wa,
    wb,
    wc,
    hid_all,
    cot_all,
    vec_all,
    wa_one,
    wb_one,
    full_a,
    full_b,
    full_c,
    wa_zero,
    wb_zero,
    sends,
    recvs,
    local,
):
    here = Slice(grid)
    d, r, c, half = here.d, here.row, here.col, here.half
    rows, lanes = hid.shape
    slot_rows = wa.shape[2]
    dh, dl = d // half, lax.rem(d, half)
    swap_needed = dh != r
    swap_to = {"dp": r * half + dl, "row": dh}
    a_target = r * half + d // 2
    slot = pl.ds(pl.multiple_of(lax.rem(d, 2) * slot_rows, slot_rows), slot_rows)
    a_selfs = [(r == k) & (a_target == d) for k in range(2)]
    a_from = [2 * dl + k for k in range(2)]
    from_selfs = [(dh == r) & (a_from[k] == d) for k in range(2)]

    count = here.greet_rings([here.z_ring, here.x_ring])
    count += here.greet_rings([here.y_ring], whole=True)
    greet(here.partner)
    for k in range(2):

        @pl.when(jnp.logical_not(from_selfs[k]))
        def _():
            greet({"dp": a_from[k], "row": dh})

    @pl.when(swap_needed)
    def _():
        greet(swap_to)

    greeted(
        count + 3 + swap_needed.astype(jnp.int32) - sum(k.astype(jnp.int32) for k in a_selfs)
    )

    copies = Copies(sends, recvs)
    copies.count = 16
    a_own, b_own = (wa_zero, wa_one), (wb_zero, wb_one)

    def a_copy(layer, k):
        return pltpu.make_async_remote_copy(
            src_ref=wa.at[layer, k],
            dst_ref=a_own[layer].at[slot],
            send_sem=sends.at[layer * 8 + k],
            recv_sem=recvs.at[layer * 8 + lax.rem(d, 2)],
            device_id={"dp": a_target, "row": k},
            device_id_type=MESH,
        )

    def a_arrival(layer, k):
        return pltpu.make_async_remote_copy(
            src_ref=wa.at[layer, 0],
            dst_ref=a_own[layer].at[pl.ds(k * slot_rows, slot_rows)],
            send_sem=sends.at[layer * 8],
            recv_sem=recvs.at[layer * 8 + k],
            device_id={"dp": a_from[k], "row": dh},
            device_id_type=MESH,
        )

    def a_local(layer, k):
        return pltpu.make_async_copy(wa.at[layer, k], a_own[layer].at[slot], local.at[8 + layer])

    def swap_copy(layer):
        return remote(wb.at[layer], b_own[layer], sends, recvs, layer * 8 + 2, swap_to)

    def swap_local(layer):
        return pltpu.make_async_copy(wb.at[layer], b_own[layer], local.at[10 + layer])

    def begin(layer):
        for k in range(2):

            @pl.when(jnp.logical_not(a_selfs[k]))
            def _():
                a_copy(layer, k).start()

            @pl.when(a_selfs[k])
            def _():
                a_local(layer, k).start()

        @pl.when(swap_needed)
        def _():
            swap_copy(layer).start()

        @pl.when(jnp.logical_not(swap_needed))
        def _():
            swap_local(layer).start()

    def complete(layer):
        for k in range(2):

            @pl.when(jnp.logical_not(a_selfs[k]))
            def _():
                a_copy(layer, k).wait_send()

            @pl.when(a_selfs[k])
            def _():
                a_local(layer, k).wait()

            @pl.when(jnp.logical_not(from_selfs[k]))
            def _():
                a_arrival(layer, k).wait_recv()

        @pl.when(swap_needed)
        def _():
            swap_copy(layer).wait()

        @pl.when(jnp.logical_not(swap_needed))
        def _():
            swap_local(layer).wait()

    begin(0)
    tokens = pl.ds(pl.multiple_of(c * rows, rows), rows)
    features = pl.ds(pl.multiple_of(r * lanes, lanes), lanes)
    small = []
    for ref, dst in (
        (hid, hid_all.at[tokens, features]),
        (cot, cot_all.at[tokens, features]),
    ):
        for step in range(1, 4):
            small.append(copies.to(ref, dst, here.y_ring.device(step)))
    small.append(copies.to(vec, vec_all.at[:, features], {"row": 1 - r}))
    for copy in small[:3] + small[6:]:
        copy.start()
    own = [
        pltpu.make_async_copy(hid, hid_all.at[tokens, features], local.at[12]),
        pltpu.make_async_copy(cot, cot_all.at[tokens, features], local.at[13]),
        pltpu.make_async_copy(vec, vec_all.at[:, features], local.at[14]),
    ]
    for copy in own:
        copy.start()
    complete(0)
    weights = WeightGather(
        here, cut, copies, local, wa_zero, wb_zero, wc, full_a, full_b, full_c
    )
    weights.start()
    begin(1)
    for copy in small[3:6]:
        copy.start()
    weights.first_middle()
    weights.turn()
    weights.second_middle()
    weights.end()
    for copy in small + own:
        copy.wait()
    complete(1)
    weights.finish()


def full_shapes(grid, a_shape, b_shape):
    nz, nx, nc = grid
    return (
        jax.ShapeDtypeStruct((nz, nx, nc, *a_shape), BF),
        jax.ShapeDtypeStruct((nz // 2, nx, nc, b_shape[0], 2 * b_shape[1]), BF),
    )


def start_exchange(grid, cut, hid, cot, vec, wa, wb, wc):
    rows, lanes = hid.shape
    a_shape, b_shape = (2 * wa.shape[2], wa.shape[3]), wb.shape[1:]
    token_rows = jax.ShapeDtypeStruct((2 * rows, 2 * lanes), BF)
    return pl.pallas_call(
        partial(start_kernel, grid, cut),
        out_shape=(
            token_rows,
            token_rows,
            jax.ShapeDtypeStruct((vec.shape[0], 2 * lanes), F32),
            jax.ShapeDtypeStruct(a_shape, BF),
            jax.ShapeDtypeStruct(b_shape, BF),
            *full_shapes(grid, a_shape, b_shape),
            jax.ShapeDtypeStruct((*grid, *wc.shape), BF),
        ),
        in_specs=[VMEM_SPEC] * 6,
        out_specs=(VMEM_SPEC,) * 8,
        scratch_shapes=[
            pltpu.VMEM(a_shape, BF),
            pltpu.VMEM(b_shape, BF),
            pltpu.SemaphoreType.DMA((96,)),
            pltpu.SemaphoreType.DMA((96,)),
            pltpu.SemaphoreType.DMA((16,)),
        ],
        compiler_params=params(0, 40),
        name="start_exchange",
    )(hid, cot, vec, wa, wb, wc)


def dot(left, right):
    return jnp.dot(left, right, preferred_element_type=F32)


def dot_rows(left, right):
    return lax.dot_general(left, right, CONTRACT_ROWS, preferred_element_type=F32)


def dot_cols(left, right):
    return lax.dot_general(left, right, CONTRACT_COLS, preferred_element_type=F32)


def norm_stats(state):
    width = state.shape[1]
    average = jnp.sum(state, 1, keepdims=True) / width
    spread = jnp.sum(state * state, 1, keepdims=True) / width - average * average
    inv_std = lax.rsqrt(spread + EPS_NORM)
    return ((state - average) * inv_std, inv_std)


def norm_back(grad_hat, hat):
    width = hat.shape[1]
    first = jnp.sum(grad_hat, 1, keepdims=True) / width
    second = jnp.sum(grad_hat * hat, 1, keepdims=True) / width
    return grad_hat - first - hat * second


class Layer:
    def __init__(self, layer, vec, tables, mask, bias, full_a, full_b, sizes):
        self.vec, self.tables, self.mask, self.bias = vec, tables, mask, bias
        self.layer, self.full_a, self.full_b = layer, full_a, full_b
        self.qkv_width, self.up_width, self.out_rows = sizes
        self.heads_here = self.qkv_width // (3 * HEAD)

    def vector(self, k):
        at = self.layer * VEC_ROWS + k
        return self.vec[at : at + 1, :]

    def a_matrix(self, start, width):
        value = self.full_a[:, :, :, :, start : start + width]
        return value.reshape(-1, width)

    def b_matrix(self, low, high, start, width):
        value = self.full_b[:, :, :, low:high, start : start + width]
        return value.reshape(-1, width)

    def out_matrix(self, start, width):
        return self.b_matrix(0, self.out_rows, start, width)

    def down_matrix(self, start, width):
        return self.b_matrix(self.out_rows, self.full_b.shape[3], start, width)

    def inputs(self, hat, attn_in, mlp_in):
        attn_in[...] = (hat * self.vector(0) + self.vector(1)).astype(BF)
        mlp_in[...] = (hat * self.vector(2) + self.vector(3)).astype(BF)

    def project(self, attn_in, joined):
        pair = 6 * HEAD
        cosine, left, right = self.tables
        for start in range(0, self.qkv_width, pair):
            value = dot(attn_in[...], self.a_matrix(start, pair))
            value = value + self.bias[0:1, start : start + pair]
            value = (
                value * cosine[...]
                + pltpu.roll(value, pair - ROT // 2, 1) * left[...]
                + pltpu.roll(value, ROT // 2, 1) * right[...]
            )
            joined[:, start : start + pair] = value.astype(BF)

    def head(self, joined, h):
        start = h * 3 * HEAD
        return [joined[:, start + k * HEAD : start + (k + 1) * HEAD] for k in range(3)]

    def attend(self, joined, probs, heads):
        for h in range(self.heads_here):
            query, key_rows, value_rows = self.head(joined, h)
            scores = dot_cols(query, key_rows) * HEAD**-0.5 + self.mask[...]
            expo = jnp.exp(scores - jnp.max(scores, 1, keepdims=True))
            low = (expo / jnp.sum(expo, 1, keepdims=True)).astype(BF)
            probs[h] = low
            heads[:, h * HEAD : (h + 1) * HEAD] = dot(low, value_rows).astype(BF)

    def units(self, mlp_in, pre, units):
        width = 256
        for start in range(0, self.up_width, width):
            at = slice(start, start + width)
            value = dot(mlp_in[...], self.a_matrix(self.qkv_width + start, width))
            value = value + self.bias[1:2, at]
            pre[:, at] = value
            units[:, at] = (0.5 * value * (1.0 + lax.erf(value * 0.5**0.5))).astype(BF)

    def outputs(self, heads, units, start, width):
        return dot(heads[...], self.out_matrix(start, width)) + dot(
            units[...], self.down_matrix(start, width)
        )

    def branch_back(self, grad, pre, grad_heads, grad_pre):
        grad_heads[...] = dot_cols(grad[...], self.out_matrix(0, D)).astype(BF)
        zls, nx, nc = self.full_b.shape[:3]
        depth = self.full_b.shape[3] - self.out_rows
        count = nx * nc
        for zl in range(zls):
            matrix = self.full_b[zl, :, :, self.out_rows :, :].reshape(-1, D)
            width = depth * count
            for start in range(0, width, 256):
                at = slice(zl * width + start, zl * width + start + 256)
                value = pre[:, at]
                slope = 0.5 * (1.0 + lax.erf(value * 0.5**0.5)) + value * jnp.exp(
                    value * value * -0.5
                ) * ((2.0 * math.pi) ** -0.5)
                pull = dot_cols(grad[...], matrix[start : start + 256])
                grad_pre[:, at] = (pull * slope).astype(BF)

    def attend_back(self, joined, probs, grad_heads, raw, grad_joined):
        for h in range(self.heads_here):
            query, key_rows, value_rows = self.head(joined, h)
            grad = grad_heads[:, h * HEAD : (h + 1) * HEAD]
            low = probs[h]
            high = low.astype(F32)
            grad_probs = dot_cols(grad, value_rows)
            inner = jnp.sum(grad_probs * high, 1, keepdims=True)
            grad_raw = (high * (grad_probs - inner) * HEAD**-0.5).astype(BF)
            start = h * 3 * HEAD
            raw[:, start : start + HEAD] = dot(grad_raw, key_rows)
            raw[:, start + HEAD : start + 2 * HEAD] = dot_rows(grad_raw, query)
            raw[:, start + 2 * HEAD : start + 3 * HEAD] = dot_rows(low, grad)
        pair = 6 * HEAD
        cosine, left, right = self.tables
        for start in range(0, self.qkv_width, pair):
            value = raw[:, start : start + pair]
            value = (
                value * cosine[...]
                + pltpu.roll(value * left[...], ROT // 2, 1)
                + pltpu.roll(value * right[...], pair - ROT // 2, 1)
            )
            grad_joined[:, start : start + pair] = value.astype(BF)

    def inputs_back(self, grad_joined, grad_pre, hat, grad, sums):
        grad_attn_in = dot_cols(grad_joined[...], self.a_matrix(0, self.qkv_width))
        rows = [
            jnp.sum(grad_attn_in * hat, 0, keepdims=True),
            jnp.sum(grad_attn_in, 0, keepdims=True),
        ]
        grad_hat = grad_attn_in * self.vector(0)
        grad_mlp_in = dot_cols(grad_pre[...], self.a_matrix(self.qkv_width, self.up_width))
        rows += [
            jnp.sum(grad_mlp_in * hat, 0, keepdims=True),
            jnp.sum(grad_mlp_in, 0, keepdims=True),
            jnp.sum(grad[...].astype(F32), 0, keepdims=True) * 0.25,
        ]
        for k, row in enumerate(rows):
            sums[k : k + 1, :] = row
        for k, (ref, width) in enumerate(
            ((grad_joined, self.qkv_width), (grad_pre, self.up_width))
        ):
            sums[5 + k : 6 + k, :] = jnp.zeros((1, D), F32)
            sums[5 + k : 6 + k, :width] = jnp.sum(ref[...].astype(F32), 0, keepdims=True)
        sums[7:8, :] = jnp.zeros((1, D), F32)
        return norm_back(grad_hat + grad_mlp_in * self.vector(2), hat)


def grads_a(left, right, out, start):
    width = right.shape[1]
    nz = out.shape[0]
    block = left.shape[1] // nz
    for k in range(nz):
        value = dot_rows(left[:, k * block : (k + 1) * block], right[...]).astype(BF)
        out[k, :, :, :, start : start + width] = value.reshape(*out.shape[1:4], width)


def grads_b(left, right, out, low, high):
    zls = out.shape[0]
    block = left.shape[1] // zls
    for k in range(zls):
        value = dot_rows(left[:, k * block : (k + 1) * block], right[...]).astype(BF)
        out[k, :, :, low:high, :] = value.reshape(*out.shape[1:3], high - low, D)


def rows_index(rows):
    def index(lead, target, start, width):
        return (
            pl.ds(pl.multiple_of(target * rows, rows), rows),
            lanes_at(start, width),
        )

    return index


def blocks_index(rows, lanes):
    def index(lead, target, start, width):
        return (
            pl.ds(pl.multiple_of(lax.rem(target, 2) * rows, rows), rows),
            lanes_at((target // 2) * lanes + start, width),
        )

    return index


def group_sum(here, copies, part, index, width, near, far):
    summand = Summand(part, index, None, width, (near.at[0], near.at[1]), (far.at[0], far.at[1]))
    return RingSum(copies, here.y_ring, [summand])


def group_gather(here, copies, whole, rows):
    def view(target, half):
        width = whole.shape[1]
        start, width = (0, width) if half is None else (half * (width // 2), width // 2)
        return whole.at[pl.ds(pl.multiple_of(target * rows, rows), rows), pl.ds(start, width)]

    return RingGather(copies, here.y_ring, [view])


def own_rows(here, rows):
    return pl.ds(pl.multiple_of(here.place * rows, rows), rows)


def ring_scratch(rows, width):
    return [pltpu.VMEM((2, rows, width // 2), BF), pltpu.VMEM((2, rows, width), BF)]


def first_kernel(
    grid,
    cut,
    sizes,
    hid_all,
    vec,
    cosine,
    left,
    right,
    mask,
    bias,
    full_a,
    full_b,
    wa,
    wb,
    state_new,
    inv_std,
    hat_all,
    joined,
    probs,
    heads,
    pre,
    units,
    next_a,
    next_b,
    attn_in,
    mlp_in,
    part,
    near,
    far,
    sends,
    recvs,
    local,
):
    here = Slice(grid)
    copies = Copies(sends, recvs)
    rows = state_new.shape[0]
    count = here.greet_rings([here.z_ring, here.x_ring, here.y_ring])
    greet(here.partner)
    greeted(count + 1)
    weights = WeightGather(here, cut, copies, local, wa, wb, None, next_a, next_b, None)
    weights.start()
    layer = Layer(0, vec, (cosine, left, right), mask, bias, full_a, full_b, sizes)
    hat, _ = norm_stats(hid_all[...].astype(F32))
    layer.inputs(hat, attn_in, mlp_in)
    layer.project(attn_in, joined)
    weights.first_middle()
    layer.attend(joined, probs, heads)
    weights.turn()
    layer.units(mlp_in, pre, units)
    weights.second_middle()
    for start in (0, D // 2):
        part[:, start : start + D // 2] = layer.outputs(heads, units, start, D // 2).astype(BF)
    summed = group_sum(here, copies, part, rows_index(rows), D, near, far)
    summed.start()
    weights.end()
    summed.middle()
    mine = own_rows(here, rows)
    state = hid_all[mine, :].astype(F32) + layer.vector(4) + layer.vector(5)
    summed.end()
    state = state + summed.total(0)
    state_new[...] = state
    hat, inverse = norm_stats(state)
    inv_std[...] = jnp.broadcast_to(inverse, inv_std.shape)
    hat_all[mine, :] = hat.astype(BF)
    spread = group_gather(here, copies, hat_all, rows)
    spread.start()
    spread.middle()
    spread.end()
    summed.finish()
    spread.finish()
    weights.finish()


def first_layer(grid, cut, sizes, hid_all, vec, tables, mask, bias, full_a, full_b, wa, wb):
    tokens = hid_all.shape[0]
    rows = tokens // 4
    qkv_width, up_width, _ = sizes
    heads_here = qkv_width // (3 * HEAD)
    shape = jax.ShapeDtypeStruct
    return pl.pallas_call(
        partial(first_kernel, grid, cut, sizes),
        out_shape=(
            shape((rows, D), F32),
            shape((rows, 128), F32),
            shape((tokens, D), BF),
            shape((tokens, qkv_width), BF),
            shape((heads_here, tokens, tokens), BF),
            shape((tokens, heads_here * HEAD), BF),
            shape((tokens, up_width), F32),
            shape((tokens, up_width), BF),
            *full_shapes(grid, wa.shape, wb.shape),
        ),
        in_specs=[VMEM_SPEC] * 11,
        out_specs=(VMEM_SPEC,) * 10,
        scratch_shapes=[
            pltpu.VMEM((tokens, D), BF),
            pltpu.VMEM((tokens, D), BF),
            pltpu.VMEM((tokens, D), BF),
            *ring_scratch(rows, D),
            pltpu.SemaphoreType.DMA((64,)),
            pltpu.SemaphoreType.DMA((64,)),
            pltpu.SemaphoreType.DMA((6,)),
        ],
        compiler_params=params(1, 56),
        name="first_layer",
    )(hid_all, vec, *tables, mask, bias, full_a, full_b, wa, wb)


def last_kernel(
    grid,
    sizes,
    hat_all,
    vec,
    cosine,
    left,
    right,
    mask,
    bias,
    full_a,
    full_b,
    state,
    inv_std,
    cot,
    live,
    hidden,
    grad_new,
    grad_all,
    ga,
    gb,
    sums,
    attn_in,
    mlp_in,
    joined,
    probs,
    heads,
    pre,
    units,
    part,
    back,
    grad,
    grad_heads,
    grad_pre,
    raw,
    grad_joined,
    near,
    far,
    near_back,
    far_back,
    sends,
    recvs,
):
    here = Slice(grid)
    copies = Copies(sends, recvs)
    rows = state.shape[0]
    greeted(here.greet_rings([here.y_ring]))
    layer = Layer(1, vec, (cosine, left, right), mask, bias, full_a, full_b, sizes)
    layer.inputs(hat_all[...].astype(F32), attn_in, mlp_in)
    layer.project(attn_in, joined)
    layer.attend(joined, probs, heads)
    layer.units(mlp_in, pre, units)
    mine = own_rows(here, rows)
    for start in (0, D // 2):
        part[:, start : start + D // 2] = layer.outputs(heads, units, start, D // 2).astype(BF)
    part[mine, :] = (part[mine, :].astype(F32) + state[...]).astype(BF)
    summed = group_sum(
        here, copies, part, blocks_index(2 * rows, D // 2), D // 2, near, far
    )
    summed.start()
    grad[...] = (cot[...].astype(F32) * live[:, :1]).astype(BF)
    layer.branch_back(grad, pre, grad_heads, grad_pre)
    summed.middle()
    layer.attend_back(joined, probs, grad_heads, raw, grad_joined)
    back[...] = layer.inputs_back(
        grad_joined, grad_pre, hat_all[...].astype(F32), grad, sums
    ).astype(BF)
    summed_back = group_sum(here, copies, back, rows_index(rows), D, near_back, far_back)
    summed_back.start()
    summed.end()
    features = pl.ds(pl.multiple_of(here.row * (D // 2), D // 2), D // 2)
    bias_sum = vec[VEC_ROWS + 4 : VEC_ROWS + 5, features] + vec[VEC_ROWS + 5 : VEC_ROWS + 6, features]
    hidden[...] = (summed.total(0) + bias_sum).astype(BF)
    grads_a(attn_in, grad_joined, ga, 0)
    summed_back.middle()
    grads_a(mlp_in, grad_pre, ga, grad_joined.shape[1])
    summed_back.end()
    total = grad[mine, :].astype(F32) + inv_std[:, :1] * summed_back.total(0)
    grad_new[...] = total
    grad_all[mine, :] = total.astype(BF)
    spread = group_gather(here, copies, grad_all, rows)
    spread.start()
    grads_b(heads, grad, gb, 0, sizes[2])
    spread.middle()
    grads_b(units, grad, gb, sizes[2], gb.shape[3])
    spread.end()
    for ring in (summed, summed_back, spread):
        ring.finish()


def last_layer(
    grid, sizes, hat_all, vec, tables, mask, bias, full_a, full_b, state, inv_std, cot, live
):
    tokens = hat_all.shape[0]
    rows = tokens // 4
    qkv_width, up_width, _ = sizes
    heads_here = qkv_width // (3 * HEAD)
    shape = jax.ShapeDtypeStruct

    def low(*dims):
        return pltpu.VMEM(dims, BF)

    return pl.pallas_call(
        partial(last_kernel, grid, sizes),
        out_shape=(
            shape((2 * rows, D // 2), BF),
            shape((rows, D), F32),
            shape((tokens, D), BF),
            shape(full_a.shape, BF),
            shape(full_b.shape, BF),
            shape((VEC_ROWS, D), F32),
        ),
        in_specs=[VMEM_SPEC] * 13,
        out_specs=(VMEM_SPEC,) * 6,
        scratch_shapes=[
            low(tokens, D),
            low(tokens, D),
            low(tokens, qkv_width),
            low(heads_here, tokens, tokens),
            low(tokens, heads_here * HEAD),
            pltpu.VMEM((tokens, up_width), F32),
            low(tokens, up_width),
            low(tokens, D),
            low(tokens, D),
            low(tokens, D),
            low(tokens, heads_here * HEAD),
            low(tokens, up_width),
            pltpu.VMEM((tokens, qkv_width), F32),
            low(tokens, qkv_width),
            *ring_scratch(2 * rows, D // 2),
            *ring_scratch(rows, D),
            pltpu.SemaphoreType.DMA((32,)),
            pltpu.SemaphoreType.DMA((32,)),
        ],
        compiler_params=params(2, 56),
        name="last_layer",
    )(hat_all, vec, *tables, mask, bias, full_a, full_b, state, inv_std, cot, live)


class GradSum:
    def __init__(self, here, cut, copies, kind, g, s, buffers):
        self.here, self.copies, self.kind, self.g, self.s = here, copies, kind, g, s
        self.near, self.far, self.mid, self.near_two, self.far_two, self.fin = buffers
        rows = g.shape[3]
        first = rows // 2 if kind == "a" else cut
        self.cuts = (pl.ds(0, first), pl.ds(first, rows - first))
        self.full = g.shape[4]
        self.lanes = self.full // 2
        self.lines, self.turns = [None, None], [None, None]

    def start(self):
        self.core = []
        for order in range(2):
            copy = self.copies.to(
                self.g.at[:, :, 1 - self.here.core, self.cuts[order]],
                self.s.at[:, :, self.cuts[order]],
                self.here.partner,
            )
            copy.start()
            self.core.append(copy)

    def line(self, order):
        here, at, zls = self.here, self.cuts[order], self.here.zls
        self.core[order].wait_recv()

        def add(zz, xx):
            self.s[zz, xx, at] = (
                self.s[zz, xx, at].astype(F32) + self.g[zz, xx, here.core, at].astype(F32)
            ).astype(BF)

        over(self.s.shape[:2], add)
        nx = self.s.shape[1]
        if order == 0:
            ring, count, width = here.x_ring, self.s.shape[0], self.full

            def index(lead, target, start, width):
                return (lead, target, at, lanes_at(start, width))

        elif self.kind == "a":
            ring, count, width = here.z_ring, nx, self.full

            def index(lead, target, start, width):
                return (target, lead, at, lanes_at(start, width))

        else:
            ring, count, width = here.z_ring, nx, self.lanes

            def index(lead, target, start, width):
                return (
                    lax.rem(target, zls),
                    lead,
                    at,
                    lanes_at((target // zls) * self.lanes + start, width),
                )

        summand = Summand(
            self.s,
            index,
            count,
            width,
            (self.near[order].at[0], self.near[order].at[1]),
            (self.far[order].at[0], self.far[order].at[1]),
        )
        self.lines[order] = RingSum(self.copies, ring, [summand])
        self.lines[order].start()

    def line_middle(self, order):
        self.lines[order].middle()

    def turn(self, order):
        here, zls, mid = self.here, self.here.zls, self.mid[order]
        line = self.lines[order]
        line.end()

        def put(lead):
            mid[lead] = line.total(0, lead).astype(BF)

        over(mid.shape[:1], put)
        ring = here.z_ring if order == 0 else here.x_ring
        if self.kind == "b" and order == 0:

            def index(lead, target, start, width):
                return (
                    lax.rem(target, zls),
                    slice(None),
                    lanes_at((target // zls) * self.lanes + start, width),
                )

        else:

            def index(lead, target, start, width):
                return (target, slice(None), lanes_at(start, width))

        summand = Summand(
            mid,
            index,
            None,
            self.full if self.kind == "a" else self.lanes,
            (self.near_two[order].at[0], self.near_two[order].at[1]),
            (self.far_two[order].at[0], self.far_two[order].at[1]),
        )
        self.turns[order] = RingSum(self.copies, ring, [summand])
        self.turns[order].start()

    def turn_middle(self, order):
        self.turns[order].middle()

    def end(self, order):
        self.turns[order].end()
        value = self.turns[order].total(0).astype(BF)
        if self.kind == "a":
            self.fin[order] = value
        else:
            self.fin[self.cuts[order]] = value

    def finish(self):
        for copy in self.core:
            copy.wait_send()
        for order in range(2):
            self.lines[order].finish()
            self.turns[order].finish()


def grad_buffers(grid, cut, g_shape, kind):
    nz, nx, _ = grid
    rows, full = g_shape[3:]
    zls = g_shape[0]
    first = rows // 2 if kind == "a" else cut
    lanes = full if kind == "a" else full // 2
    cuts = (first, rows - first)

    def low(*dims):
        return pltpu.VMEM(dims, BF)

    counts = (zls, nx)
    widths = (full, lanes)
    fin = low(2, first, full) if kind == "a" else low(rows, lanes)
    return [
        low(zls, nx, rows, full),
        *[low(2, counts[o], cuts[o], widths[o] // 2) for o in range(2)],
        *[low(2, counts[o], cuts[o], widths[o]) for o in range(2)],
        *[low(counts[o], cuts[o], widths[o]) for o in range(2)],
        *[low(2, cuts[o], lanes // 2) for o in range(2)],
        *[low(2, cuts[o], lanes) for o in range(2)],
        fin,
    ]


def grad_sum(here, cut, copies, kind, g, refs):
    s, near0, near1, far0, far1, mid0, mid1, low0, low1, top0, top1, fin = refs
    return GradSum(
        here,
        cut,
        copies,
        kind,
        g,
        s,
        ((near0, near1), (far0, far1), (mid0, mid1), (low0, low1), (top0, top1), fin),
    )


def final_kernel(grid, cut, sizes, *refs):
    (
        hid_all,
        vec,
        cosine,
        left,
        right,
        mask,
        bias,
        full_a,
        full_b,
        joined,
        probs,
        heads,
        pre,
        units,
        grad,
        grad_one,
        ga_one,
        gb_one,
        sums_one,
    ) = refs[:19]
    grad_out, out_a, out_b, out_v = refs[19:23]
    (
        ga,
        gb,
        sums,
        hat_ref,
        attn_in,
        mlp_in,
        back,
        grad_heads,
        grad_pre,
        raw,
        grad_joined,
        near,
        far,
        v_core,
        v_line,
        v_last,
        v_group,
    ) = refs[23:40]
    buffers = refs[40:88]
    sends, recvs, local = refs[88:]
    here = Slice(grid)
    nz, nx, _ = grid
    copies = Copies(sends, recvs)
    rows = grad_one.shape[0]
    d, r, half = here.d, here.row, here.half
    dh, dl = d // half, lax.rem(d, half)
    swap_needed = dh != r
    swap_to = {"dp": r * half + dl, "row": dh}
    a_target = [{"dp": 2 * dl + s, "row": dh} for s in range(2)]
    to_self = [(dh == r) & (2 * dl + s == d) for s in range(2)]
    a_source = r * half + d // 2
    from_self = [(r == k) & (a_source == d) for k in range(2)]

    count = here.greet_rings([here.z_ring, here.x_ring, here.y_ring], whole=True)
    greet(here.partner)
    for k in range(2):

        @pl.when(jnp.logical_not(from_self[k]))
        def _():
            greet({"dp": a_source, "row": k})

    @pl.when(swap_needed)
    def _():
        greet(swap_to)

    greeted(
        count + 3 + swap_needed.astype(jnp.int32) - sum(s.astype(jnp.int32) for s in to_self)
    )
    copies.count = 24

    sum_a_one = grad_sum(here, cut, copies, "a", ga_one, buffers[0:12])
    sum_b_one = grad_sum(here, cut, copies, "b", gb_one, buffers[12:24])
    sum_a = grad_sum(here, cut, copies, "a", ga, buffers[24:36])
    sum_b = grad_sum(here, cut, copies, "b", gb, buffers[36:48])

    def owner_copy(layer, fin, order):
        return pltpu.make_async_remote_copy(
            src_ref=fin.at[order],
            dst_ref=out_a.at[layer, r],
            send_sem=sends.at[layer * 8 + order],
            recv_sem=recvs.at[layer * 8 + r],
            device_id=a_target[order],
            device_id_type=MESH,
        )

    def owner_arrival(layer, fin, k):
        return pltpu.make_async_remote_copy(
            src_ref=fin.at[0],
            dst_ref=out_a.at[layer, k],
            send_sem=sends.at[layer * 8],
            recv_sem=recvs.at[layer * 8 + k],
            device_id={"dp": a_source, "row": k},
            device_id_type=MESH,
        )

    def owner_local(layer, fin, order):
        return pltpu.make_async_copy(fin.at[order], out_a.at[layer, r], local.at[layer])

    def swap_copy(layer, fin):
        return remote(fin, out_b.at[layer], sends, recvs, layer * 8 + 2, swap_to)

    def swap_local(layer, fin):
        return pltpu.make_async_copy(fin, out_b.at[layer], local.at[2 + layer])

    def hand_a(layer, fin, order):
        @pl.when(jnp.logical_not(to_self[order]))
        def _():
            owner_copy(layer, fin, order).start()

        @pl.when(to_self[order])
        def _():
            owner_local(layer, fin, order).start()

    def hand_b(layer, fin):
        @pl.when(swap_needed)
        def _():
            swap_copy(layer, fin).start()

        @pl.when(jnp.logical_not(swap_needed))
        def _():
            swap_local(layer, fin).start()

    def handed(layer, fin_a, fin_b):
        for k in range(2):

            @pl.when(jnp.logical_not(to_self[k]))
            def _():
                owner_copy(layer, fin_a, k).wait_send()

            @pl.when(to_self[k])
            def _():
                owner_local(layer, fin_a, k).wait()

            @pl.when(jnp.logical_not(from_self[k]))
            def _():
                owner_arrival(layer, fin_a, k).wait_recv()

        @pl.when(swap_needed)
        def _():
            swap_copy(layer, fin_b).wait()

        @pl.when(jnp.logical_not(swap_needed))
        def _():
            swap_local(layer, fin_b).wait()

    def phase(name, which):
        for order in range(2):
            for one in which:
                getattr(one, name)(order)

    ones = [sum_a_one, sum_b_one]
    for one in ones:
        one.start()
    layer = Layer(0, vec, (cosine, left, right), mask, bias, full_a, full_b, sizes)
    grads_b(heads, grad, gb, 0, sizes[2])
    grads_b(units, grad, gb, sizes[2], gb.shape[3])
    phase("line", ones)
    sum_b.start()
    hat, inverse = norm_stats(hid_all[...].astype(F32))
    hat_ref[...] = hat
    layer.inputs(hat, attn_in, mlp_in)
    layer.branch_back(grad, pre, grad_heads, grad_pre)
    phase("line_middle", ones)
    layer.attend_back(joined, probs, grad_heads, raw, grad_joined)
    phase("turn", ones)
    phase("line", [sum_b])
    grads_a(attn_in, grad_joined, ga, 0)
    grads_a(mlp_in, grad_pre, ga, grad_joined.shape[1])
    phase("turn_middle", ones)
    sum_a.start()
    phase("line_middle", [sum_b])
    value = layer.inputs_back(grad_joined, grad_pre, hat_ref[...], grad, sums)
    _, inverse = norm_stats(hid_all[...].astype(F32))
    back[...] = (inverse * value).astype(BF)
    mine = own_rows(here, rows)
    back[mine, :] = (back[mine, :].astype(F32) + grad_one[...]).astype(BF)
    summed = group_sum(
        here, copies, back, blocks_index(2 * rows, D // 2), D // 2, near, far
    )
    summed.start()
    v_lanes = D // 2
    v_mine = pl.ds(pl.multiple_of(here.core * v_lanes, v_lanes), v_lanes)
    v_other = pl.ds(pl.multiple_of((1 - here.core) * v_lanes, v_lanes), v_lanes)
    v_copies = [
        copies.to(sums.at[:, v_other], v_core.at[0], here.partner),
        copies.to(sums_one.at[:, v_other], v_core.at[1], here.partner),
    ]
    for copy in v_copies:
        copy.start()
    phase("line", [sum_a])
    for order in range(2):
        sum_a_one.end(order)
        sum_b_one.end(order)
        hand_a(1, sum_a_one.fin, order)
    hand_b(1, sum_b_one.fin)
    for copy in v_copies:
        copy.wait()
    v_line[here.x, 0:VEC_ROWS] = v_core[0] + sums[:, v_mine]
    v_line[here.x, VEC_ROWS:] = v_core[1] + sums_one[:, v_mine]
    v_x = [copies.to(v_line.at[here.x], v_line.at[here.x], here.x_ring.device(k)) for k in range(1, nx)]
    for copy in v_x:
        copy.start()
    phase("turn", [sum_b])
    summed.middle()
    phase("line_middle", [sum_a])
    for copy in v_x:
        copy.wait()
    total = v_line[0]
    for k in range(1, nx):
        total = total + v_line[k]
    v_last[here.z] = total
    v_z = [copies.to(v_last.at[here.z], v_last.at[here.z], here.z_ring.device(k)) for k in range(1, nz)]
    for copy in v_z:
        copy.start()
    phase("turn_middle", [sum_b])
    summed.end()
    grad_out[...] = summed.total(0)
    phase("turn", [sum_a])
    for copy in v_z:
        copy.wait()
    total = v_last[0]
    for k in range(1, nz):
        total = total + v_last[k]
    v_group[here.place] = total
    v_y = [
        copies.to(v_group.at[here.place], v_group.at[here.place], here.y_ring.device(k))
        for k in range(1, 4)
    ]
    for copy in v_y:
        copy.start()
    for order in range(2):
        sum_b.end(order)
    hand_b(0, sum_b.fin)
    phase("turn_middle", [sum_a])
    for copy in v_y:
        copy.wait()
    total = v_group[0]
    for k in range(1, 4):
        total = total + v_group[k]
    out_v[0, :, v_mine] = total
    out_v[1, :, v_mine] = v_group[here.place]
    v_swap = copies.to(out_v.at[:, :, v_mine], out_v.at[:, :, v_mine], here.partner)
    v_swap.start()
    for order in range(2):
        sum_a.end(order)
        hand_a(0, sum_a.fin, order)
    v_swap.wait()
    handed(1, sum_a_one.fin, sum_b_one.fin)
    handed(0, sum_a.fin, sum_b.fin)
    summed.finish()
    for one in (sum_a_one, sum_b_one, sum_a, sum_b):
        one.finish()


def final_layer(
    grid,
    cut,
    sizes,
    hid_all,
    vec,
    tables,
    mask,
    bias,
    full_a,
    full_b,
    cache,
    grad_all,
    grad_one,
    ga_one,
    gb_one,
    sums_one,
):
    nz, nx, _ = grid
    tokens = hid_all.shape[0]
    rows = tokens // 4
    qkv_width, up_width, _ = sizes
    heads_here = qkv_width // (3 * HEAD)
    shape = jax.ShapeDtypeStruct
    a_rows, a_lanes = full_a.shape[3:]
    b_rows, b_lanes = full_b.shape[3:]

    def low(*dims):
        return pltpu.VMEM(dims, BF)

    def high(*dims):
        return pltpu.VMEM(dims, F32)

    buffers_a = grad_buffers(grid, cut, full_a.shape, "a")
    buffers_b = grad_buffers(grid, cut, full_b.shape, "b")
    return pl.pallas_call(
        partial(final_kernel, grid, cut, sizes),
        out_shape=(
            shape((2 * rows, D // 2), F32),
            shape((LAYERS, 2, a_rows // 2, a_lanes), BF),
            shape((LAYERS, b_rows, b_lanes // 2), BF),
            shape((2, LAYERS * VEC_ROWS, D), F32),
        ),
        in_specs=[VMEM_SPEC] * 19,
        out_specs=(VMEM_SPEC,) * 4,
        scratch_shapes=[
            low(*full_a.shape),
            low(*full_b.shape),
            high(VEC_ROWS, D),
            high(tokens, D),
            low(tokens, D),
            low(tokens, D),
            low(tokens, D),
            low(tokens, heads_here * HEAD),
            low(tokens, up_width),
            high(tokens, qkv_width),
            low(tokens, qkv_width),
            *ring_scratch(2 * rows, D // 2),
            high(2, VEC_ROWS, D // 2),
            high(nx, LAYERS * VEC_ROWS, D // 2),
            high(nz, LAYERS * VEC_ROWS, D // 2),
            high(4, LAYERS * VEC_ROWS, D // 2),
            *buffers_a,
            *buffers_b,
            *buffers_a,
            *buffers_b,
            pltpu.SemaphoreType.DMA((128,)),
            pltpu.SemaphoreType.DMA((128,)),
            pltpu.SemaphoreType.DMA((4,)),
        ],
        compiler_params=params(3, 60),
        name="final_layer",
    )(
        hid_all,
        vec,
        *tables,
        mask,
        bias,
        full_a,
        full_b,
        *cache,
        grad_all,
        grad_one,
        ga_one,
        gb_one,
        sums_one,
    )


def rope_lanes(cosine, sine):
    half = ROT // 2
    length = cosine.shape[0]
    ones = jnp.ones((length, HEAD), F32)
    zeros = jnp.zeros((length, HEAD), F32)

    def pair(rotated, rest):
        block = jnp.concatenate([rotated, rest[:, ROT:]], 1)
        return jnp.concatenate([block, block, rest] * 2, 1)

    return (
        pair(cosine, ones),
        pair(jnp.concatenate([-sine[:, :half], zeros[:, :half]], 1), zeros),
        pair(jnp.concatenate([zeros[:, :half], sine[:, half:]], 1), zeros),
    )


def on_device(
    hidden_in,
    cotangent,
    seq_ids,
    qkv_weight,
    qkv_first,
    qkv_second,
    out_weight,
    out_first,
    out_second,
    up_weight,
    up_first,
    up_second,
    down_weight,
    down_first,
    down_second,
    qkv_bias,
    qkv_bias_first,
    qkv_bias_second,
    up_bias,
    up_bias_first,
    up_bias_second,
    row_vectors,
    row_first,
    row_second,
):
    n_dp = lax.axis_size("dp")
    grid = GRIDS[n_dp]
    d, r = lax.axis_index("dp"), lax.axis_index("row")
    group_len = seq_ids.shape[0]
    qkv_width, up_width = qkv_weight.shape[2] // 2, up_weight.shape[2] // 2
    out_rows, down_rows = out_weight.shape[1], down_weight.shape[1]
    bias_widths = qkv_bias.shape[1], up_bias.shape[1]
    cut = out_rows + down_rows // 2
    sizes = (qkv_width, up_width, out_rows)

    wa = jnp.stack(
        [
            jnp.concatenate(
                [
                    qkv_weight[:, :, k * qkv_width : (k + 1) * qkv_width],
                    up_weight[:, :, k * up_width : (k + 1) * up_width],
                ],
                2,
            )
            for k in range(2)
        ],
        1,
    ).astype(BF)
    wb = jnp.concatenate([out_weight, down_weight], 1).astype(BF)
    wc = jnp.pad(
        jnp.concatenate([qkv_bias, up_bias], 1), ((0, 14), (0, -sum(bias_widths) % 128))
    ).astype(BF)
    vec = jnp.pad(row_vectors, ((0, 0), (0, 2), (0, 0))).reshape(LAYERS * VEC_ROWS, -1)
    hid_all, cot_all, vec, wa_one, wb_one, full_a, full_b, full_c = start_exchange(
        grid, cut, hidden_in, cotangent, vec, wa, wb, wc
    )
    full_c = full_c.reshape(n_dp, *wc.shape)
    biases = []
    for k in range(LAYERS):
        rows = [
            full_c[:, k, : bias_widths[0]].reshape(1, -1),
            full_c[:, k, bias_widths[0] : sum(bias_widths)].reshape(1, -1),
        ]
        biases.append(
            jnp.concatenate([jnp.pad(v, ((0, 0), (0, D - v.shape[1]))) for v in rows], 0).astype(F32)
        )

    positions, allowed, live_rows = sequence_layout(seq_ids)
    tables = rope_lanes(*rope_tables(positions))
    mask = jnp.where(allowed, 0.0, MASK_VALUE).astype(F32)
    live = jnp.broadcast_to(live_rows[:, None], (group_len, 128))

    state_one, inv_one, hat_one, *cache, next_a, next_b = first_layer(
        grid, cut, sizes, hid_all, vec, tables, mask, biases[0], full_a, full_b, wa_one, wb_one
    )
    hidden_out, grad_one, grad_all, ga_one, gb_one, sums_one = last_layer(
        grid,
        sizes,
        hat_one,
        vec,
        tables,
        mask,
        biases[1],
        next_a,
        next_b,
        state_one,
        inv_one,
        cot_all,
        live,
    )
    grad_state, own_a, own_b, all_v = final_layer(
        grid,
        cut,
        sizes,
        hid_all,
        vec,
        tables,
        mask,
        biases[0],
        full_a,
        full_b,
        cache,
        grad_all,
        grad_one,
        ga_one,
        gb_one,
        sums_one,
    )
    grad_qkv = jnp.concatenate([own_a[:, 0, :, :qkv_width], own_a[:, 1, :, :qkv_width]], 2)
    grad_up = jnp.concatenate([own_a[:, 0, :, qkv_width:], own_a[:, 1, :, qkv_width:]], 2)
    all_v = all_v.reshape(2, LAYERS, VEC_ROWS, D)
    lanes = hidden_in.shape[1]
    vector_grad = lax.dynamic_slice_in_dim(all_v[0], r * lanes, lanes, axis=2)
    vector_grad = jnp.concatenate([vector_grad[:, :5], vector_grad[:, 4:5]], 1)
    grad_qkv_bias = lax.dynamic_slice_in_dim(
        all_v[1, :, 5], d * bias_widths[0], bias_widths[0], axis=1
    )
    grad_up_bias = lax.dynamic_slice_in_dim(
        all_v[1, :, 6], d * bias_widths[1], bias_widths[1], axis=1
    )
    stacked = (
        grad_qkv.astype(F32),
        own_b[:, :out_rows].astype(F32),
        grad_up.astype(F32),
        own_b[:, out_rows:].astype(F32),
        grad_qkv_bias,
        grad_up_bias,
    )
    qkv_new = adamw(qkv_weight, qkv_first, qkv_second, stacked[0], RATE_MATRIX, DECAY_MATRIX)
    out_new = adamw(out_weight, out_first, out_second, stacked[1], RATE_MATRIX, DECAY_MATRIX)
    up_new = adamw(up_weight, up_first, up_second, stacked[2], RATE_MATRIX, DECAY_MATRIX)
    down_new = adamw(down_weight, down_first, down_second, stacked[3], RATE_MATRIX, DECAY_MATRIX)
    qkv_bias_new = adamw(qkv_bias, qkv_bias_first, qkv_bias_second, stacked[4], RATE_MATRIX, 0.0)
    up_bias_new = adamw(up_bias, up_bias_first, up_bias_second, stacked[5], RATE_MATRIX, 0.0)
    row_new = adamw(row_vectors, row_first, row_second, vector_grad, RATE_VECTOR, 0.0)
    return (
        hidden_out,
        grad_state,
        qkv_new[0],
        qkv_new[1],
        qkv_new[2],
        out_new[0],
        out_new[1],
        out_new[2],
        up_new[0],
        up_new[1],
        up_new[2],
        down_new[0],
        down_new[1],
        down_new[2],
        qkv_bias_new[0],
        qkv_bias_new[1],
        qkv_bias_new[2],
        up_bias_new[0],
        up_bias_new[1],
        up_bias_new[2],
        row_new[0],
        row_new[1],
        row_new[2],
    )


def solution(mesh):
    placed = (
        P(("dp", "col"), "row"),
        P(("dp", "col"), "row"),
        P("dp"),
        P(None, ("row", "dp"), "col"),
        P(None, ("row", "dp"), "col"),
        P(None, ("row", "dp"), "col"),
        P(None, ("col", "dp"), "row"),
        P(None, ("col", "dp"), "row"),
        P(None, ("col", "dp"), "row"),
        P(None, ("row", "dp"), "col"),
        P(None, ("row", "dp"), "col"),
        P(None, ("row", "dp"), "col"),
        P(None, ("col", "dp"), "row"),
        P(None, ("col", "dp"), "row"),
        P(None, ("col", "dp"), "row"),
        P(None, ("col", "row", "dp")),
        P(None, ("col", "row", "dp")),
        P(None, ("col", "row", "dp")),
        P(None, ("col", "row", "dp")),
        P(None, ("col", "row", "dp")),
        P(None, ("col", "row", "dp")),
        P(None, None, "row"),
        P(None, None, "row"),
        P(None, None, "row"),
    )
    return jax.shard_map(
        on_device,
        mesh=mesh,
        in_specs=placed,
        out_specs=(
            P(("dp", "col"), "row"),
            P(("dp", "col"), "row"),
            P(None, ("row", "dp"), "col"),
            P(None, ("row", "dp"), "col"),
            P(None, ("row", "dp"), "col"),
            P(None, ("col", "dp"), "row"),
            P(None, ("col", "dp"), "row"),
            P(None, ("col", "dp"), "row"),
            P(None, ("row", "dp"), "col"),
            P(None, ("row", "dp"), "col"),
            P(None, ("row", "dp"), "col"),
            P(None, ("col", "dp"), "row"),
            P(None, ("col", "dp"), "row"),
            P(None, ("col", "dp"), "row"),
            P(None, ("col", "row", "dp")),
            P(None, ("col", "row", "dp")),
            P(None, ("col", "row", "dp")),
            P(None, ("col", "row", "dp")),
            P(None, ("col", "row", "dp")),
            P(None, ("col", "row", "dp")),
            P(None, None, "row"),
            P(None, None, "row"),
            P(None, None, "row"),
        ),
        check_vma=False,
    )
```

time: 809 us -> 245 us (0.30)
  the two profiles are of different devices: /device:TPU:8 before, /device:TPU:1 now
where the time goes in v1:
time: 245 us; the launch traced here: 244 us
  Pallas kernels  210 us (86%)
  local copies, waits for them, and re-layouts  20.4 us (8%)
  other arithmetic  12 us (5%)
    pallas_call x1, Pallas kernels, final_layer(): pl.pallas_call(partial(final_kernel, grid, cut, sizes), out_shape=(shape(...  79.5 us
    pallas_call x1, Pallas kernels, first_layer(): pl.pallas_call(partial(first_kernel, grid, cut, sizes), out_shape=(shape(...  50.2 us
    pallas_call x1, Pallas kernels, start_exchange(): pl.pallas_call(partial(start_kernel, grid, cut), out_shape=(token_rows, t...  43 us
    pallas_call x1, Pallas kernels, last_layer(): pl.pallas_call(partial(last_kernel, grid, sizes), out_shape=(shape((2 * r...  37.2 us
    unnamed x72, local copies, waits for them, and re-layouts  8.45 us
    sub x7, other arithmetic, adamw(): master - step_rate * (one_hat / (jnp.sqrt(two_hat) + EPS_ADAM) + step_dec...  5.49 us

profile of v1, /device:TPU:1, one launch (start us, length us, event | category | flops | bytes accessed | tf_op | source)
XLA Modules:
  0.0 243.7 jit_solution(1413659737796151133)
XLA Ops:
  0.7 1.0 convert.31
  1.8 0.9 convert.30
  2.8 1.0 convert.33
  3.8 0.8 convert.32
  4.8 43.0 %start_exchange.1 = (bf16[320,1024]{1,0:T(8,128)(2,1)S(1)}, bf16[320,1024]{1,0:T(8,128)(2,1)S(1)}, f32[16,1024]{1,0:T(8,128)S(1)}, bf16[32,1792]{1,0:T(8,128)(2,...) custom-call(bf16[160,512]{1,0:T(8,128)(2,1)S(1)} %copy-done.5, ...), custom_call_target="tpu_custom_call" | custom-call | tf_op jit(solution)/shard_map/start_exchange/pallas_call | solution.py:563
  47.8 1.8 copy-done
  49.6 1.5 copy-done.1
  51.2 0.8 copy-done.2
  52.0 0.8 copy-done.3
  53.5 0.6 copy-done.7
  54.1 0.6 copy-done.8
  57.0 1.5 concatenate.55.left.refs_3_
  58.5 1.5 concatenate.56.right.refs_4_
  60.2 1.3 concatenate.54.cosine.refs_2_
  61.4 0.9 fusion.1.mask.refs_5_
  62.4 50.2 %first_layer.1 = (f32[80,1024]{1,0:T(8,128)}, f32[80,128]{1,0:T(8,128)}, bf16[320,1024]{1,0:T(8,128)(2,1)}, bf16[320,768]{1,0:T(8,128)(2,1)}, bf16[4,320,320]{2,...) custom-call(bf16[320,1024]{1,0:T(8,128)(2,1)} %copy-done.2, ...), custom_call_target="tpu_custom_call" | custom-call | tf_op jit(solution)/shard_map/first_layer/pallas_call | solution.py:888
  113.4 0.8 broadcast_in_dim.18.live
  114.2 37.2 %last_layer.1 = (bf16[160,512]{1,0:T(8,128)(2,1)}, f32[80,1024]{1,0:T(8,128)}, bf16[320,1024]{1,0:T(8,128)(2,1)}, bf16[4,4,2,32,1792]{4,3,2,1,0:T(8,128)(2,1)}, ...) custom-call(bf16[320,1024]{1,0:T(8,128)(2,1)} %get-tuple-element.58.hat_all, f32[16,1024]{1,0:T(8,128)} %copy-done.4, ...), custom_call_target="tpu_custom_call" | custom-call | tf_op jit(solution)/shard_map/last_layer/pallas_call | solution.py:1019
  151.5 79.5 %final_layer.1 = (f32[160,512]{1,0:T(8,128)}, bf16[2,2,16,1792]{3,2,1,0:T(8,128)(2,1)}, bf16[2,80,512]{2,1,0:T(8,128)(2,1)}, f32[2,16,1024]{2,1,0:T(8,128)}) custom-call(bf16[320,1024]{1,0:T(8,128)(2,1)} %copy-done.2, f32[16,1024]{1,0:T(8,128)} %copy-done.4, f32[320,384]{1,0:T(8,128)} %concatenate.54.cosine.refs_2_, f32[320,384]{1,0:T(8,128)} %concatenate.55.left.refs_3_, ...), custom_call_target="tpu_custom_call" | custom-call | tf_op jit(solution)/shard_map/final_layer/pallas_call | solution.py:1511
  231.1 1.0 slice_bitcast_fusion.1
  232.2 0.7 multiply_subtract_fusion.4
  232.9 0.9 slice_bitcast_fusion
  233.8 0.8 slice_bitcast_fusion.2
  234.7 1.0 multiply_subtract_fusion.1
  235.7 0.8 slice_bitcast_fusion.3
  236.5 0.8 slice_bitcast_fusion.4
  237.3 0.9 multiply_subtract_fusion.2
  238.3 1.0 multiply_subtract_fusion
  239.3 0.7 multiply_subtract_fusion.3
  240.0 0.9 fusion.38
  242.3 0.7 copy.132
  242.9 0.7 copy.133
  (104 shorter events, 5.5 us)
Async XLA Ops:
  0.7 4.0 %copy-start.22 = (f32[2,6,512]{2,0,1:T(2,128)S(1)}, f32[2,6,512]{2,0,1:T(2,128)}, u32[]{:S(2)}) copy-start(f32[2,6,512]{2,0,1:T(2,128)} %param.45) | copy-start | bytes 73732
  0.7 4.0 %copy-start.28 = (f32[2,24]{1,0:T(2,128)S(1)}, f32[2,24]{1,0:T(2,128)}, u32[]{:S(2)}) copy-start(f32[2,24]{1,0:T(2,128)} %param.39) | copy-start | bytes 580
  0.7 4.0 %copy-start.31 = (f32[2,32]{1,0:T(2,128)S(1)}, f32[2,32]{1,0:T(2,128)}, u32[]{:S(2)}) copy-start(f32[2,32]{1,0:T(2,128)} %param.42) | copy-start | bytes 772
  0.7 4.1 %copy-start.5 = (bf16[160,512]{1,0:T(8,128)(2,1)S(1)}, bf16[160,512]{1,0:T(8,128)(2,1)}, u32[]{:S(2)}) copy-start(bf16[160,512]{1,0:T(8,128)(2,1)} %hid.1) | copy-start | bytes 491524
  0.7 4.1 %copy-start.6 = (bf16[160,512]{1,0:T(8,128)(2,1)S(1)}, bf16[160,512]{1,0:T(8,128)(2,1)}, u32[]{:S(2)}) copy-start(bf16[160,512]{1,0:T(8,128)(2,1)} %cot.1) | copy-start | bytes 491524
  0.7 55.1 %copy-start.25 = (s32[320]{0:T(512)S(1)}, s32[320]{0:T(512)}, u32[]{:S(2)}) copy-start(s32[320]{0:T(512)} %param.26) | copy-start | bytes 3844
  47.8 1.8 copy-start
  49.6 1.5 copy-start.1
  51.2 0.8 copy-start.2
  52.0 0.8 copy-start.3
  53.5 0.6 copy-start.7
  151.4 80.8 %copy-start.26 = (f32[2,6,512]{2,0,1:T(2,128)S(1)}, f32[2,6,512]{2,0,1:T(2,128)}, u32[]{:S(2)}) copy-start(f32[2,6,512]{2,0,1:T(2,128)} %param.46) | copy-start | bytes 73732
  151.4 80.7 %copy-start.27 = (f32[2,6,512]{2,0,1:T(2,128)S(1)}, f32[2,6,512]{2,0,1:T(2,128)}, u32[]{:S(2)}) copy-start(f32[2,6,512]{2,0,1:T(2,128)} %param.47) | copy-start | bytes 73732
  151.5 83.2 %copy-start.9 = (f32[2,16,2048]{2,1,0:T(8,128)S(1)}, f32[2,16,2048]{2,1,0:T(8,128)}, u32[]{:S(2)}) copy-start(f32[2,16,2048]{2,1,0:T(8,128)} %param.33) | copy-start | bytes 786436
  151.5 83.2 %copy-start.14 = (f32[2,16,2048]{2,1,0:T(8,128)S(1)}, f32[2,16,2048]{2,1,0:T(8,128)}, u32[]{:S(2)}) copy-start(f32[2,16,2048]{2,1,0:T(8,128)} %param.34) | copy-start | bytes 786436
  151.5 83.2 %copy-start.15 = (f32[2,16,2048]{2,1,0:T(8,128)S(1)}, f32[2,16,2048]{2,1,0:T(8,128)}, u32[]{:S(2)}) copy-start(f32[2,16,2048]{2,1,0:T(8,128)} %param.35) | copy-start | bytes 786436
  231.0 6.3 %copy-start.11 = (f32[2,16,1536]{2,1,0:T(8,128)S(1)}, f32[2,16,1536]{2,1,0:T(8,128)}, u32[]{:S(2)}) copy-start(f32[2,16,1536]{2,1,0:T(8,128)} %param.27) | copy-start | bytes 589828
  231.0 6.3 %copy-start.18 = (f32[2,16,1536]{2,1,0:T(8,128)S(1)}, f32[2,16,1536]{2,1,0:T(8,128)}, u32[]{:S(2)}) copy-start(f32[2,16,1536]{2,1,0:T(8,128)} %param.28) | copy-start | bytes 589828
  231.0 6.3 %copy-start.19 = (f32[2,16,1536]{2,1,0:T(8,128)S(1)}, f32[2,16,1536]{2,1,0:T(8,128)}, u32[]{:S(2)}) copy-start(f32[2,16,1536]{2,1,0:T(8,128)} %param.29) | copy-start | bytes 589828
  231.1 7.2 %copy-start.10 = (f32[2,64,512]{2,1,0:T(8,128)S(1)}, f32[2,64,512]{2,1,0:T(8,128)}, u32[]{:S(2)}) copy-start(f32[2,64,512]{2,1,0:T(8,128)} %param.36) | copy-start | bytes 786436
  231.1 7.2 %copy-start.16 = (f32[2,64,512]{2,1,0:T(8,128)S(1)}, f32[2,64,512]{2,1,0:T(8,128)}, u32[]{:S(2)}) copy-start(f32[2,64,512]{2,1,0:T(8,128)} %param.37) | copy-start | bytes 786436
  231.1 7.2 %copy-start.17 = (f32[2,64,512]{2,1,0:T(8,128)S(1)}, f32[2,64,512]{2,1,0:T(8,128)}, u32[]{:S(2)}) copy-start(f32[2,64,512]{2,1,0:T(8,128)} %param.38) | copy-start | bytes 786436
  231.1 7.2 %copy-start.21 = (bf16[2,80,512]{2,1,0:T(8,128)(2,1)S(1)}, bf16[2,80,512]{2,1,0:T(8,128)(2,1)}, u32[]{:S(2)}) copy-start(bf16[2,80,512]{2,1,0:T(8,128)(2,1)} %get-tuple-element.77) | copy-start | bytes 491524
  232.9 6.4 %copy-start.13 = (f32[2,16,512]{2,1,0:T(8,128)S(1)}, f32[2,16,512]{2,1,0:T(8,128)}, u32[]{:S(2)}) copy-start(f32[2,16,512]{2,1,0:T(8,128)} %param.30) | copy-start | bytes 196612
  232.9 6.4 %copy-start.23 = (f32[2,16,512]{2,1,0:T(8,128)S(1)}, f32[2,16,512]{2,1,0:T(8,128)}, u32[]{:S(2)}) copy-start(f32[2,16,512]{2,1,0:T(8,128)} %param.31) | copy-start | bytes 196612
  232.9 6.4 %copy-start.24 = (f32[2,16,512]{2,1,0:T(8,128)S(1)}, f32[2,16,512]{2,1,0:T(8,128)}, u32[]{:S(2)}) copy-start(f32[2,16,512]{2,1,0:T(8,128)} %param.32) | copy-start | bytes 196612
  234.7 6.3 %copy-start.29 = (f32[2,24]{1,0:T(2,128)S(1)}, f32[2,24]{1,0:T(2,128)}, u32[]{:S(2)}) copy-start(f32[2,24]{1,0:T(2,128)} %param.40) | copy-start | bytes 580
  234.7 6.3 %copy-start.30 = (f32[2,24]{1,0:T(2,128)S(1)}, f32[2,24]{1,0:T(2,128)}, u32[]{:S(2)}) copy-start(f32[2,24]{1,0:T(2,128)} %param.41) | copy-start | bytes 580
  234.7 7.0 %copy-start.32 = (f32[2,32]{1,0:T(2,128)S(1)}, f32[2,32]{1,0:T(2,128)}, u32[]{:S(2)}) copy-start(f32[2,32]{1,0:T(2,128)} %param.43) | copy-start | bytes 772
  234.7 7.0 %copy-start.33 = (f32[2,32]{1,0:T(2,128)S(1)}, f32[2,32]{1,0:T(2,128)}, u32[]{:S(2)}) copy-start(f32[2,32]{1,0:T(2,128)} %param.44) | copy-start | bytes 772
  234.7 7.6 %copy-start.20 = (bf16[160,512]{1,0:T(8,128)(2,1)S(1)}, bf16[160,512]{1,0:T(8,128)(2,1)}, u32[]{:S(2)}) copy-start(bf16[160,512]{1,0:T(8,128)(2,1)} %get-tuple-element.139) | copy-start | bytes 491524
  234.7 8.2 %copy-start.12 = (f32[160,512]{1,0:T(8,128)S(1)}, f32[160,512]{1,0:T(8,128)}, u32[]{:S(2)}) copy-start(f32[160,512]{1,0:T(8,128)} %get-tuple-element.140) | copy-start | bytes 983044
  (2 other events, 1.3 us)

commit v2 on v1

v2 whole, which is shorter than its diff:
```python
import math
from functools import partial
from types import SimpleNamespace

import jax
import jax.numpy as jnp
from jax import lax
from jax.experimental import pallas as pl
from jax.experimental.pallas import tpu as pltpu
from jax.sharding import PartitionSpec as P

D = 1024
HEAD = 64
ROT = 16
LAYERS = 2
SEQS = 3
STEP = 10


EPS_NORM = 1e-05
EPS_ADAM = 1e-08
BETA_ONE = 0.9
BETA_TWO = 0.95
RATE_MATRIX = 0.06
RATE_VECTOR = 0.6
DECAY_MATRIX = 0.01
ROPE_BASE = 10000.0
MASK_VALUE = -1e30
CONTRACT_ROWS = (((0,), (0,)), ((), ()))
CONTRACT_COLS = (((1,), (1,)), ((), ()))

BF = jnp.bfloat16
F32 = jnp.float32
MESH = pl.DeviceIdType.MESH
GRIDS = {32: (4, 4, 2), 8: (2, 2, 2)}
VEC_ROWS = 8
VMEM_SPEC = pl.BlockSpec(memory_space=pltpu.VMEM)


def params(collective_id, mib):
    return pltpu.CompilerParams(
        collective_id=collective_id, has_side_effects=True, vmem_limit_bytes=mib << 20
    )


def remote(src, dst, sends, recvs, at, device):
    return pltpu.make_async_remote_copy(
        src_ref=src,
        dst_ref=dst,
        send_sem=sends.at[at],
        recv_sem=recvs.at[at],
        device_id=device,
        device_id_type=MESH,
    )


def greet(device):
    pl.semaphore_signal(
        pltpu.get_barrier_semaphore(), inc=1, device_id=device, device_id_type=MESH
    )


def greeted(count):
    pl.semaphore_wait(pltpu.get_barrier_semaphore(), count)


def group_place():
    return lax.axis_index("row") * 2 + lax.axis_index("col")


def group_peer(place, step):
    other = lax.rem(place + step, 4)
    return {"row": other // 2, "col": lax.rem(other, 2)}


def over(lengths, body):
    total = math.prod(lengths)

    def one(index, carry):
        place, rest = [], index
        for length in reversed(lengths):
            place.append(lax.rem(rest, length))
            rest = rest // length
        body(*reversed(place))
        return carry

    lax.fori_loop(0, total, one, 0)


def adamw(master, moment_one, moment_two, gradient, step_rate, step_decay):
    one_new = BETA_ONE * moment_one + (1.0 - BETA_ONE) * gradient
    two_new = BETA_TWO * moment_two + (1.0 - BETA_TWO) * gradient * gradient
    one_hat = one_new / (1.0 - BETA_ONE**STEP)
    two_hat = two_new / (1.0 - BETA_TWO**STEP)
    master_new = master - step_rate * (
        one_hat / (jnp.sqrt(two_hat) + EPS_ADAM) + step_decay * master
    )
    return (master_new, one_new, two_new)


class Copies:
    def __init__(self, sends, recvs):
        self.sends, self.recvs, self.count = sends, recvs, 0

    def to(self, src, dst, device):
        copy = remote(src, dst, self.sends, self.recvs, self.count, device)
        self.count += 1
        return copy


class Ring:
    def __init__(self, length, place, device_at):
        self.length, self.place, self.device_at = length, place, device_at
        self.ways = ((0, 1), (1, -1)) if length > 2 else ((0, 1),)

    def at(self, step):
        return lax.rem(self.place + step + self.length, self.length)

    def device(self, step):
        return self.device_at(self.at(step))


class RingGather:
    def __init__(self, copies, ring, views, sources=None, arrived=None):
        self.copies, self.ring, self.views = copies, ring, views
        self.sources, self.arrived = sources, arrived
        self.near, self.far = [[], []], [[], []]

    def start(self):
        for way, step in self.ring.ways:
            for k, view in enumerate(self.views):
                own = view(self.ring.place, None)
                src = self.sources[k] if self.sources else own
                copy = self.copies.to(src, own, self.ring.device(step))
                copy.start()
                self.near[way].append(copy)

    def middle(self):
        for way, step in self.ring.ways:
            for copy in self.near[way]:
                copy.wait_recv()
            came_from = self.ring.at(-step)
            if self.ring.length > 2:
                for view in self.views:
                    ref = view(came_from, way)
                    if ref is not None:
                        copy = self.copies.to(ref, ref, self.ring.device(step))
                        copy.start()
                        self.far[way].append(copy)
            if self.arrived:
                self.arrived(came_from)

    def end(self):
        for copy in self.far[0] + self.far[1]:
            copy.wait_recv()
        if self.arrived and self.ring.length > 2:
            self.arrived(self.ring.at(2))

    def finish(self):
        for copy in self.near[0] + self.near[1] + self.far[0] + self.far[1]:
            copy.wait_send()


class Summand:
    def __init__(self, ref, index, count, width, near, far):
        self.ref, self.index, self.count, self.width = ref, index, count, width
        self.near, self.far = near, far

    def view(self, target, start, width):
        return self.ref.at[self.index(slice(None), target, start, width)]

    def add(self, target, start, width, other):
        def one(lead):
            at = self.index(lead, target, start, width)
            more = other[...] if self.count is None else other[lead]
            self.ref[at] = (self.ref[at].astype(F32) + more.astype(F32)).astype(BF)

        if self.count is None:
            one(None)
        else:
            over((self.count,), one)

    def total(self, lead, target, ways):
        value = self.ref[self.index(lead, target, 0, self.width)].astype(F32)
        for way in range(ways):
            more = self.far[way][...] if self.count is None else self.far[way][lead]
            value = value + more.astype(F32)
        return value


class RingSum:
    def __init__(self, copies, ring, summands):
        self.copies, self.ring, self.summands = copies, ring, summands
        self.near, self.far = [[], []], [[], []]

    def start(self):
        if self.ring.length == 2:
            return
        for way, step in self.ring.ways:
            for s in self.summands:
                half = s.width // 2
                copy = self.copies.to(
                    s.view(self.ring.at(2), way * half, half), s.near[way], self.ring.device(step)
                )
                copy.start()
                self.near[way].append(copy)

    def middle(self):
        for way, step in self.ring.ways:
            target = self.ring.at(step)
            for k, s in enumerate(self.summands):
                if self.ring.length > 2:
                    self.near[way][k].wait_recv()
                    s.add(target, way * (s.width // 2), s.width // 2, s.near[way])
                copy = self.copies.to(
                    s.view(target, 0, s.width), s.far[way], self.ring.device(step)
                )
                copy.start()
                self.far[way].append(copy)

    def end(self):
        for copy in self.far[0] + self.far[1]:
            copy.wait_recv()

    def total(self, k, lead=None):
        return self.summands[k].total(lead, self.ring.place, len(self.ring.ways))

    def finish(self):
        for copy in self.near[0] + self.near[1] + self.far[0] + self.far[1]:
            copy.wait_send()


def lanes_at(start, width):
    if not isinstance(start, int):
        start = pl.multiple_of(start, 128)
    return pl.ds(start, width)


class Slice:
    def __init__(self, grid):
        self.grid = grid
        nz, nx, nc = grid
        d = lax.axis_index("dp")
        self.d, self.z, self.x, self.core = d, d // (nx * nc), lax.rem(d // nc, nx), lax.rem(d, nc)
        self.row, self.col = lax.axis_index("row"), lax.axis_index("col")
        self.half = nz * nx * nc // 2
        self.place = group_place()
        self.zls = nz // 2
        self.partner = self.dp(self.z, self.x, 1 - self.core)
        self.z_ring = Ring(nz, self.z, lambda z: self.dp(z, self.x, self.core))
        self.x_ring = Ring(nx, self.x, lambda x: self.dp(self.z, x, self.core))
        self.y_ring = Ring(4, self.place, lambda q: {"row": q // 2, "col": lax.rem(q, 2)})

    def dp(self, z, x, core):
        _, nx, nc = self.grid
        return {"dp": (z * nx + x) * nc + core}

    def greet_rings(self, rings, whole=False):
        count = 0
        for ring in rings:
            steps = range(1, ring.length) if whole else [step for _, step in ring.ways]
            for step in steps:
                greet(ring.device(step))
                count += 1
        return count


class WeightGather:
    def __init__(self, here, cut, copies, local, own, full, spread):
        self.here, self.copies, self.core_copies = here, copies, []
        rows, lanes = own.shape
        pair = full.shape[-1] != lanes
        first = cut if pair else rows // 2
        cuts = (pl.ds(0, first), pl.ds(first, rows - first))
        z, x, core, zls = here.z, here.x, here.core, here.zls

        def part(width, half):
            return (0, width) if half is None else (half * (width // 2), width // 2)

        def chunk(order, along, half):
            zz, xx = (along, x) if order == 0 else (z, along)
            start, width = part(lanes, half)
            if pair:
                at = lanes_at((zz // zls) * lanes + start, width)
                return full.at[lax.rem(zz, zls), xx, core, cuts[order], at]
            return full.at[zz, xx, core, cuts[order], pl.ds(start, width)]

        def line(order, along, half):
            if order == 0:
                at = pl.ds(*part(full.shape[-1], half))
                return full.at[:, along, core, cuts[0], at]
            start, width = part(lanes, half)
            if pair:
                at = lanes_at((along // zls) * lanes + start, width)
                return full.at[lax.rem(along, zls), :, core, cuts[1], at]
            return full.at[along, :, core, cuts[1], pl.ds(start, width)]

        def small(order, along, half):
            return None if half == 1 else spread[1].at[along, x, core]

        def small_line(order, along, half):
            return None if half == 1 else spread[1].at[:, along, core]

        rings = ((here.z_ring, here.x_ring), (here.x_ring, here.z_ring))
        self.first, self.second, self.lines, self.own = [], [], [], []
        for order in range(2):
            sources = [own.at[cuts[order]]]
            chunks, lines = [partial(chunk, order)], [partial(line, order)]
            if order == 0 and spread:
                sources.append(spread[0])
                chunks.append(partial(small, order))
                lines.append(partial(small_line, order))
            for k, view in enumerate(chunks):
                self.own.append(
                    pltpu.make_async_copy(
                        sources[k], view(rings[order][0].place, None), local.at[order * 2 + k]
                    )
                )
            self.first.append(RingGather(copies, rings[order][0], chunks, sources))
            self.second.append(
                RingGather(copies, rings[order][1], lines, None, partial(self.forward, order))
            )
            self.lines.append(lines)

    def forward(self, order, along):
        for view in self.lines[order]:
            ref = view(along, None)
            copy = self.copies.to(ref, ref, self.here.partner)
            copy.start()
            self.core_copies.append(copy)

    def start(self):
        for ring in self.first:
            ring.start()
        for copy in self.own:
            copy.start()

    def first_middle(self):
        for ring in self.first:
            ring.middle()

    def turn(self):
        for copy in self.own:
            copy.wait()
        for order in range(2):
            self.first[order].end()
            self.second[order].start()
            self.forward(order, self.second[order].ring.place)

    def second_middle(self):
        for ring in self.second:
            ring.middle()

    def end(self):
        for ring in self.second:
            ring.end()

    def arrive(self):
        for copy in self.core_copies:
            copy.wait_recv()

    def finish(self):
        for ring in self.first + self.second:
            ring.finish()
        for copy in self.core_copies:
            copy.wait_send()


def dot(left, right):
    return jnp.dot(left, right, preferred_element_type=F32)


def dot_rows(left, right):
    return lax.dot_general(left, right, CONTRACT_ROWS, preferred_element_type=F32)


def dot_cols(left, right):
    return lax.dot_general(left, right, CONTRACT_COLS, preferred_element_type=F32)


def norm_stats(state):
    width = state.shape[1]
    average = jnp.sum(state, 1, keepdims=True) / width
    spread = jnp.sum(state * state, 1, keepdims=True) / width - average * average
    inv_std = lax.rsqrt(spread + EPS_NORM)
    return ((state - average) * inv_std, inv_std)


def norm_back(grad_hat, hat):
    width = hat.shape[1]
    first = jnp.sum(grad_hat, 1, keepdims=True) / width
    second = jnp.sum(grad_hat * hat, 1, keepdims=True) / width
    return grad_hat - first - hat * second


class Layer:
    def __init__(self, layer, vec, tables, mask, bias, full_q, full_u, full_b, sizes):
        self.vec, self.tables, self.mask, self.bias = vec, tables, mask, bias
        self.layer, self.full_q, self.full_u, self.full_b = layer, full_q, full_u, full_b
        self.qkv_width, self.up_width, self.out_rows = sizes
        self.heads_here = self.qkv_width // (3 * HEAD)

    def vector(self, k):
        at = self.layer * VEC_ROWS + k
        return self.vec[at : at + 1, :]

    def q_matrix(self, start, width):
        return self.full_q[:, :, :, :, start : start + width].reshape(-1, width)

    def u_matrix(self, start, width):
        return self.full_u[:, :, :, :, start : start + width].reshape(-1, width)

    def b_matrix(self, low, high, start, width):
        value = self.full_b[:, :, :, low:high, start : start + width]
        return value.reshape(-1, width)

    def out_matrix(self, start, width):
        return self.b_matrix(0, self.out_rows, start, width)

    def down_matrix(self, start, width):
        return self.b_matrix(self.out_rows, self.full_b.shape[3], start, width)

    def inputs(self, hat, attn_in, mlp_in):
        attn_in[...] = (hat * self.vector(0) + self.vector(1)).astype(BF)
        mlp_in[...] = (hat * self.vector(2) + self.vector(3)).astype(BF)

    def project(self, attn_in, joined):
        pair = 6 * HEAD
        cosine, left, right = self.tables
        for start in range(0, self.qkv_width, pair):
            value = dot(attn_in[...], self.q_matrix(start, pair))
            value = value + self.bias[0:1, start : start + pair]
            value = (
                value * cosine[...]
                + pltpu.roll(value, pair - ROT // 2, 1) * left[...]
                + pltpu.roll(value, ROT // 2, 1) * right[...]
            )
            joined[:, start : start + pair] = value.astype(BF)

    def head(self, joined, h):
        start = h * 3 * HEAD
        return [joined[:, start + k * HEAD : start + (k + 1) * HEAD] for k in range(3)]

    def attend(self, joined, probs, heads):
        for h in range(self.heads_here):
            query, key_rows, value_rows = self.head(joined, h)
            scores = dot_cols(query, key_rows) * HEAD**-0.5 + self.mask[...]
            expo = jnp.exp(scores - jnp.max(scores, 1, keepdims=True))
            low = (expo / jnp.sum(expo, 1, keepdims=True)).astype(BF)
            probs[h] = low
            heads[:, h * HEAD : (h + 1) * HEAD] = dot(low, value_rows).astype(BF)

    def units(self, mlp_in, slope, units):
        width = 256
        for start in range(0, self.up_width, width):
            at = slice(start, start + width)
            value = dot(mlp_in[...], self.u_matrix(start, width))
            value = value + self.bias[1:2, at]
            below = 0.5 * (1.0 + lax.erf(value * 0.5**0.5))
            density = jnp.exp(value * value * -0.5) * ((2.0 * math.pi) ** -0.5)
            units[:, at] = (value * below).astype(BF)
            slope[:, at] = (below + value * density).astype(BF)

    def outputs(self, heads, units, start, width):
        return dot(heads[...], self.out_matrix(start, width)) + dot(
            units[...], self.down_matrix(start, width)
        )

    def branch_back(self, grad, slope, grad_heads, grad_pre):
        grad_heads[...] = dot_cols(grad[...], self.out_matrix(0, D)).astype(BF)
        zls = self.full_b.shape[0]
        width = self.up_width // zls
        step = min(width, 256)
        for zl in range(zls):
            matrix = self.full_b[zl, :, :, self.out_rows :, :].reshape(-1, D)
            for start in range(0, width, step):
                at = slice(zl * width + start, zl * width + start + step)
                pull = dot_cols(grad[...], matrix[start : start + step])
                grad_pre[:, at] = (pull * slope[:, at].astype(F32)).astype(BF)

    def attend_back(self, joined, probs, grad_heads, raw, grad_joined):
        for h in range(self.heads_here):
            query, key_rows, value_rows = self.head(joined, h)
            grad = grad_heads[:, h * HEAD : (h + 1) * HEAD]
            low = probs[h]
            high = low.astype(F32)
            grad_probs = dot_cols(grad, value_rows)
            inner = jnp.sum(grad_probs * high, 1, keepdims=True)
            grad_raw = (high * (grad_probs - inner) * HEAD**-0.5).astype(BF)
            start = h * 3 * HEAD
            raw[:, start : start + HEAD] = dot(grad_raw, key_rows)
            raw[:, start + HEAD : start + 2 * HEAD] = dot_rows(grad_raw, query)
            raw[:, start + 2 * HEAD : start + 3 * HEAD] = dot_rows(low, grad)
        pair = 6 * HEAD
        cosine, left, right = self.tables
        for start in range(0, self.qkv_width, pair):
            value = raw[:, start : start + pair]
            value = (
                value * cosine[...]
                + pltpu.roll(value * left[...], ROT // 2, 1)
                + pltpu.roll(value * right[...], pair - ROT // 2, 1)
            )
            grad_joined[:, start : start + pair] = value.astype(BF)

    def inputs_back(self, grad_joined, grad_pre, hat, grad, sums):
        grad_attn_in = dot_cols(grad_joined[...], self.q_matrix(0, self.qkv_width))
        rows = [
            jnp.sum(grad_attn_in * hat, 0, keepdims=True),
            jnp.sum(grad_attn_in, 0, keepdims=True),
        ]
        grad_hat = grad_attn_in * self.vector(0)
        grad_mlp_in = dot_cols(grad_pre[...], self.u_matrix(0, self.up_width))
        rows += [
            jnp.sum(grad_mlp_in * hat, 0, keepdims=True),
            jnp.sum(grad_mlp_in, 0, keepdims=True),
            jnp.sum(grad[...].astype(F32), 0, keepdims=True) * 0.25,
        ]
        for k, row in enumerate(rows):
            sums[k : k + 1, :] = row
        for k, (ref, width) in enumerate(
            ((grad_joined, self.qkv_width), (grad_pre, self.up_width))
        ):
            sums[5 + k : 6 + k, :] = jnp.zeros((1, D), F32)
            sums[5 + k : 6 + k, :width] = jnp.sum(ref[...].astype(F32), 0, keepdims=True)
        sums[7:8, :] = jnp.zeros((1, D), F32)
        return norm_back(grad_hat + grad_mlp_in * self.vector(2), hat)


def grads_a(left, right, out):
    width = right.shape[1]
    nz = out.shape[0]
    block = left.shape[1] // nz
    for k in range(nz):
        value = dot_rows(left[:, k * block : (k + 1) * block], right[...]).astype(BF)
        out[k] = value.reshape(*out.shape[1:4], width)


def grads_b(left, right, out, low, high):
    zls = out.shape[0]
    block = left.shape[1] // zls
    for k in range(zls):
        value = dot_rows(left[:, k * block : (k + 1) * block], right[...]).astype(BF)
        out[k, :, :, low:high, :] = value.reshape(*out.shape[1:3], high - low, D)


def rows_index(rows):
    def index(lead, target, start, width):
        return (
            pl.ds(pl.multiple_of(target * rows, rows), rows),
            lanes_at(start, width),
        )

    return index


def blocks_index(rows, lanes):
    def index(lead, target, start, width):
        return (
            pl.ds(pl.multiple_of(lax.rem(target, 2) * rows, rows), rows),
            lanes_at((target // 2) * lanes + start, width),
        )

    return index


def group_sum(here, copies, part, index, width, near, far):
    summand = Summand(part, index, None, width, (near.at[0], near.at[1]), (far.at[0], far.at[1]))
    return RingSum(copies, here.y_ring, [summand])


def group_gather(here, copies, whole, rows):
    def view(target, half):
        width = whole.shape[1]
        start, width = (0, width) if half is None else (half * (width // 2), width // 2)
        return whole.at[pl.ds(pl.multiple_of(target * rows, rows), rows), pl.ds(start, width)]

    return RingGather(copies, here.y_ring, [view])


def own_rows(here, rows):
    return pl.ds(pl.multiple_of(here.place * rows, rows), rows)


def ring_scratch(rows, width):
    return [pltpu.VMEM((2, rows, width // 2), BF), pltpu.VMEM((2, rows, width), BF)]


class GradSum:
    def __init__(self, here, cut, copies, kind, g, s, buffers):
        self.here, self.copies, self.kind, self.g, self.s = here, copies, kind, g, s
        self.near, self.far, self.mid, self.near_two, self.far_two, self.fin = buffers
        rows = g.shape[3]
        first = rows // 2 if kind == "a" else cut
        self.cuts = (pl.ds(0, first), pl.ds(first, rows - first))
        self.full = g.shape[4]
        self.lanes = self.full // 2
        self.lines, self.turns = [None, None], [None, None]

    def start(self):
        self.core = []
        for order in range(2):
            copy = self.copies.to(
                self.g.at[:, :, 1 - self.here.core, self.cuts[order]],
                self.s.at[:, :, self.cuts[order]],
                self.here.partner,
            )
            copy.start()
            self.core.append(copy)

    def line(self, order):
        here, at, zls = self.here, self.cuts[order], self.here.zls
        self.core[order].wait_recv()

        def add(zz, xx):
            self.s[zz, xx, at] = (
                self.s[zz, xx, at].astype(F32) + self.g[zz, xx, here.core, at].astype(F32)
            ).astype(BF)

        over(self.s.shape[:2], add)
        nx = self.s.shape[1]
        if order == 0:
            ring, count, width = here.x_ring, self.s.shape[0], self.full

            def index(lead, target, start, width):
                return (lead, target, at, lanes_at(start, width))

        elif self.kind == "a":
            ring, count, width = here.z_ring, nx, self.full

            def index(lead, target, start, width):
                return (target, lead, at, lanes_at(start, width))

        else:
            ring, count, width = here.z_ring, nx, self.lanes

            def index(lead, target, start, width):
                return (
                    lax.rem(target, zls),
                    lead,
                    at,
                    lanes_at((target // zls) * self.lanes + start, width),
                )

        summand = Summand(
            self.s,
            index,
            count,
            width,
            (self.near[order].at[0], self.near[order].at[1]),
            (self.far[order].at[0], self.far[order].at[1]),
        )
        self.lines[order] = RingSum(self.copies, ring, [summand])
        self.lines[order].start()

    def line_middle(self, order):
        self.lines[order].middle()

    def turn(self, order):
        here, zls, mid = self.here, self.here.zls, self.mid[order]
        line = self.lines[order]
        line.end()

        def put(lead):
            mid[lead] = line.total(0, lead).astype(BF)

        over(mid.shape[:1], put)
        ring = here.z_ring if order == 0 else here.x_ring
        if self.kind == "b" and order == 0:

            def index(lead, target, start, width):
                return (
                    lax.rem(target, zls),
                    slice(None),
                    lanes_at((target // zls) * self.lanes + start, width),
                )

        else:

            def index(lead, target, start, width):
                return (target, slice(None), lanes_at(start, width))

        summand = Summand(
            mid,
            index,
            None,
            self.full if self.kind == "a" else self.lanes,
            (self.near_two[order].at[0], self.near_two[order].at[1]),
            (self.far_two[order].at[0], self.far_two[order].at[1]),
        )
        self.turns[order] = RingSum(self.copies, ring, [summand])
        self.turns[order].start()

    def turn_middle(self, order):
        self.turns[order].middle()

    def end(self, order):
        self.turns[order].end()
        value = self.turns[order].total(0).astype(BF)
        if self.kind == "a":
            self.fin[order] = value
        else:
            self.fin[self.cuts[order]] = value

    def finish(self):
        for copy in self.core:
            copy.wait_send()
        for order in range(2):
            self.lines[order].finish()
            self.turns[order].finish()


def grad_buffers(grid, cut, g_shape, kind):
    nz, nx, _ = grid
    rows, full = g_shape[3:]
    zls = g_shape[0]
    first = rows // 2 if kind == "a" else cut
    lanes = full if kind == "a" else full // 2
    cuts = (first, rows - first)

    def low(*dims):
        return pltpu.VMEM(dims, BF)

    counts = (zls, nx)
    widths = (full, lanes)
    fin = low(2, first, full) if kind == "a" else low(rows, lanes)
    return [
        low(zls, nx, rows, full),
        *[low(2, counts[o], cuts[o], widths[o] // 2) for o in range(2)],
        *[low(2, counts[o], cuts[o], widths[o]) for o in range(2)],
        *[low(counts[o], cuts[o], widths[o]) for o in range(2)],
        *[low(2, cuts[o], lanes // 2) for o in range(2)],
        *[low(2, cuts[o], lanes) for o in range(2)],
        fin,
    ]


def grad_sum(here, cut, copies, kind, g, refs):
    s, near0, near1, far0, far1, mid0, mid1, low0, low1, top0, top1, fin = refs
    return GradSum(
        here,
        cut,
        copies,
        kind,
        g,
        s,
        ((near0, near1), (far0, far1), (mid0, mid1), (low0, low1), (top0, top1), fin),
    )


def lane_iota(rows, lanes):
    return lax.broadcasted_iota(jnp.int32, (rows, lanes), 1)


def make_tables(ids, live, cosine, left, right, mask):
    length = ids.shape[1]
    other = ids[...]
    row = lax.broadcasted_iota(jnp.int32, (length, length), 0)
    column = lax.broadcasted_iota(jnp.int32, (length, length), 1)
    other = jnp.broadcast_to(other.astype(F32), (length, length))
    own = jnp.sum(jnp.where(row == column, other, 0.0), 1, keepdims=True)
    live[...] = jnp.broadcast_to(jnp.where(own < SEQS, 1.0, 0.0), live.shape)
    earlier = jnp.sum((other < own).astype(F32), 1, keepdims=True)
    mask[...] = jnp.where((other == own) & (column <= row), 0.0, MASK_VALUE)
    place = lax.broadcasted_iota(jnp.int32, (length, 1), 0).astype(F32) - earlier
    lane = lane_iota(1, 128)
    at = lax.rem(lane, HEAD)
    turned = at < ROT
    power = lax.rem(at, ROT // 2).astype(F32)
    frequency = jnp.exp(power * (-2.0 / ROT * math.log(ROPE_BASE)))
    angles = place * frequency
    cos_part = jnp.where(turned, jnp.cos(angles), 1.0)
    sin_part = jnp.sin(angles)
    left_part = jnp.where(at < ROT // 2, -sin_part, 0.0)
    right_part = jnp.where(turned & (at >= ROT // 2), sin_part, 0.0)
    low_half = lane < HEAD
    for ref, value, rest in ((cosine, cos_part, 1.0), (left, left_part, 0.0), (right, right_part, 0.0)):
        ref[:, 0:128] = value
        ref[:, 128:256] = jnp.where(low_half, rest, value)
        ref[:, 256:384] = jnp.where(low_half, value, rest)


def make_biases(full_c, bias, widths):
    n_dp = math.prod(full_c.shape[:3])
    table = full_c[...].reshape(n_dp, *full_c.shape[3:])
    lanes = full_c.shape[4]
    for layer in range(LAYERS):
        values = table[:, layer, :].astype(BF)
        first = 0
        for k, width in enumerate(widths):
            total = n_dp * width
            lane = lax.broadcasted_iota(jnp.int32, (lanes, total), 0)
            column = lax.broadcasted_iota(jnp.int32, (lanes, total), 1)
            pick = jnp.where(lane == lax.rem(column, width) + first, 1.0, 0.0).astype(BF)
            spread = dot(values, pick)
            device = lax.broadcasted_iota(jnp.int32, (n_dp, total), 0)
            column = lax.broadcasted_iota(jnp.int32, (n_dp, total), 1)
            mine = jnp.where(column // width == device, spread, 0.0)
            bias[layer * 2 + k : layer * 2 + k + 1, :total] = jnp.sum(mine, 0, keepdims=True)
            first += width


def whole_kernel(grid, cut, sizes, widths, tree, *refs):
    at = SimpleNamespace(**jax.tree.unflatten(tree, refs))
    sends, recvs, local = at.sends, at.recvs, at.local
    here = Slice(grid)
    nz, nx, _ = grid
    copies = Copies(sends, recvs)
    copies.count = 48
    d, r, c, half = here.d, here.row, here.col, here.half
    hid, cot = at.hid, at.cot
    hid_all, cot_all, vec = at.hid_all, at.cot_all, at.vec
    rows, lanes = hid.shape
    quarter = rows // 2
    dh, dl = d // half, lax.rem(d, half)
    swap_needed = dh != r
    swap_to = {"dp": r * half + dl, "row": dh}
    slot_rows = at.qkv_weight.shape[1]
    forth = [{"dp": r * half + d // 2, "row": k} for k in range(2)]
    back_to = [{"dp": 2 * dl + k, "row": dh} for k in range(2)]
    forth_self = [(r == k) & (r * half + d // 2 == d) for k in range(2)]
    back_self = [(dh == r) & (2 * dl + k == d) for k in range(2)]
    slot = lax.rem(d, 2)

    count = here.greet_rings([here.z_ring, here.x_ring, here.y_ring], whole=True)
    greet(here.partner)
    for k in range(2):
        for device, itself in ((forth[k], forth_self[k]), (back_to[k], back_self[k])):

            @pl.when(jnp.logical_not(itself))
            def _():
                greet(device)

    @pl.when(swap_needed)
    def _():
        greet(swap_to)

    qkv_width, up_width, out_rows = sizes
    wa, wb = (at.wq, at.wu), at.wb

    def cast(layer):
        for ref, given, width in ((wa[0], at.qkv_weight, qkv_width), (wa[1], at.up_weight, up_width)):
            for k in range(2):
                ref[layer, k] = given[layer, :, k * width : (k + 1) * width].astype(BF)
        wb[layer, :out_rows] = at.out_weight[layer].astype(BF)
        wb[layer, out_rows:] = at.down_weight[layer].astype(BF)

    cast(0)
    vec_own, wc = at.vec_own, at.wc
    vec_own[...] = jnp.zeros(vec_own.shape, F32)
    for layer in range(LAYERS):
        vec_own[layer * VEC_ROWS : layer * VEC_ROWS + 6] = at.row_vectors[layer]
    wc[...] = jnp.zeros(wc.shape, F32)
    wc[:LAYERS, : widths[0]] = at.qkv_bias[...]
    wc[:LAYERS, widths[0] : sum(widths)] = at.up_bias[...]
    greeted(
        count
        + 5
        + swap_needed.astype(jnp.int32)
        - sum(k.astype(jnp.int32) for k in forth_self + back_self)
    )

    def when_else(condition, there, here_do):
        pl.when(condition)(there)
        pl.when(jnp.logical_not(condition))(here_do)

    def pair(src, dst, send, recv, device):
        return pltpu.make_async_remote_copy(
            src_ref=src,
            dst_ref=dst,
            send_sem=sends.at[send],
            recv_sem=recvs.at[recv],
            device_id=device,
            device_id_type=MESH,
        )

    a_own, b_own = (at.q_own, at.u_own), at.b_own
    slot_at = pl.ds(pl.multiple_of(slot * slot_rows, slot_rows), slot_rows)

    def a_copy(layer, kind, k):
        base = layer * 8 + kind * 2
        return pair(
            wa[kind].at[layer, k], a_own[kind].at[layer, slot_at], base + k, base + slot, forth[k]
        )

    def a_arrival(layer, kind, k):
        base = layer * 8 + kind * 2
        into = a_own[kind].at[layer, pl.ds(k * slot_rows, slot_rows)]
        return pair(wa[kind].at[layer, 0], into, base, base + k, back_to[k])

    def a_local(layer, kind, k):
        return pltpu.make_async_copy(
            wa[kind].at[layer, k], a_own[kind].at[layer, slot_at], local.at[24 + layer * 2 + kind]
        )

    def swap_copy(layer):
        return pair(wb.at[layer], b_own.at[layer], layer * 8 + 4, layer * 8 + 4, swap_to)

    def swap_local(layer):
        return pltpu.make_async_copy(wb.at[layer], b_own.at[layer], local.at[28 + layer])

    def begin(layer):
        for kind in range(2):
            for k in range(2):
                when_else(
                    forth_self[k],
                    lambda: a_local(layer, kind, k).start(),
                    lambda: a_copy(layer, kind, k).start(),
                )
        when_else(
            swap_needed, lambda: swap_copy(layer).start(), lambda: swap_local(layer).start()
        )

    def complete_a(layer, kind):
        for k in range(2):
            when_else(
                forth_self[k],
                lambda: a_local(layer, kind, k).wait(),
                lambda: a_copy(layer, kind, k).wait_send(),
            )

            @pl.when(jnp.logical_not(back_self[k]))
            def _():
                a_arrival(layer, kind, k).wait_recv()

    def complete_b(layer):
        when_else(swap_needed, lambda: swap_copy(layer).wait(), lambda: swap_local(layer).wait())

    begin(0)
    tokens = pl.ds(pl.multiple_of(c * rows, rows), rows)
    features = pl.ds(pl.multiple_of(r * lanes, lanes), lanes)
    hid_copies = [
        copies.to(hid, hid_all.at[tokens, features], here.y_ring.device(k)) for k in range(1, 4)
    ]
    cot_copies = [
        copies.to(cot, cot_all.at[tokens, features], here.y_ring.device(k)) for k in range(1, 4)
    ]
    hid_copies.append(copies.to(vec_own, vec.at[:, features], {"row": 1 - r}))
    own = [
        pltpu.make_async_copy(hid, hid_all.at[tokens, features], local.at[36]),
        pltpu.make_async_copy(cot, cot_all.at[tokens, features], local.at[37]),
        pltpu.make_async_copy(vec_own, vec.at[:, features], local.at[38]),
    ]
    for copy in hid_copies + own:
        copy.start()
    tables, mask, bias = (at.cosine, at.left, at.right), at.mask, at.bias
    complete_a(0, 0)

    full = ((at.q_zero, at.u_zero, at.b_zero), (at.q_one, at.u_one, at.b_one))
    full_c = at.full_c
    gathers = []
    for k in range(LAYERS):
        for kind in range(3):
            source = (a_own + (b_own,))[kind].at[k]
            spread = (wc, full_c) if k == 0 and kind == 0 else None
            count = 4 * (3 * k + kind)
            gathers.append(
                WeightGather(
                    here, cut, copies, local.at[pl.ds(count, 4)], source, full[k][kind], spread
                )
            )
    near, late = gathers[:3], gathers[3:]
    near[0].start()
    complete_a(0, 1)
    near[1].start()
    complete_b(0)
    near[2].start()
    cast(1)
    begin(1)
    near[0].first_middle()
    for copy in hid_copies + own:
        copy.wait()
    layers = [
        Layer(k, vec, tables, mask, bias.at[pl.ds(2 * k, 2)], *full[k], sizes)
        for k in range(LAYERS)
    ]
    attn_in, mlp_in, joined, probs = at.attn_in, at.mlp_in, at.joined, at.probs
    heads, slope, units = at.heads, at.slope, at.units
    near[0].turn()
    near[1].first_middle()
    near[2].first_middle()
    make_tables(at.ids, at.live, *tables, mask)
    near[1].turn()
    near[0].second_middle()
    near[2].turn()
    near[0].end()
    near[1].second_middle()
    hat, _ = norm_stats(hid_all[...].astype(F32))
    layers[0].inputs(hat, attn_in[0], mlp_in[0])
    near[0].arrive()
    near[1].end()
    near[2].second_middle()
    make_biases(full_c, bias, widths)
    complete_a(1, 0)
    late[0].start()
    complete_a(1, 1)
    late[1].start()
    complete_b(1)
    late[2].start()
    for copy in cot_copies:
        copy.start()
    mine = own_rows(here, quarter)
    layers[0].project(attn_in[0], joined[0])
    near[2].end()
    for one in late:
        one.first_middle()
    layers[0].attend(joined[0], probs[0], heads[0])
    for one in late:
        one.turn()
    near[1].arrive()
    layers[0].units(mlp_in[0], slope[0], units[0])
    for one in late[:2]:
        one.second_middle()
    near[2].arrive()
    part = at.part[0]
    for start in (0, D // 2):
        part[:, start : start + D // 2] = (
            layers[0].outputs(heads[0], units[0], start, D // 2).astype(BF)
        )
    summed = group_sum(here, copies, part, rows_index(quarter), D, at.near[0], at.far[0])
    summed.start()
    late[2].second_middle()
    summed.middle()
    state = hid_all[mine, :].astype(F32) + layers[0].vector(4) + layers[0].vector(5)
    summed.end()
    state = state + summed.total(0)
    at.state[...] = state
    hat, inverse = norm_stats(state)
    inv_std, hat_all = at.inv_std, at.hat_all
    inv_std[...] = jnp.broadcast_to(inverse, inv_std.shape)
    hat_all[mine, :] = hat.astype(BF)
    spread = group_gather(here, copies, hat_all, quarter)
    spread.start()
    grad = (at.grad[0], at.grad[1])
    for copy in cot_copies:
        copy.wait()
    grad[1][...] = (
        cot_all[...].astype(F32) * at.live[:, :1]
    ).astype(BF)
    spread.middle()
    for one in late:
        one.end()
    spread.end()
    for one in late:
        one.arrive()
    for one in gathers:
        one.finish()
    rings = [summed, spread]

    layer = layers[1]
    layer.inputs(hat_all[...].astype(F32), attn_in[1], mlp_in[1])
    layer.project(attn_in[1], joined[1])
    layer.attend(joined[1], probs[1], heads[1])
    layer.units(mlp_in[1], slope[1], units[1])
    part = at.part[1]
    for start in (0, D // 2):
        part[:, start : start + D // 2] = (
            layer.outputs(heads[1], units[1], start, D // 2).astype(BF)
        )
    part[mine, :] = (part[mine, :].astype(F32) + at.state[...]).astype(BF)
    out_sum = group_sum(
        here, copies, part, blocks_index(rows, lanes), lanes, at.near[1], at.far[1]
    )
    out_sum.start()
    grad_heads, grad_pre, raw, grad_joined = (
        at.grad_heads,
        at.grad_pre,
        at.raw,
        at.grad_joined,
    )
    sums = (at.sums[0], at.sums[1])
    layer.branch_back(grad[1], slope[1], grad_heads, grad_pre)
    out_sum.middle()
    layer.attend_back(joined[1], probs[1], grad_heads, raw, grad_joined)
    back = at.back[1]
    back[...] = layer.inputs_back(
        grad_joined, grad_pre, hat_all[...].astype(F32), grad[1], sums[1]
    ).astype(BF)
    summed = group_sum(here, copies, back, rows_index(quarter), D, at.near[2], at.far[2])
    summed.start()

    grads = [
        full[1],
        (at.gq, at.gu, at.gb),
    ]
    sum_q, sum_u, sum_b = [
        [
            grad_sum(
                here,
                cut,
                copies,
                "aab"[kind],
                grads[k][kind],
                at.sum_buffers[k][kind],
            )
            for k in range(LAYERS)
        ]
        for kind in range(3)
    ]
    out_q, out_u, out_b = at.out_q, at.out_u, at.out_b

    def owner_copy(layer, kind, order):
        out, one = ((out_q, sum_q), (out_u, sum_u))[kind]
        base = 16 + layer * 8 + kind * 2
        return pair(
            one[layer].fin.at[order], out.at[layer, r], base + order, base + r, back_to[order]
        )

    def owner_arrival(layer, kind, k):
        out, one = ((out_q, sum_q), (out_u, sum_u))[kind]
        base = 16 + layer * 8 + kind * 2
        return pair(one[layer].fin.at[0], out.at[layer, k], base, base + k, forth[k])

    def owner_local(layer, kind, order):
        out, one = ((out_q, sum_q), (out_u, sum_u))[kind]
        return pltpu.make_async_copy(
            one[layer].fin.at[order], out.at[layer, r], local.at[30 + layer * 2 + kind]
        )

    def out_swap(layer):
        return pair(sum_b[layer].fin, out_b.at[layer], 20 + layer * 8, 20 + layer * 8, swap_to)

    def out_local(layer):
        return pltpu.make_async_copy(sum_b[layer].fin, out_b.at[layer], local.at[34 + layer])

    def hand_a(layer, kind):
        for order in range(2):
            when_else(
                back_self[order],
                lambda: owner_local(layer, kind, order).start(),
                lambda: owner_copy(layer, kind, order).start(),
            )

    def hand_b(layer):
        when_else(swap_needed, lambda: out_swap(layer).start(), lambda: out_local(layer).start())

    def handed(layer):
        for kind in range(2):
            for k in range(2):
                when_else(
                    back_self[k],
                    lambda: owner_local(layer, kind, k).wait(),
                    lambda: owner_copy(layer, kind, k).wait_send(),
                )

                @pl.when(jnp.logical_not(forth_self[k]))
                def _():
                    owner_arrival(layer, kind, k).wait_recv()

        when_else(swap_needed, lambda: out_swap(layer).wait(), lambda: out_local(layer).wait())

    def phase(step, which):
        for order in range(2):
            for one in which:
                step(one, order)

    grads_a(mlp_in[1], grad_pre, grads[1][1])
    sum_u[1].start()
    summed.middle()
    grads_a(attn_in[1], grad_joined, grads[1][0])
    sum_q[1].start()
    out_sum.end()
    bias_sum = vec[VEC_ROWS + 4 : VEC_ROWS + 5, features] + vec[VEC_ROWS + 5 : VEC_ROWS + 6, features]
    at.hidden[...] = (out_sum.total(0) + bias_sum).astype(BF)
    summed.end()
    grad_one = at.grad_one
    total = grad[1][mine, :].astype(F32) + inv_std[:, :1] * summed.total(0)
    grad_one[...] = total
    grad[0][mine, :] = total.astype(BF)
    spread = group_gather(here, copies, grad[0], quarter)
    spread.start()
    grads_b(heads[1], grad[1], grads[1][2], 0, out_rows)
    grads_b(units[1], grad[1], grads[1][2], out_rows, at.gb.shape[3])
    sum_b[1].start()
    spread.middle()
    phase(GradSum.line, [sum_u[1], sum_q[1]])
    spread.end()
    rings += [out_sum, summed, spread]

    layer = layers[0]
    grads_b(heads[0], grad[0], grads[0][2], 0, out_rows)
    grads_b(units[0], grad[0], grads[0][2], out_rows, at.gb.shape[3])
    sum_b[0].start()
    phase(GradSum.line, [sum_b[1]])
    phase(GradSum.line_middle, [sum_u[1], sum_q[1]])
    layer.branch_back(grad[0], slope[0], grad_heads, grad_pre)
    phase(GradSum.line_middle, [sum_b[1]])
    grads_a(mlp_in[0], grad_pre, grads[0][1])
    sum_u[0].start()
    phase(GradSum.turn, [sum_u[1], sum_q[1]])
    layer.attend_back(joined[0], probs[0], grad_heads, raw, grad_joined)
    phase(GradSum.turn, [sum_b[1]])
    phase(GradSum.line, [sum_b[0]])
    grads_a(attn_in[0], grad_joined, grads[0][0])
    sum_q[0].start()
    phase(GradSum.line, [sum_u[0]])
    phase(GradSum.turn_middle, [sum_u[1], sum_q[1], sum_b[1]])
    hat, inverse = norm_stats(hid_all[...].astype(F32))
    value = layer.inputs_back(grad_joined, grad_pre, hat, grad[0], sums[0])
    back = at.back[0]
    back[...] = (inverse * value).astype(BF)
    back[mine, :] = (back[mine, :].astype(F32) + grad_one[...]).astype(BF)
    summed = group_sum(
        here, copies, back, blocks_index(rows, lanes), lanes, at.near[3], at.far[3]
    )
    summed.start()
    phase(GradSum.line_middle, [sum_b[0]])
    phase(GradSum.line, [sum_q[0]])
    phase(GradSum.line_middle, [sum_u[0]])
    v_core, v_line, v_last, v_group = at.v_core, at.v_line, at.v_last, at.v_group
    v_lanes = D // 2
    v_mine = pl.ds(pl.multiple_of(here.core * v_lanes, v_lanes), v_lanes)
    v_other = pl.ds(pl.multiple_of((1 - here.core) * v_lanes, v_lanes), v_lanes)
    v_copies = [copies.to(sums[k].at[:, v_other], v_core.at[k], here.partner) for k in range(2)]
    for copy in v_copies:
        copy.start()
    summed.middle()
    for order in range(2):
        for one in (sum_q[1], sum_u[1], sum_b[1]):
            one.end(order)
    hand_a(1, 0)
    hand_a(1, 1)
    hand_b(1)
    for copy in v_copies:
        copy.wait()
    for k in range(LAYERS):
        v_line[here.x, k * VEC_ROWS : (k + 1) * VEC_ROWS] = v_core[k] + sums[k][:, v_mine]
    v_x = [
        copies.to(v_line.at[here.x], v_line.at[here.x], here.x_ring.device(k))
        for k in range(1, nx)
    ]
    for copy in v_x:
        copy.start()
    phase(GradSum.line_middle, [sum_q[0]])
    phase(GradSum.turn, [sum_b[0], sum_u[0]])
    summed.end()
    at.grad_out[...] = summed.total(0)
    rings.append(summed)
    for copy in v_x:
        copy.wait()
    total = v_line[0]
    for k in range(1, nx):
        total = total + v_line[k]
    v_last[here.z] = total
    v_z = [
        copies.to(v_last.at[here.z], v_last.at[here.z], here.z_ring.device(k))
        for k in range(1, nz)
    ]
    for copy in v_z:
        copy.start()
    phase(GradSum.turn_middle, [sum_b[0], sum_u[0]])
    phase(GradSum.turn, [sum_q[0]])
    for copy in v_z:
        copy.wait()
    total = v_last[0]
    for k in range(1, nz):
        total = total + v_last[k]
    v_group[here.place] = total
    v_y = [
        copies.to(v_group.at[here.place], v_group.at[here.place], here.y_ring.device(k))
        for k in range(1, 4)
    ]
    for copy in v_y:
        copy.start()
    phase(GradSum.turn_middle, [sum_q[0]])
    for order in range(2):
        sum_b[0].end(order)
        sum_u[0].end(order)
    hand_b(0)
    hand_a(0, 1)
    for copy in v_y:
        copy.wait()
    total = v_group[0]
    for k in range(1, 4):
        total = total + v_group[k]
    out_v = at.out_v
    out_v[0, :, v_mine] = total
    out_v[1, :, v_mine] = v_group[here.place]
    v_swap = copies.to(out_v.at[:, :, v_mine], out_v.at[:, :, v_mine], here.partner)
    v_swap.start()
    for order in range(2):
        sum_q[0].end(order)
    hand_a(0, 0)
    v_swap.wait()
    handed(1)
    handed(0)
    assert copies.count <= sends.shape[0], copies.count
    for ring in rings:
        ring.finish()
    for one in sum_q + sum_u + sum_b:
        one.finish()


def whole(grid, cut, sizes, widths, ins):
    nz, nx, nc = grid
    qkv_width, up_width, out_rows = sizes
    rows, lanes = ins["hid"].shape
    group, quarter = 2 * rows, rows // 2
    slot_rows, down_rows = ins["qkv_weight"].shape[1], ins["down_weight"].shape[1]
    b_rows = out_rows + down_rows
    heads_here = qkv_width // (3 * HEAD)

    def low(*dims):
        return pltpu.VMEM(dims, BF)

    def high(*dims):
        return pltpu.VMEM(dims, F32)

    def twice(make, *dims):
        return [make(*dims) for _ in range(LAYERS)]

    shape = jax.ShapeDtypeStruct
    outs = dict(
        hidden=shape((rows, lanes), BF),
        grad_out=shape((rows, lanes), F32),
        out_q=shape((LAYERS, 2, slot_rows, qkv_width), BF),
        out_u=shape((LAYERS, 2, slot_rows, up_width), BF),
        out_b=shape((LAYERS, b_rows, lanes), BF),
        out_v=shape((2, LAYERS * VEC_ROWS, D), F32),
    )
    q_shape = (nz, nx, nc, 2 * slot_rows, qkv_width)
    u_shape = (nz, nx, nc, 2 * slot_rows, up_width)
    b_shape = (nz // 2, nx, nc, b_rows, 2 * lanes)
    c_shape = (8, -(-sum(widths) // 128) * 128)
    kinds = ((q_shape, "a"), (u_shape, "a"), (b_shape, "b"))
    blocks = [ring_scratch(quarter, D), ring_scratch(rows, lanes)] * 2
    scratch = dict(
        hid_all=low(group, D),
        cot_all=low(group, D),
        vec=high(LAYERS * VEC_ROWS, D),
        vec_own=high(LAYERS * VEC_ROWS, lanes),
        wq=low(LAYERS, 2, slot_rows, qkv_width),
        wu=low(LAYERS, 2, slot_rows, up_width),
        wb=low(LAYERS, b_rows, lanes),
        wc=high(*c_shape),
        q_own=low(LAYERS, 2 * slot_rows, qkv_width),
        u_own=low(LAYERS, 2 * slot_rows, up_width),
        b_own=low(LAYERS, b_rows, lanes),
        q_zero=low(*q_shape),
        q_one=low(*q_shape),
        u_zero=low(*u_shape),
        u_one=low(*u_shape),
        b_zero=low(*b_shape),
        b_one=low(*b_shape),
        full_c=high(nz, nx, nc, *c_shape),
        cosine=high(group, 6 * HEAD),
        left=high(group, 6 * HEAD),
        right=high(group, 6 * HEAD),
        mask=high(group, group),
        live=high(group, 128),
        bias=high(2 * LAYERS, D),
        state=high(quarter, D),
        inv_std=high(quarter, 128),
        hat_all=low(group, D),
        grad_one=high(quarter, D),
        grad_heads=low(group, heads_here * HEAD),
        grad_pre=low(group, up_width),
        raw=high(group, qkv_width),
        grad_joined=low(group, qkv_width),
        gq=low(*q_shape),
        gu=low(*u_shape),
        gb=low(*b_shape),
        v_core=high(2, VEC_ROWS, D // 2),
        v_line=high(nx, LAYERS * VEC_ROWS, D // 2),
        v_last=high(nz, LAYERS * VEC_ROWS, D // 2),
        v_group=high(4, LAYERS * VEC_ROWS, D // 2),
        attn_in=twice(low, group, D),
        mlp_in=twice(low, group, D),
        joined=twice(low, group, qkv_width),
        probs=twice(low, heads_here, group, group),
        heads=twice(low, group, heads_here * HEAD),
        slope=twice(low, group, up_width),
        units=twice(low, group, up_width),
        part=twice(low, group, D),
        back=twice(low, group, D),
        grad=twice(low, group, D),
        sums=twice(high, VEC_ROWS, D),
        sum_buffers=[
            [grad_buffers(grid, cut, dims, kind) for dims, kind in kinds] for _ in range(LAYERS)
        ],
        near=[block[0] for block in blocks],
        far=[block[1] for block in blocks],
        sends=pltpu.SemaphoreType.DMA((480,)),
        recvs=pltpu.SemaphoreType.DMA((480,)),
        local=pltpu.SemaphoreType.DMA((40,)),
    )
    flat = jax.tree.leaves(scratch)
    tree = jax.tree.structure(dict(**ins, **outs, **scratch))
    order = [*ins.values(), *outs.values(), *scratch.values()]
    names = [*ins, *outs, *scratch]
    ranks = jax.tree.unflatten(
        jax.tree.structure(dict(zip(names, order))), range(tree.num_leaves)
    )
    given = jax.tree.leaves([ranks[name] for name in names])

    def kernel(*refs):
        placed = [None] * len(refs)
        for rank, ref in zip(given, refs):
            placed[rank] = ref
        whole_kernel(grid, cut, sizes, widths, tree, *placed)

    flat = jax.tree.leaves(list(scratch.values()))
    return pl.pallas_call(
        kernel,
        out_shape=tuple(outs.values()),
        in_specs=[VMEM_SPEC] * len(ins),
        out_specs=(VMEM_SPEC,) * len(outs),
        scratch_shapes=flat,
        compiler_params=params(0, 63),
        name="whole_step",
    )(*ins.values())


def update_kernel(n_dp, bias_widths, out_rows, *refs):
    own_q, own_u, own_b, all_v = refs[:4]
    old, new = refs[4:25], refs[25:]
    d, r = lax.axis_index("dp"), lax.axis_index("row")

    def update(k, gradient, rate, decay):
        values = adamw(*[ref[...] for ref in old[3 * k : 3 * k + 3]], gradient, rate, decay)
        for ref, value in zip(new[3 * k : 3 * k + 3], values):
            ref[...] = value

    for k, own in ((0, own_q), (2, own_u)):
        width = own.shape[3]
        for layer in range(LAYERS):
            for side in range(2):
                at = (layer, slice(None), slice(side * width, (side + 1) * width))
                gradient = own[layer, side].astype(F32)
                values = adamw(
                    *[ref[at] for ref in old[3 * k : 3 * k + 3]], gradient, RATE_MATRIX, DECAY_MATRIX
                )
                for ref, value in zip(new[3 * k : 3 * k + 3], values):
                    ref[at] = value
    update(1, own_b[:, :out_rows].astype(F32), RATE_MATRIX, DECAY_MATRIX)
    update(3, own_b[:, out_rows:].astype(F32), RATE_MATRIX, DECAY_MATRIX)
    for k, width in enumerate(bias_widths):
        for layer in range(LAYERS):
            rows = all_v[1, layer * VEC_ROWS : (layer + 1) * VEC_ROWS, :]
            moved = pltpu.roll(rows, lax.rem(D - d * width, D), 1)
            at = (slice(layer, layer + 1), slice(None))
            values = adamw(
                *[ref[at] for ref in old[12 + 3 * k : 15 + 3 * k]],
                moved[5 + k : 6 + k, :width],
                RATE_MATRIX,
                0.0,
            )
            for ref, value in zip(new[12 + 3 * k : 15 + 3 * k], values):
                ref[at] = value
    lanes = old[18].shape[2]
    features = pl.ds(pl.multiple_of(r * lanes, lanes), lanes)
    for layer in range(LAYERS):
        for k in range(6):
            row = layer * VEC_ROWS + min(k, 4)
            at = (layer, slice(k, k + 1), slice(None))
            values = adamw(
                *[ref[at] for ref in old[18:21]],
                all_v[0, row : row + 1, features],
                RATE_VECTOR,
                0.0,
            )
            for ref, value in zip(new[18:21], values):
                ref[at] = value


def update_all(n_dp, bias_widths, out_rows, gradients, old):
    return pl.pallas_call(
        partial(update_kernel, n_dp, bias_widths, out_rows),
        out_shape=tuple(jax.ShapeDtypeStruct(a.shape, F32) for a in old),
        in_specs=[VMEM_SPEC] * (4 + len(old)),
        out_specs=(VMEM_SPEC,) * len(old),
        compiler_params=pltpu.CompilerParams(vmem_limit_bytes=32 << 20),
        name="update_all",
    )(*gradients, *old)


def on_device(
    hidden_in,
    cotangent,
    seq_ids,
    qkv_weight,
    qkv_first,
    qkv_second,
    out_weight,
    out_first,
    out_second,
    up_weight,
    up_first,
    up_second,
    down_weight,
    down_first,
    down_second,
    qkv_bias,
    qkv_bias_first,
    qkv_bias_second,
    up_bias,
    up_bias_first,
    up_bias_second,
    row_vectors,
    row_first,
    row_second,
):
    n_dp = lax.axis_size("dp")
    grid = GRIDS[n_dp]
    group_len = seq_ids.shape[0]
    qkv_width, up_width = qkv_weight.shape[2] // 2, up_weight.shape[2] // 2
    out_rows, down_rows = out_weight.shape[1], down_weight.shape[1]
    bias_widths = qkv_bias.shape[1], up_bias.shape[1]
    cut = out_rows + down_rows // 2
    sizes = (qkv_width, up_width, out_rows)

    ins = dict(
        hid=hidden_in,
        cot=cotangent,
        ids=seq_ids.reshape(1, group_len),
        row_vectors=row_vectors,
        qkv_bias=qkv_bias,
        up_bias=up_bias,
        qkv_weight=qkv_weight,
        out_weight=out_weight,
        up_weight=up_weight,
        down_weight=down_weight,
    )
    hidden_out, grad_state, *gradients = whole(grid, cut, sizes, bias_widths, ins)
    old = (
        qkv_weight,
        qkv_first,
        qkv_second,
        out_weight,
        out_first,
        out_second,
        up_weight,
        up_first,
        up_second,
        down_weight,
        down_first,
        down_second,
        qkv_bias,
        qkv_bias_first,
        qkv_bias_second,
        up_bias,
        up_bias_first,
        up_bias_second,
        row_vectors,
        row_first,
        row_second,
    )
    return hidden_out, grad_state, *update_all(n_dp, bias_widths, out_rows, gradients, old)


def solution(mesh):
    placed = (
        P(("dp", "col"), "row"),
        P(("dp", "col"), "row"),
        P("dp"),
        P(None, ("row", "dp"), "col"),
        P(None, ("row", "dp"), "col"),
        P(None, ("row", "dp"), "col"),
        P(None, ("col", "dp"), "row"),
        P(None, ("col", "dp"), "row"),
        P(None, ("col", "dp"), "row"),
        P(None, ("row", "dp"), "col"),
        P(None, ("row", "dp"), "col"),
        P(None, ("row", "dp"), "col"),
        P(None, ("col", "dp"), "row"),
        P(None, ("col", "dp"), "row"),
        P(None, ("col", "dp"), "row"),
        P(None, ("col", "row", "dp")),
        P(None, ("col", "row", "dp")),
        P(None, ("col", "row", "dp")),
        P(None, ("col", "row", "dp")),
        P(None, ("col", "row", "dp")),
        P(None, ("col", "row", "dp")),
        P(None, None, "row"),
        P(None, None, "row"),
        P(None, None, "row"),
    )
    return jax.shard_map(
        on_device,
        mesh=mesh,
        in_specs=placed,
        out_specs=(
            P(("dp", "col"), "row"),
            P(("dp", "col"), "row"),
            P(None, ("row", "dp"), "col"),
            P(None, ("row", "dp"), "col"),
            P(None, ("row", "dp"), "col"),
            P(None, ("col", "dp"), "row"),
            P(None, ("col", "dp"), "row"),
            P(None, ("col", "dp"), "row"),
            P(None, ("row", "dp"), "col"),
            P(None, ("row", "dp"), "col"),
            P(None, ("row", "dp"), "col"),
            P(None, ("col", "dp"), "row"),
            P(None, ("col", "dp"), "row"),
            P(None, ("col", "dp"), "row"),
            P(None, ("col", "row", "dp")),
            P(None, ("col", "row", "dp")),
            P(None, ("col", "row", "dp")),
            P(None, ("col", "row", "dp")),
            P(None, ("col", "row", "dp")),
            P(None, ("col", "row", "dp")),
            P(None, None, "row"),
            P(None, None, "row"),
            P(None, None, "row"),
        ),
        check_vma=False,
    )
```

time: 245 us -> 192 us (0.78)
  Pallas kernels: 210 us -> 173 us
  other arithmetic: 12 us -> 0 us
  local copies, waits for them, and re-layouts: 20.4 us -> 17.4 us
    pallas_call x4 -> x2, Pallas kernels: 210 us -> 173 us  [the longest x1 171 us: whole(): pl.pallas_call(kernel, out_shape=tuple(outs.values()), in_specs=[VMEM_SPE...]
    unnamed x72 -> x62, local copies, waits for them, and re-layouts: 8.45 us -> 16.1 us
    sub x7 -> x0, other arithmetic: 5.49 us -> none  [adamw(): master - step_rate * (one_hat / (jnp.sqrt(two_hat) + EPS_ADAM) + step_dec...]
    concatenate x5 -> x0, local copies, waits for them, and re-layouts: 4.38 us -> none  [the longest x3 4.26 us: pair(): return jnp.concatenate([block, block, rest] * 2, 1)]
    squeeze x5 -> x0, local copies, waits for them, and re-layouts: 4.29 us -> none  [the longest x1 0.96 us: on_device(): vector_grad = lax.dynamic_slice_in_dim(all_v[0], r * lanes, lanes, axis=2)]
    another operation x8 -> x0, other arithmetic: 3.84 us -> none
where the time goes in v2:
time: 192 us; the launch traced here: 191 us
  Pallas kernels  173 us (90%)
  local copies, waits for them, and re-layouts  17.4 us (9%)
    pallas_call x1, Pallas kernels, whole(): pl.pallas_call(kernel, out_shape=tuple(outs.values()), in_specs=[VMEM_SPE...  171 us
    unnamed x62, local copies, waits for them, and re-layouts  16.1 us

profile of v2, /device:TPU:1, one launch (start us, length us, event | category | flops | bytes accessed | tf_op | source)
XLA Modules:
  0.0 191.4 jit_solution(3429676411769912762)
XLA Ops:
  0.7 1.2 reshape.49.refs_2_
  1.9 1.4 copy.47.refs_3_.refs_22_
  3.3 0.7 copy-done.26
  4.0 0.0 copy-start.1
  4.0 0.0 copy-start.2
  4.1 0.0 copy-start.3
  4.1 0.0 copy-start.8
  4.1 0.0 copy-start.15
  4.1 0.0 copy-start.18
  4.1 0.0 copy-start.19
  4.1 0.0 copy-start.20
  4.1 0.0 copy-start.21
  4.1 171.3 %whole_step.1 = (bf16[160,512]{1,0:T(8,128)(2,1)}, f32[160,512]{1,0:T(8,128)}, bf16[2,2,16,768]{3,2,1,0:T(8,128)(2,1)}, bf16[2,2,16,1024]{3,2,1,0:T(8,128)(2,1)}...) custom-call(bf16[160,512]{1,0:T(8,128)(2,1)} %refs_0_.1, bf16[160,512]{1,0:T(8,128)(2,1)} %refs_1_.1, ...), custom_call_target="tpu_custom_call" | custom-call | tf_op jit(solution)/shard_map/whole_step/pallas_call | solution.py:1402
  175.5 0.0 copy-start.17
  175.6 0.6 copy-done.17
  176.2 0.9 copy-done.4
  177.1 0.9 copy-done.5
  178.1 0.9 copy-done.6
  179.0 0.9 copy-done.7
  180.0 0.9 copy-done.9
  180.9 0.9 copy-done.10
  181.8 0.9 copy-done.11
  182.8 0.9 copy-done.12
  183.7 0.9 copy-done.13
  184.6 0.9 copy-done.14
  185.5 0.8 copy-done.16
  186.3 1.8 update_all.1
  188.1 0.6 copy.51
  188.8 0.6 copy.52
  189.4 0.6 copy.53
  190.0 0.7 copy.56
  190.7 0.7 copy.57
  (33 shorter events, 0.1 us)
Async XLA Ops:
  1.9 1.4 copy-start.25
  3.3 0.7 copy-start.26
  4.0 171.5 %copy-start = (f32[2,16,2048]{2,1,0:T(8,128)S(1)}, f32[2,16,2048]{2,1,0:T(8,128)}, u32[]{:S(2)}) copy-start(f32[2,16,2048]{2,1,0:T(8,128)} %refs_10_.1) | copy-start | bytes 786436
  4.0 171.5 %copy-start.1 = (f32[2,64,512]{2,1,0:T(8,128)S(1)}, f32[2,64,512]{2,1,0:T(8,128)}, u32[]{:S(2)}) copy-start(f32[2,64,512]{2,1,0:T(8,128)} %refs_13_.1) | copy-start | bytes 786436
  4.0 171.5 %copy-start.2 = (f32[2,16,1536]{2,1,0:T(8,128)S(1)}, f32[2,16,1536]{2,1,0:T(8,128)}, u32[]{:S(2)}) copy-start(f32[2,16,1536]{2,1,0:T(8,128)} %refs_4_.3) | copy-start | bytes 589828
  4.1 171.5 %copy-start.3 = (f32[2,6,512]{2,1,0:T(8,128)S(1)}, f32[2,6,512]{2,1,0:T(8,128)}, u32[]{:S(2)}) copy-start(f32[2,6,512]{2,1,0:T(8,128)} %copy.47.refs_3_.refs_22_) | copy-start | bytes 73732
  4.1 171.5 %copy-start.8 = (f32[2,16,512]{2,1,0:T(8,128)S(1)}, f32[2,16,512]{2,1,0:T(8,128)}, u32[]{:S(2)}) copy-start(f32[2,16,512]{2,1,0:T(8,128)} %refs_7_.3) | copy-start | bytes 196612
  4.1 171.5 %copy-start.15 = (f32[2,16,512]{2,1,0:T(8,128)S(1)}, f32[2,16,512]{2,1,0:T(8,128)}, u32[]{:S(2)}) copy-start(f32[2,16,512]{2,1,0:T(8,128)} %refs_8_.3) | copy-start | bytes 196612
  4.1 171.5 %copy-start.18 = (f32[2,32]{1,0:T(2,128)S(1)}, f32[2,32]{1,0:T(2,128)}, u32[]{:S(2)}) copy-start(f32[2,32]{1,0:T(2,128)} %refs_19_.1) | copy-start | bytes 772
  4.1 171.5 %copy-start.19 = (f32[2,24]{1,0:T(2,128)S(1)}, f32[2,24]{1,0:T(2,128)}, u32[]{:S(2)}) copy-start(f32[2,24]{1,0:T(2,128)} %refs_17_.1) | copy-start | bytes 580
  4.1 171.5 %copy-start.20 = (f32[2,24]{1,0:T(2,128)S(1)}, f32[2,24]{1,0:T(2,128)}, u32[]{:S(2)}) copy-start(f32[2,24]{1,0:T(2,128)} %refs_18_.1) | copy-start | bytes 580
  4.1 171.5 %copy-start.21 = (f32[2,32]{1,0:T(2,128)S(1)}, f32[2,32]{1,0:T(2,128)}, u32[]{:S(2)}) copy-start(f32[2,32]{1,0:T(2,128)} %refs_20_.1) | copy-start | bytes 772
  4.1 171.5 %copy-start.22 = (f32[2,32]{1,0:T(2,128)S(1)}, f32[2,32]{1,0:T(2,128)}, u32[]{:S(2)}) copy-start(f32[2,32]{1,0:T(2,128)} %refs_21_.1) | copy-start | bytes 772
  175.5 0.7 copy-start.17
  176.2 0.9 copy-start.4
  177.1 0.9 copy-start.5
  178.1 0.9 copy-start.6
  179.0 0.9 copy-start.7
  180.0 0.9 copy-start.9
  180.9 0.9 copy-start.10
  181.8 0.9 copy-start.11
  182.8 0.9 copy-start.12
  183.7 0.9 copy-start.13
  184.6 0.9 copy-start.14
  185.5 0.8 copy-start.16
  186.3 3.7 %copy-start.24 = (bf16[160,512]{1,0:T(8,128)(2,1)S(1)}, bf16[160,512]{1,0:T(8,128)(2,1)}, u32[]{:S(2)}) copy-start(bf16[160,512]{1,0:T(8,128)(2,1)} %get-tuple-element.123) | copy-start | bytes 491524
  188.1 2.6 %copy-start.23 = (f32[160,512]{1,0:T(8,128)S(1)}, f32[160,512]{1,0:T(8,128)}, u32[]{:S(2)}) copy-start(f32[160,512]{1,0:T(8,128)} %get-tuple-element.124) | copy-start | bytes 983044

commit v3 on v2

--- a/solution.py
+++ b/solution.py
@@ -161,6 +161,28 @@
             copy.wait_send()
 
 
+class DirectGather:
+    def __init__(self, copies, ring, views, sources):
+        self.copies, self.ring, self.views, self.sources = copies, ring, views, sources
+        self.sent = []
+
+    def start(self):
+        for step in range(1, self.ring.length):
+            for view, source in zip(self.views, self.sources):
+                own = view(self.ring.place, None)
+                copy = self.copies.to(source, own, self.ring.device(step))
+                copy.start()
+                self.sent.append(copy)
+
+    def end(self):
+        for copy in self.sent:
+            copy.wait_recv()
+
+    def finish(self):
+        for copy in self.sent:
+            copy.wait_send()
+
+
 class Summand:
     def __init__(self, ref, index, count, width, near, far):
         self.ref, self.index, self.count, self.width = ref, index, count, width
@@ -227,6 +249,33 @@
 
     def finish(self):
         for copy in self.near[0] + self.near[1] + self.far[0] + self.far[1]:
+            copy.wait_send()
+
+
+class DirectSum:
+    def __init__(self, copies, ring, summand):
+        self.copies, self.ring, self.summand = copies, ring, summand
+        self.sent = []
+
+    def start(self):
+        for step in range(1, self.ring.length):
+            copy = self.copies.to(
+                self.summand.view(self.ring.at(step), 0, self.summand.width),
+                self.summand.far[step - 1],
+                self.ring.device(step),
+            )
+            copy.start()
+            self.sent.append(copy)
+
+    def end(self):
+        for copy in self.sent:
+            copy.wait_recv()
+
+    def total(self):
+        return self.summand.total(None, self.ring.place, self.ring.length - 1)
+
+    def finish(self):
+        for copy in self.sent:
             copy.wait_send()
 
 
@@ -316,7 +365,7 @@
                         sources[k], view(rings[order][0].place, None), local.at[order * 2 + k]
                     )
                 )
-            self.first.append(RingGather(copies, rings[order][0], chunks, sources))
+            self.first.append(DirectGather(copies, rings[order][0], chunks, sources))
             self.second.append(
                 RingGather(copies, rings[order][1], lines, None, partial(self.forward, order))
             )
@@ -334,10 +383,6 @@
             ring.start()
         for copy in self.own:
             copy.start()
-
-    def first_middle(self):
-        for ring in self.first:
-            ring.middle()
 
     def turn(self):
         for copy in self.own:
@@ -588,7 +633,7 @@
 class GradSum:
     def __init__(self, here, cut, copies, kind, g, s, buffers):
         self.here, self.copies, self.kind, self.g, self.s = here, copies, kind, g, s
-        self.near, self.far, self.mid, self.near_two, self.far_two, self.fin = buffers
+        self.near, self.far, self.mid, self.top, self.fin = buffers
         rows = g.shape[3]
         first = rows // 2 if kind == "a" else cut
         self.cuts = (pl.ds(0, first), pl.ds(first, rows - first))
@@ -684,18 +729,15 @@
             index,
             None,
             self.full if self.kind == "a" else self.lanes,
-            (self.near_two[order].at[0], self.near_two[order].at[1]),
-            (self.far_two[order].at[0], self.far_two[order].at[1]),
+            None,
+            [self.top[order].at[k] for k in range(ring.length - 1)],
         )
-        self.turns[order] = RingSum(self.copies, ring, [summand])
+        self.turns[order] = DirectSum(self.copies, ring, summand)
         self.turns[order].start()
-
-    def turn_middle(self, order):
-        self.turns[order].middle()
 
     def end(self, order):
         self.turns[order].end()
-        value = self.turns[order].total(0).astype(BF)
+        value = self.turns[order].total().astype(BF)
         if self.kind == "a":
             self.fin[order] = value
         else:
@@ -728,14 +770,13 @@
         *[low(2, counts[o], cuts[o], widths[o] // 2) for o in range(2)],
         *[low(2, counts[o], cuts[o], widths[o]) for o in range(2)],
         *[low(counts[o], cuts[o], widths[o]) for o in range(2)],
-        *[low(2, cuts[o], lanes // 2) for o in range(2)],
-        *[low(2, cuts[o], lanes) for o in range(2)],
+        *[low((nz, nx)[o] - 1, cuts[o], lanes) for o in range(2)],
         fin,
     ]
 
 
 def grad_sum(here, cut, copies, kind, g, refs):
-    s, near0, near1, far0, far1, mid0, mid1, low0, low1, top0, top1, fin = refs
+    s, near0, near1, far0, far1, mid0, mid1, top0, top1, fin = refs
     return GradSum(
         here,
         cut,
@@ -743,7 +784,7 @@
         kind,
         g,
         s,
-        ((near0, near1), (far0, far1), (mid0, mid1), (low0, low1), (top0, top1), fin),
+        ((near0, near1), (far0, far1), (mid0, mid1), (top0, top1), fin),
     )
 
 
@@ -848,7 +889,9 @@
     vec_own, wc = at.vec_own, at.wc
     vec_own[...] = jnp.zeros(vec_own.shape, F32)
     for layer in range(LAYERS):
-        vec_own[layer * VEC_ROWS : layer * VEC_ROWS + 6] = at.row_vectors[layer]
+        for k in range(6):
+            row = layer * VEC_ROWS + k
+            vec_own[row : row + 1] = at.row_vectors[k, layer : layer + 1]
     wc[...] = jnp.zeros(wc.shape, F32)
     wc[:LAYERS, : widths[0]] = at.qkv_bias[...]
     wc[:LAYERS, widths[0] : sum(widths)] = at.up_bias[...]
@@ -964,11 +1007,7 @@
     near[1].start()
     complete_b(0)
     near[2].start()
-    cast(1)
-    begin(1)
-    near[0].first_middle()
-    for copy in hid_copies + own:
-        copy.wait()
+    make_tables(at.ids, at.live, *tables, mask)
     layers = [
         Layer(k, vec, tables, mask, bias.at[pl.ds(2 * k, 2)], *full[k], sizes)
         for k in range(LAYERS)
@@ -976,20 +1015,22 @@
     attn_in, mlp_in, joined, probs = at.attn_in, at.mlp_in, at.joined, at.probs
     heads, slope, units = at.heads, at.slope, at.units
     near[0].turn()
-    near[1].first_middle()
-    near[2].first_middle()
-    make_tables(at.ids, at.live, *tables, mask)
+    for copy in hid_copies + own:
+        copy.wait()
+    near[0].second_middle()
     near[1].turn()
-    near[0].second_middle()
-    near[2].turn()
+    hat, _ = norm_stats(hid_all[...].astype(F32))
+    layers[0].inputs(hat, attn_in[0], mlp_in[0])
     near[0].end()
     near[1].second_middle()
-    hat, _ = norm_stats(hid_all[...].astype(F32))
-    layers[0].inputs(hat, attn_in[0], mlp_in[0])
+    near[2].turn()
+    cast(1)
+    begin(1)
     near[0].arrive()
+    make_biases(full_c, bias, widths)
+    layers[0].project(attn_in[0], joined[0])
     near[1].end()
     near[2].second_middle()
-    make_biases(full_c, bias, widths)
     complete_a(1, 0)
     late[0].start()
     complete_a(1, 1)
@@ -999,17 +1040,13 @@
     for copy in cot_copies:
         copy.start()
     mine = own_rows(here, quarter)
-    layers[0].project(attn_in[0], joined[0])
+    layers[0].attend(joined[0], probs[0], heads[0])
     near[2].end()
-    for one in late:
-        one.first_middle()
-    layers[0].attend(joined[0], probs[0], heads[0])
-    for one in late:
-        one.turn()
     near[1].arrive()
+    late[0].turn()
     layers[0].units(mlp_in[0], slope[0], units[0])
-    for one in late[:2]:
-        one.second_middle()
+    late[0].second_middle()
+    late[1].turn()
     near[2].arrive()
     part = at.part[0]
     for start in (0, D // 2):
@@ -1018,7 +1055,8 @@
         )
     summed = group_sum(here, copies, part, rows_index(quarter), D, at.near[0], at.far[0])
     summed.start()
-    late[2].second_middle()
+    late[1].second_middle()
+    late[2].turn()
     summed.middle()
     state = hid_all[mine, :].astype(F32) + layers[0].vector(4) + layers[0].vector(5)
     summed.end()
@@ -1037,6 +1075,7 @@
         cot_all[...].astype(F32) * at.live[:, :1]
     ).astype(BF)
     spread.middle()
+    late[2].second_middle()
     for one in late:
         one.end()
     spread.end()
@@ -1045,38 +1084,6 @@
     for one in gathers:
         one.finish()
     rings = [summed, spread]
-
-    layer = layers[1]
-    layer.inputs(hat_all[...].astype(F32), attn_in[1], mlp_in[1])
-    layer.project(attn_in[1], joined[1])
-    layer.attend(joined[1], probs[1], heads[1])
-    layer.units(mlp_in[1], slope[1], units[1])
-    part = at.part[1]
-    for start in (0, D // 2):
-        part[:, start : start + D // 2] = (
-            layer.outputs(heads[1], units[1], start, D // 2).astype(BF)
-        )
-    part[mine, :] = (part[mine, :].astype(F32) + at.state[...]).astype(BF)
-    out_sum = group_sum(
-        here, copies, part, blocks_index(rows, lanes), lanes, at.near[1], at.far[1]
-    )
-    out_sum.start()
-    grad_heads, grad_pre, raw, grad_joined = (
-        at.grad_heads,
-        at.grad_pre,
-        at.raw,
-        at.grad_joined,
-    )
-    sums = (at.sums[0], at.sums[1])
-    layer.branch_back(grad[1], slope[1], grad_heads, grad_pre)
-    out_sum.middle()
-    layer.attend_back(joined[1], probs[1], grad_heads, raw, grad_joined)
-    back = at.back[1]
-    back[...] = layer.inputs_back(
-        grad_joined, grad_pre, hat_all[...].astype(F32), grad[1], sums[1]
-    ).astype(BF)
-    summed = group_sum(here, copies, back, rows_index(quarter), D, at.near[2], at.far[2])
-    summed.start()
 
     grads = [
         full[1],
@@ -1153,14 +1160,44 @@
             for one in which:
                 step(one, order)
 
+    layer = layers[1]
+    layer.inputs(hat_all[...].astype(F32), attn_in[1], mlp_in[1])
+    layer.project(attn_in[1], joined[1])
+    layer.attend(joined[1], probs[1], heads[1])
+    layer.units(mlp_in[1], slope[1], units[1])
+    b_high = at.gb.shape[3]
+    grads_b(heads[1], grad[1], grads[1][2], 0, out_rows)
+    grads_b(units[1], grad[1], grads[1][2], out_rows, b_high)
+    sum_b[1].start()
+    part = at.part[1]
+    for start in (0, D // 2):
+        part[:, start : start + D // 2] = (
+            layer.outputs(heads[1], units[1], start, D // 2).astype(BF)
+        )
+    part[mine, :] = (part[mine, :].astype(F32) + at.state[...]).astype(BF)
+    out_sum = group_sum(
+        here, copies, part, blocks_index(rows, lanes), lanes, at.near[1], at.far[1]
+    )
+    out_sum.start()
+    grad_heads, grad_pre, raw, grad_joined = at.grad_heads, at.grad_pre, at.raw, at.grad_joined
+    sums = at.sums
+    layer.branch_back(grad[1], slope[1], grad_heads, grad_pre)
+    phase(GradSum.line, [sum_b[1]])
+    layer.attend_back(joined[1], probs[1], grad_heads, raw, grad_joined)
+    phase(GradSum.line_middle, [sum_b[1]])
+    back = at.back[1]
+    back[...] = layer.inputs_back(
+        grad_joined, grad_pre, hat_all[...].astype(F32), grad[1], sums[1]
+    ).astype(BF)
+    summed = group_sum(here, copies, back, rows_index(quarter), D, at.near[2], at.far[2])
+    summed.start()
     grads_a(mlp_in[1], grad_pre, grads[1][1])
     sum_u[1].start()
     summed.middle()
     grads_a(attn_in[1], grad_joined, grads[1][0])
     sum_q[1].start()
-    out_sum.end()
-    bias_sum = vec[VEC_ROWS + 4 : VEC_ROWS + 5, features] + vec[VEC_ROWS + 5 : VEC_ROWS + 6, features]
-    at.hidden[...] = (out_sum.total(0) + bias_sum).astype(BF)
+    out_sum.middle()
+    phase(GradSum.turn, [sum_b[1]])
     summed.end()
     grad_one = at.grad_one
     total = grad[1][mine, :].astype(F32) + inv_std[:, :1] * summed.total(0)
@@ -1168,32 +1205,42 @@
     grad[0][mine, :] = total.astype(BF)
     spread = group_gather(here, copies, grad[0], quarter)
     spread.start()
-    grads_b(heads[1], grad[1], grads[1][2], 0, out_rows)
-    grads_b(units[1], grad[1], grads[1][2], out_rows, at.gb.shape[3])
-    sum_b[1].start()
+    phase(GradSum.line, [sum_u[1]])
     spread.middle()
-    phase(GradSum.line, [sum_u[1], sum_q[1]])
+    phase(GradSum.line, [sum_q[1]])
+    out_sum.end()
+    first_bias = vec[VEC_ROWS + 4 : VEC_ROWS + 5, features]
+    bias_sum = first_bias + vec[VEC_ROWS + 5 : VEC_ROWS + 6, features]
+    at.hidden[...] = (out_sum.total(0) + bias_sum).astype(BF)
+    phase(GradSum.line_middle, [sum_u[1]])
     spread.end()
     rings += [out_sum, summed, spread]
 
+    def conclude(layer_index, one, kind):
+        for order in range(2):
+            one.end(order)
+        if kind == 2:
+            hand_b(layer_index)
+        else:
+            hand_a(layer_index, kind)
+
     layer = layers[0]
     grads_b(heads[0], grad[0], grads[0][2], 0, out_rows)
-    grads_b(units[0], grad[0], grads[0][2], out_rows, at.gb.shape[3])
+    grads_b(units[0], grad[0], grads[0][2], out_rows, b_high)
     sum_b[0].start()
-    phase(GradSum.line, [sum_b[1]])
-    phase(GradSum.line_middle, [sum_u[1], sum_q[1]])
+    phase(GradSum.line_middle, [sum_q[1]])
     layer.branch_back(grad[0], slope[0], grad_heads, grad_pre)
-    phase(GradSum.line_middle, [sum_b[1]])
+    conclude(1, sum_b[1], 2)
+    phase(GradSum.turn, [sum_u[1]])
+    phase(GradSum.line, [sum_b[0]])
     grads_a(mlp_in[0], grad_pre, grads[0][1])
     sum_u[0].start()
-    phase(GradSum.turn, [sum_u[1], sum_q[1]])
+    phase(GradSum.turn, [sum_q[1]])
     layer.attend_back(joined[0], probs[0], grad_heads, raw, grad_joined)
-    phase(GradSum.turn, [sum_b[1]])
-    phase(GradSum.line, [sum_b[0]])
+    phase(GradSum.line_middle, [sum_b[0]])
     grads_a(attn_in[0], grad_joined, grads[0][0])
     sum_q[0].start()
     phase(GradSum.line, [sum_u[0]])
-    phase(GradSum.turn_middle, [sum_u[1], sum_q[1], sum_b[1]])
     hat, inverse = norm_stats(hid_all[...].astype(F32))
     value = layer.inputs_back(grad_joined, grad_pre, hat, grad[0], sums[0])
     back = at.back[0]
@@ -1203,9 +1250,7 @@
         here, copies, back, blocks_index(rows, lanes), lanes, at.near[3], at.far[3]
     )
     summed.start()
-    phase(GradSum.line_middle, [sum_b[0]])
     phase(GradSum.line, [sum_q[0]])
-    phase(GradSum.line_middle, [sum_u[0]])
     v_core, v_line, v_last, v_group = at.v_core, at.v_line, at.v_last, at.v_group
     v_lanes = D // 2
     v_mine = pl.ds(pl.multiple_of(here.core * v_lanes, v_lanes), v_lanes)
@@ -1213,13 +1258,11 @@
     v_copies = [copies.to(sums[k].at[:, v_other], v_core.at[k], here.partner) for k in range(2)]
     for copy in v_copies:
         copy.start()
+    phase(GradSum.line_middle, [sum_u[0]])
     summed.middle()
-    for order in range(2):
-        for one in (sum_q[1], sum_u[1], sum_b[1]):
-            one.end(order)
-    hand_a(1, 0)
-    hand_a(1, 1)
-    hand_b(1)
+    conclude(1, sum_u[1], 1)
+    conclude(1, sum_q[1], 0)
+    phase(GradSum.turn, [sum_b[0]])
     for copy in v_copies:
         copy.wait()
     for k in range(LAYERS):
@@ -1231,7 +1274,7 @@
     for copy in v_x:
         copy.start()
     phase(GradSum.line_middle, [sum_q[0]])
-    phase(GradSum.turn, [sum_b[0], sum_u[0]])
+    phase(GradSum.turn, [sum_u[0]])
     summed.end()
     at.grad_out[...] = summed.total(0)
     rings.append(summed)
@@ -1247,8 +1290,8 @@
     ]
     for copy in v_z:
         copy.start()
-    phase(GradSum.turn_middle, [sum_b[0], sum_u[0]])
     phase(GradSum.turn, [sum_q[0]])
+    conclude(0, sum_b[0], 2)
     for copy in v_z:
         copy.wait()
     total = v_last[0]
@@ -1261,12 +1304,8 @@
     ]
     for copy in v_y:
         copy.start()
-    phase(GradSum.turn_middle, [sum_q[0]])
-    for order in range(2):
-        sum_b[0].end(order)
-        sum_u[0].end(order)
-    hand_b(0)
-    hand_a(0, 1)
+    conclude(0, sum_u[0], 1)
+    conclude(0, sum_q[0], 0)
     for copy in v_y:
         copy.wait()
     total = v_group[0]
@@ -1277,9 +1316,6 @@
     out_v[1, :, v_mine] = v_group[here.place]
     v_swap = copies.to(out_v.at[:, :, v_mine], out_v.at[:, :, v_mine], here.partner)
     v_swap.start()
-    for order in range(2):
-        sum_q[0].end(order)
-    hand_a(0, 0)
     v_swap.wait()
     handed(1)
     handed(0)
@@ -1410,67 +1446,95 @@
     )(*ins.values())
 
 
-def update_kernel(n_dp, bias_widths, out_rows, *refs):
-    own_q, own_u, own_b, all_v = refs[:4]
-    old, new = refs[4:25], refs[25:]
+def update_kernel(n_dp, bias_widths, out_rows, whole_count, *refs):
+    passed, refs = refs[:whole_count], refs[whole_count:]
+    given, refs = refs[:25], refs[25:]
+    passed_out, refs = refs[:whole_count], refs[whole_count:]
+    results, refs = refs[:21], refs[21:]
+    held, made, in_sems, out_sems = refs[:25], refs[25:46], refs[46], refs[47]
     d, r = lax.axis_index("dp"), lax.axis_index("row")
-
-    def update(k, gradient, rate, decay):
-        values = adamw(*[ref[...] for ref in old[3 * k : 3 * k + 3]], gradient, rate, decay)
-        for ref, value in zip(new[3 * k : 3 * k + 3], values):
-            ref[...] = value
+    loads = [
+        pltpu.make_async_copy(src, dst, in_sems.at[k])
+        for k, (src, dst) in enumerate(zip(given, held))
+    ]
+    stores = [
+        pltpu.make_async_copy(src, dst, out_sems.at[k])
+        for k, (src, dst) in enumerate(zip(made + passed, results + passed_out))
+    ]
+    for copy in loads:
+        copy.start()
+    for copy in stores[21:]:
+        copy.start()
+    own_q, own_u, own_b, all_v = held[:4]
+    old = held[4:]
+    for copy in loads[:4]:
+        copy.wait()
+
+    def update(k, at, gradient, rate, decay):
+        values = adamw(*[ref[at] for ref in old[3 * k : 3 * k + 3]], gradient, rate, decay)
+        for ref, value in zip(made[3 * k : 3 * k + 3], values):
+            ref[at] = value
+
+    def begin(k):
+        for copy in loads[4 + 3 * k : 7 + 3 * k]:
+            copy.wait()
+
+    def finish(k):
+        for copy in stores[3 * k : 3 * k + 3]:
+            copy.start()
 
     for k, own in ((0, own_q), (2, own_u)):
+        begin(k)
         width = own.shape[3]
         for layer in range(LAYERS):
             for side in range(2):
                 at = (layer, slice(None), slice(side * width, (side + 1) * width))
-                gradient = own[layer, side].astype(F32)
-                values = adamw(
-                    *[ref[at] for ref in old[3 * k : 3 * k + 3]], gradient, RATE_MATRIX, DECAY_MATRIX
-                )
-                for ref, value in zip(new[3 * k : 3 * k + 3], values):
-                    ref[at] = value
-    update(1, own_b[:, :out_rows].astype(F32), RATE_MATRIX, DECAY_MATRIX)
-    update(3, own_b[:, out_rows:].astype(F32), RATE_MATRIX, DECAY_MATRIX)
+                update(k, at, own[layer, side].astype(F32), RATE_MATRIX, DECAY_MATRIX)
+        finish(k)
+    for k, rows in ((1, slice(0, out_rows)), (3, slice(out_rows, None))):
+        begin(k)
+        update(k, ..., own_b[:, rows].astype(F32), RATE_MATRIX, DECAY_MATRIX)
+        finish(k)
     for k, width in enumerate(bias_widths):
+        begin(4 + k)
         for layer in range(LAYERS):
             rows = all_v[1, layer * VEC_ROWS : (layer + 1) * VEC_ROWS, :]
             moved = pltpu.roll(rows, lax.rem(D - d * width, D), 1)
             at = (slice(layer, layer + 1), slice(None))
-            values = adamw(
-                *[ref[at] for ref in old[12 + 3 * k : 15 + 3 * k]],
-                moved[5 + k : 6 + k, :width],
-                RATE_MATRIX,
-                0.0,
-            )
-            for ref, value in zip(new[12 + 3 * k : 15 + 3 * k], values):
-                ref[at] = value
+            update(4 + k, at, moved[5 + k : 6 + k, :width], RATE_MATRIX, 0.0)
+        finish(4 + k)
     lanes = old[18].shape[2]
     features = pl.ds(pl.multiple_of(r * lanes, lanes), lanes)
+    begin(6)
     for layer in range(LAYERS):
         for k in range(6):
             row = layer * VEC_ROWS + min(k, 4)
-            at = (layer, slice(k, k + 1), slice(None))
-            values = adamw(
-                *[ref[at] for ref in old[18:21]],
-                all_v[0, row : row + 1, features],
-                RATE_VECTOR,
-                0.0,
-            )
-            for ref, value in zip(new[18:21], values):
-                ref[at] = value
-
-
-def update_all(n_dp, bias_widths, out_rows, gradients, old):
+            at = (k, slice(layer, layer + 1), slice(None))
+            update(6, at, all_v[0, row : row + 1, features], RATE_VECTOR, 0.0)
+    finish(6)
+    for copy in stores:
+        copy.wait()
+
+
+def update_all(n_dp, bias_widths, out_rows, passed, gradients, old):
+    anywhere = pl.BlockSpec(memory_space=pl.ANY)
+    given = (*gradients, *old)
+    results = [jax.ShapeDtypeStruct(a.shape, F32) for a in old]
+    count = len(passed)
     return pl.pallas_call(
-        partial(update_kernel, n_dp, bias_widths, out_rows),
-        out_shape=tuple(jax.ShapeDtypeStruct(a.shape, F32) for a in old),
-        in_specs=[VMEM_SPEC] * (4 + len(old)),
-        out_specs=(VMEM_SPEC,) * len(old),
-        compiler_params=pltpu.CompilerParams(vmem_limit_bytes=32 << 20),
+        partial(update_kernel, n_dp, bias_widths, out_rows, count),
+        out_shape=(*[jax.ShapeDtypeStruct(a.shape, a.dtype) for a in passed], *results),
+        in_specs=[anywhere] * (count + len(given)),
+        out_specs=(anywhere,) * (count + len(old)),
+        scratch_shapes=[
+            *[pltpu.VMEM(a.shape, a.dtype) for a in given],
+            *[pltpu.VMEM(a.shape, F32) for a in old],
+            pltpu.SemaphoreType.DMA((len(given),)),
+            pltpu.SemaphoreType.DMA((count + len(old),)),
+        ],
+        compiler_params=pltpu.CompilerParams(vmem_limit_bytes=60 << 20),
         name="update_all",
-    )(*gradients, *old)
+    )(*passed, *given)
 
 
 def on_device(
@@ -1512,7 +1576,7 @@
         hid=hidden_in,
         cot=cotangent,
         ids=seq_ids.reshape(1, group_len),
-        row_vectors=row_vectors,
+        row_vectors=row_vectors.transpose(1, 0, 2),
         qkv_bias=qkv_bias,
         up_bias=up_bias,
         qkv_weight=qkv_weight,
@@ -1520,7 +1584,8 @@
         up_weight=up_weight,
         down_weight=down_weight,
     )
-    hidden_out, grad_state, *gradients = whole(grid, cut, sizes, bias_widths, ins)
+    *passed, own_q, own_u, own_b, all_v = whole(grid, cut, sizes, bias_widths, ins)
+    gradients = (own_q, own_u, own_b, all_v)
     old = (
         qkv_weight,
         qkv_first,
@@ -1540,11 +1605,14 @@
         up_bias,
         up_bias_first,
         up_bias_second,
-        row_vectors,
-        row_first,
-        row_second,
+        row_vectors.transpose(1, 0, 2),
+        row_first.transpose(1, 0, 2),
+        row_second.transpose(1, 0, 2),
     )
-    return hidden_out, grad_state, *update_all(n_dp, bias_widths, out_rows, gradients, old)
+    *new, row_new, row_one, row_two = update_all(
+        n_dp, bias_widths, out_rows, passed, gradients, old
+    )
+    return *new, *[a.transpose(1, 0, 2) for a in (row_new, row_one, row_two)]
 
 
 def solution(mesh):

time: 192 us -> 181 us (0.943)
  local copies, waits for them, and re-layouts: 17.4 us -> 1.24 us
  Pallas kernels: 173 us -> 178 us
    unnamed x62 -> x2, local copies, waits for them, and re-layouts: 16.1 us -> 0.67 us
    pallas_call x1, Pallas kernels: 1.82 us -> 16.6 us  [update_all(): pl.pallas_call(partial(update_kernel, n_dp, bias_widths, out_rows, count)...]
    pallas_call x1, Pallas kernels: 171 us -> 162 us  [whole(): pl.pallas_call(kernel, out_shape=tuple(outs.values()), in_specs=[VMEM_SPE...]
where the time goes in v3:
time: 181 us; the launch traced here: 180 us
  Pallas kernels  178 us (98%)
    pallas_call x1, Pallas kernels, whole(): pl.pallas_call(kernel, out_shape=tuple(outs.values()), in_specs=[VMEM_SPE...  162 us
    pallas_call x1, Pallas kernels, update_all(): pl.pallas_call(partial(update_kernel, n_dp, bias_widths, out_rows, count)...  16.6 us

profile of v3, /device:TPU:1, one launch (start us, length us, event | category | flops | bytes accessed | tf_op | source)
XLA Modules:
  0.0 180.5 jit_solution(14130719687382608578)
XLA Ops:
  0.7 0.0 copy-start
  0.7 0.7 copy-done
  1.3 0.6 reshape.49.refs_2_
  1.9 161.8 %whole_step.1 = (bf16[160,512]{1,0:T(8,128)(2,1)}, f32[160,512]{1,0:T(8,128)}, bf16[2,2,16,768]{3,2,1,0:T(8,128)(2,1)}, bf16[2,2,16,1024]{3,2,1,0:T(8,128)(2,1)}...) custom-call(bf16[160,512]{1,0:T(8,128)(2,1)} %refs_0_.1, bf16[160,512]{1,0:T(8,128)(2,1)} %refs_1_.1, ...), custom_call_target="tpu_custom_call" | custom-call | tf_op jit(solution)/shard_map/whole_step/pallas_call | solution.py:1438
  163.7 16.6 %update_all.1 = (bf16[160,512]{1,0:T(8,128)(2,1)}, f32[160,512]{1,0:T(8,128)}, f32[2,16,1536]{2,1,0:T(8,128)}, f32[2,16,1536]{2,1,0:T(8,128)}, f32[2,16,1536]{2,...) custom-call(bf16[160,512]{1,0:T(8,128)(2,1)} %get-tuple-element.52.r, ...), custom_call_target="tpu_custom_call" | custom-call | tf_op jit(solution)/shard_map/update_all/pallas_call | solution.py:1524
Async XLA Ops:
  0.7 0.7 copy-start

commit v4 on v3

--- a/solution.py
+++ b/solution.py
@@ -195,7 +195,7 @@
         def one(lead):
             at = self.index(lead, target, start, width)
             more = other[...] if self.count is None else other[lead]
-            self.ref[at] = (self.ref[at].astype(F32) + more.astype(F32)).astype(BF)
+            self.ref[at] = self.ref[at] + more
 
         if self.count is None:
             one(None)
@@ -656,12 +656,8 @@
         here, at, zls = self.here, self.cuts[order], self.here.zls
         self.core[order].wait_recv()
 
-        def add(zz, xx):
-            self.s[zz, xx, at] = (
-                self.s[zz, xx, at].astype(F32) + self.g[zz, xx, here.core, at].astype(F32)
-            ).astype(BF)
-
-        over(self.s.shape[:2], add)
+        for zz in range(self.s.shape[0]):
+            self.s[zz, :, at] = self.s[zz, :, at] + self.g[zz, :, here.core, at]
         nx = self.s.shape[1]
         if order == 0:
             ring, count, width = here.x_ring, self.s.shape[0], self.full
@@ -1014,23 +1010,22 @@
     ]
     attn_in, mlp_in, joined, probs = at.attn_in, at.mlp_in, at.joined, at.probs
     heads, slope, units = at.heads, at.slope, at.units
-    near[0].turn()
+    for one in near:
+        one.turn()
     for copy in hid_copies + own:
         copy.wait()
     near[0].second_middle()
-    near[1].turn()
     hat, _ = norm_stats(hid_all[...].astype(F32))
     layers[0].inputs(hat, attn_in[0], mlp_in[0])
-    near[0].end()
     near[1].second_middle()
-    near[2].turn()
+    near[2].second_middle()
     cast(1)
     begin(1)
+    for one in near:
+        one.end()
     near[0].arrive()
     make_biases(full_c, bias, widths)
     layers[0].project(attn_in[0], joined[0])
-    near[1].end()
-    near[2].second_middle()
     complete_a(1, 0)
     late[0].start()
     complete_a(1, 1)
@@ -1041,12 +1036,10 @@
         copy.start()
     mine = own_rows(here, quarter)
     layers[0].attend(joined[0], probs[0], heads[0])
-    near[2].end()
+    for one in late:
+        one.turn()
     near[1].arrive()
-    late[0].turn()
     layers[0].units(mlp_in[0], slope[0], units[0])
-    late[0].second_middle()
-    late[1].turn()
     near[2].arrive()
     part = at.part[0]
     for start in (0, D // 2):
@@ -1055,9 +1048,9 @@
         )
     summed = group_sum(here, copies, part, rows_index(quarter), D, at.near[0], at.far[0])
     summed.start()
+    late[0].second_middle()
+    summed.middle()
     late[1].second_middle()
-    late[2].turn()
-    summed.middle()
     state = hid_all[mine, :].astype(F32) + layers[0].vector(4) + layers[0].vector(5)
     summed.end()
     state = state + summed.total(0)
@@ -1074,15 +1067,12 @@
     grad[1][...] = (
         cot_all[...].astype(F32) * at.live[:, :1]
     ).astype(BF)
+    late[2].second_middle()
     spread.middle()
-    late[2].second_middle()
     for one in late:
         one.end()
     spread.end()
-    for one in late:
-        one.arrive()
-    for one in gathers:
-        one.finish()
+    late[0].arrive()
     rings = [summed, spread]
 
     grads = [
@@ -1164,7 +1154,11 @@
     layer.inputs(hat_all[...].astype(F32), attn_in[1], mlp_in[1])
     layer.project(attn_in[1], joined[1])
     layer.attend(joined[1], probs[1], heads[1])
+    late[1].arrive()
     layer.units(mlp_in[1], slope[1], units[1])
+    late[2].arrive()
+    for one in gathers:
+        one.finish()
     b_high = at.gb.shape[3]
     grads_b(heads[1], grad[1], grads[1][2], 0, out_rows)
     grads_b(units[1], grad[1], grads[1][2], out_rows, b_high)
@@ -1185,6 +1179,7 @@
     phase(GradSum.line, [sum_b[1]])
     layer.attend_back(joined[1], probs[1], grad_heads, raw, grad_joined)
     phase(GradSum.line_middle, [sum_b[1]])
+    out_sum.middle()
     back = at.back[1]
     back[...] = layer.inputs_back(
         grad_joined, grad_pre, hat_all[...].astype(F32), grad[1], sums[1]
@@ -1196,8 +1191,6 @@
     summed.middle()
     grads_a(attn_in[1], grad_joined, grads[1][0])
     sum_q[1].start()
-    out_sum.middle()
-    phase(GradSum.turn, [sum_b[1]])
     summed.end()
     grad_one = at.grad_one
     total = grad[1][mine, :].astype(F32) + inv_std[:, :1] * summed.total(0)
@@ -1207,6 +1200,7 @@
     spread.start()
     phase(GradSum.line, [sum_u[1]])
     spread.middle()
+    phase(GradSum.turn, [sum_b[1]])
     phase(GradSum.line, [sum_q[1]])
     out_sum.end()
     first_bias = vec[VEC_ROWS + 4 : VEC_ROWS + 5, features]
@@ -1446,12 +1440,10 @@
     )(*ins.values())
 
 
-def update_kernel(n_dp, bias_widths, out_rows, whole_count, *refs):
-    passed, refs = refs[:whole_count], refs[whole_count:]
-    given, refs = refs[:25], refs[25:]
-    passed_out, refs = refs[:whole_count], refs[whole_count:]
-    results, refs = refs[:21], refs[21:]
-    held, made, in_sems, out_sems = refs[:25], refs[25:46], refs[46], refs[47]
+def update_kernel(n_dp, bias_widths, out_rows, *refs):
+    given, refs = refs[:27], refs[27:]
+    results, refs = refs[:23], refs[23:]
+    held, made, in_sems, out_sems = refs[:27], refs[27:48], refs[48], refs[49]
     d, r = lax.axis_index("dp"), lax.axis_index("row")
     loads = [
         pltpu.make_async_copy(src, dst, in_sems.at[k])
@@ -1459,14 +1451,12 @@
     ]
     stores = [
         pltpu.make_async_copy(src, dst, out_sems.at[k])
-        for k, (src, dst) in enumerate(zip(made + passed, results + passed_out))
+        for k, (src, dst) in enumerate(zip((*made, *held[25:]), results))
     ]
     for copy in loads:
         copy.start()
-    for copy in stores[21:]:
-        copy.start()
     own_q, own_u, own_b, all_v = held[:4]
-    old = held[4:]
+    old = held[4:25]
     for copy in loads[:4]:
         copy.wait()
 
@@ -1512,29 +1502,30 @@
             at = (k, slice(layer, layer + 1), slice(None))
             update(6, at, all_v[0, row : row + 1, features], RATE_VECTOR, 0.0)
     finish(6)
+    for load, store in zip(loads[25:], stores[21:]):
+        load.wait()
+        store.start()
     for copy in stores:
         copy.wait()
 
 
 def update_all(n_dp, bias_widths, out_rows, passed, gradients, old):
     anywhere = pl.BlockSpec(memory_space=pl.ANY)
-    given = (*gradients, *old)
-    results = [jax.ShapeDtypeStruct(a.shape, F32) for a in old]
-    count = len(passed)
+    given = (*gradients, *old, *passed)
     return pl.pallas_call(
-        partial(update_kernel, n_dp, bias_widths, out_rows, count),
-        out_shape=(*[jax.ShapeDtypeStruct(a.shape, a.dtype) for a in passed], *results),
-        in_specs=[anywhere] * (count + len(given)),
-        out_specs=(anywhere,) * (count + len(old)),
+        partial(update_kernel, n_dp, bias_widths, out_rows),
+        out_shape=tuple(jax.ShapeDtypeStruct(a.shape, a.dtype) for a in (*old, *passed)),
+        in_specs=[anywhere] * len(given),
+        out_specs=(anywhere,) * (len(old) + len(passed)),
         scratch_shapes=[
             *[pltpu.VMEM(a.shape, a.dtype) for a in given],
             *[pltpu.VMEM(a.shape, F32) for a in old],
             pltpu.SemaphoreType.DMA((len(given),)),
-            pltpu.SemaphoreType.DMA((count + len(old),)),
+            pltpu.SemaphoreType.DMA((len(old) + len(passed),)),
         ],
         compiler_params=pltpu.CompilerParams(vmem_limit_bytes=60 << 20),
         name="update_all",
-    )(*passed, *given)
+    )(*given)
 
 
 def on_device(
@@ -1609,10 +1600,11 @@
         row_first.transpose(1, 0, 2),
         row_second.transpose(1, 0, 2),
     )
-    *new, row_new, row_one, row_two = update_all(
+    *new, row_new, row_one, row_two, hidden_out, grad_state = update_all(
         n_dp, bias_widths, out_rows, passed, gradients, old
     )
-    return *new, *[a.transpose(1, 0, 2) for a in (row_new, row_one, row_two)]
+    rows = [a.transpose(1, 0, 2) for a in (row_new, row_one, row_two)]
+    return hidden_out, grad_state, *new, *rows
 
 
 def solution(mesh):

time: 181 us -> 165 us (0.912)
  Pallas kernels: 178 us -> 162 us
    pallas_call x1, Pallas kernels: 16.6 us -> 3.78 us  [update_all(): pl.pallas_call(partial(update_kernel, n_dp, bias_widths, out_rows), out_s...]
    pallas_call x1, Pallas kernels: 162 us -> 158 us  [whole(): pl.pallas_call(kernel, out_shape=tuple(outs.values()), in_specs=[VMEM_SPE...]
where the time goes in v4:
time: 165 us; the launch traced here: 164 us
  Pallas kernels  162 us (98%)
    pallas_call x1, Pallas kernels, whole(): pl.pallas_call(kernel, out_shape=tuple(outs.values()), in_specs=[VMEM_SPE...  158 us
    pallas_call x1, Pallas kernels, update_all(): pl.pallas_call(partial(update_kernel, n_dp, bias_widths, out_rows), out_s...  3.78 us

profile of v4, /device:TPU:1, one launch (start us, length us, event | category | flops | bytes accessed | tf_op | source)
XLA Modules:
  0.0 164.4 jit_solution(1345207942915397908)
XLA Ops:
  0.7 0.0 copy-start
  0.7 0.7 copy-done
  1.3 0.6 reshape.49.refs_2_
  1.9 158.5 %whole_step.1 = (bf16[160,512]{1,0:T(8,128)(2,1)}, f32[160,512]{1,0:T(8,128)}, bf16[2,2,16,768]{3,2,1,0:T(8,128)(2,1)}, bf16[2,2,16,1024]{3,2,1,0:T(8,128)(2,1)}...) custom-call(bf16[160,512]{1,0:T(8,128)(2,1)} %refs_0_.1, bf16[160,512]{1,0:T(8,128)(2,1)} %refs_1_.1, ...), custom_call_target="tpu_custom_call" | custom-call | tf_op jit(solution)/shard_map/whole_step/pallas_call | solution.py:1432
  160.4 3.8 %update_all.1 = (f32[2,16,1536]{2,1,0:T(8,128)}, f32[2,16,1536]{2,1,0:T(8,128)}, f32[2,16,1536]{2,1,0:T(8,128)}, f32[2,16,512]{2,1,0:T(8,128)}, f32[2,16,512]{2,...) custom-call(bf16[2,2,16,768]{3,2,1,0:T(8,128)(2,1)} %get-tuple-eleme, ...), custom_call_target="tpu_custom_call" | custom-call | tf_op jit(solution)/shard_map/update_all/pallas_call | solution.py:1515
Async XLA Ops:
  0.7 0.7 copy-start

commit v5 on v4

--- a/solution.py
+++ b/solution.py
@@ -1299,7 +1299,6 @@
     for copy in v_y:
         copy.start()
     conclude(0, sum_u[0], 1)
-    conclude(0, sum_q[0], 0)
     for copy in v_y:
         copy.wait()
     total = v_group[0]
@@ -1310,6 +1309,7 @@
     out_v[1, :, v_mine] = v_group[here.place]
     v_swap = copies.to(out_v.at[:, :, v_mine], out_v.at[:, :, v_mine], here.partner)
     v_swap.start()
+    conclude(0, sum_q[0], 0)
     v_swap.wait()
     handed(1)
     handed(0)

time: 165 us -> 168 us (1.018)
  Pallas kernels: 162 us -> 165 us
    pallas_call x1, Pallas kernels: 158 us -> 161 us  [whole(): pl.pallas_call(kernel, out_shape=tuple(outs.values()), in_specs=[VMEM_SPE...]
where the time goes in v5:
time: 168 us; the launch traced here: 167 us
  Pallas kernels  165 us (98%)
    pallas_call x1, Pallas kernels, whole(): pl.pallas_call(kernel, out_shape=tuple(outs.values()), in_specs=[VMEM_SPE...  161 us
    pallas_call x1, Pallas kernels, update_all(): pl.pallas_call(partial(update_kernel, n_dp, bias_widths, out_rows), out_s...  3.78 us

profile of v5, /device:TPU:1, one launch (start us, length us, event | category | flops | bytes accessed | tf_op | source)
XLA Modules:
  0.0 166.9 jit_solution(7622675290869315367)
XLA Ops:
  0.7 0.0 copy-start
  0.7 0.7 copy-done
  1.3 0.6 reshape.49.refs_2_
  1.9 161.0 %whole_step.1 = (bf16[160,512]{1,0:T(8,128)(2,1)}, f32[160,512]{1,0:T(8,128)}, bf16[2,2,16,768]{3,2,1,0:T(8,128)(2,1)}, bf16[2,2,16,1024]{3,2,1,0:T(8,128)(2,1)}...) custom-call(bf16[160,512]{1,0:T(8,128)(2,1)} %refs_0_.1, bf16[160,512]{1,0:T(8,128)(2,1)} %refs_1_.1, ...), custom_call_target="tpu_custom_call" | custom-call | tf_op jit(solution)/shard_map/whole_step/pallas_call | solution.py:1432
  162.9 3.8 %update_all.1 = (f32[2,16,1536]{2,1,0:T(8,128)}, f32[2,16,1536]{2,1,0:T(8,128)}, f32[2,16,1536]{2,1,0:T(8,128)}, f32[2,16,512]{2,1,0:T(8,128)}, f32[2,16,512]{2,...) custom-call(bf16[2,2,16,768]{3,2,1,0:T(8,128)(2,1)} %get-tuple-eleme, ...), custom_call_target="tpu_custom_call" | custom-call | tf_op jit(solution)/shard_map/update_all/pallas_call | solution.py:1515
Async XLA Ops:
  0.7 0.7 copy-start
